TPU v7x, 32 devices: a whole 2x2x4 slice. The times are simulated.
32 devices in a mesh: dp: 8 (over y, x, core), mp: 4 (over z).
Axes of the slice: x: 2, y: 2, z: 4, core: 2. Of those that a mesh axis runs over, the one named last changes fastest.
Arguments:
- tokens: bfloat16 [2, 16, 944, 768], P(None, 'dp', 'mp'), may hold values from -6 to 6
- w_qkv: bfloat16 [3, 768, 768], P(None, 'dp', 'mp'), may hold values from -0.21875 to 0.21875
- w_up: bfloat16 [768, 3072], P('dp', 'mp'), may hold values from -0.21875 to 0.21875
- w_proj: bfloat16 [768, 768], P('mp', 'dp'), may hold values from -1.75 to 1.75
- w_down: bfloat16 [3072, 768], P('mp', 'dp'), may hold values from -0.109375 to 0.109375
- norm_gain: float32 [768], replicated, may hold values from 0.25 to 1.75
- query_gain: float32 [64], replicated, may hold values from 0.25 to 1.75
- key_gain: float32 [64], replicated, may hold values from 0.25 to 1.75
- image_ids: int32 [2, 16, 944], P(None, 'dp'), may hold values from 0 to 7, never falling along the last dimension, each value on 1 to 709 neighbouring positions
- cotangent: bfloat16 [2, 16, 944, 768], P(None, 'dp', 'mp'), may hold values from -6 to 6
Outputs:
- output: bfloat16 [2, 16, 944, 768], P(None, 'dp', 'mp')
- input_grad: float32 [2, 16, 944, 768], P(None, 'dp', 'mp')
- grad_qkv: float32 [3, 768, 768], P(None, 'dp', 'mp')
- grad_up: float32 [768, 3072], P('dp', 'mp')
- grad_proj: float32 [768, 768], P('mp', 'dp')
- grad_down: float32 [3072, 768], P('mp', 'dp')
- grad_norm_gain: float32 [768], replicated
- grad_query_gain: float32 [64], replicated
- grad_key_gain: float32 [64], replicated
Inputs may be any that keep to these rules, and one draw needn't show every extreme that they name: `image_ids`: within each sequence the numbers never fall, start at 0 and rise by one from image to image; each image holds 1 to 709 tokens and one image of every sequence holds exactly 709.
All inputs are finite; a program needn't handle non-finite values.
Results may differ from a plain program's by a relative error of at most 0.011.
Values may be sent and summed in bfloat16 or wider, within the bound.
A program may use at most 320 MiB of HBM per device.

v0:
```python
import jax
import jax.numpy as jnp
from jax import lax
from jax.sharding import PartitionSpec as P

HD = 64


def norm_rows(values, gain):
    centered = values - jnp.mean(values, axis=-1, keepdims=True)
    spread = lax.rsqrt(jnp.mean(centered * centered, axis=-1, keepdims=True) + 1e-06)
    return centered * spread * gain


def gelu_tanh(values):
    return jax.nn.gelu(values, approximate=True)


def inner_rows(left, right):
    return lax.dot_general(
        left, right, (((0,), (0,)), ((), ())), preferred_element_type=jnp.float32
    )


def times_trans(left, right):
    return lax.dot_general(
        left, right, (((1,), (1,)), ((), ())), preferred_element_type=jnp.float32
    )


def score_block(query_heads, key_heads, same_image):
    scores = jnp.einsum(
        "sqhd,skhd->shqk", query_heads, key_heads, preferred_element_type=jnp.float32
    )
    scores = scores * query_heads.shape[-1] ** (-0.5)
    return jnp.where(same_image, scores, -1e30)


def forward_pass(token_rows, image_rows, full_weights, gains):
    w_qkv, w_up, w_proj, w_down = full_weights
    norm_gain, query_gain, key_gain = gains
    seq_count, part_len, model_width = token_rows.shape
    normed = norm_rows(token_rows.astype(jnp.float32), norm_gain).astype(jnp.bfloat16)
    gathered = lax.all_gather(normed, "mp", axis=1, tiled=True)
    seq_length = gathered.shape[1]
    row_count = seq_count * seq_length
    flat_rows = gathered.reshape(row_count, model_width)
    head_count = w_qkv.shape[2] // HD
    projected = jnp.einsum("rd,cdh->crh", flat_rows, w_qkv, preferred_element_type=jnp.float32)
    q_raw = projected[0].reshape(seq_count, seq_length, head_count, HD)
    k_raw = projected[1].reshape(seq_count, seq_length, head_count, HD)
    query_heads = norm_rows(q_raw, query_gain).astype(jnp.bfloat16)
    key_heads = norm_rows(k_raw, key_gain).astype(jnp.bfloat16)
    value_heads = projected[2].astype(jnp.bfloat16).reshape(seq_count, seq_length, head_count, HD)
    same_image = image_rows[:, None, :, None] == image_rows[:, None, None, :]
    scores = score_block(query_heads, key_heads, same_image)
    row_peak = jnp.max(scores, axis=-1, keepdims=True)
    row_total = jnp.sum(jnp.exp(scores - row_peak), axis=-1, keepdims=True)
    log_total = row_peak + jnp.log(row_total)
    attn_probs = jnp.exp(scores - log_total).astype(jnp.bfloat16)
    attended = jnp.einsum(
        "shqk,skhd->sqhd", attn_probs, value_heads, preferred_element_type=jnp.float32
    )
    attended = attended.astype(jnp.bfloat16).reshape(row_count, head_count * HD)
    upper_proj = jnp.dot(flat_rows, w_up, preferred_element_type=jnp.float32)
    hidden = gelu_tanh(upper_proj).astype(jnp.bfloat16)
    branch = jnp.dot(attended, w_proj, preferred_element_type=jnp.float32)
    branch = branch + jnp.dot(hidden, w_down, preferred_element_type=jnp.float32)
    branch = lax.psum_scatter(
        branch.reshape(seq_count, seq_length, model_width), "mp", scatter_dimension=1, tiled=True
    )
    output = (token_rows.astype(jnp.float32) + branch).astype(jnp.bfloat16)
    saved_state = (
        flat_rows,
        q_raw,
        k_raw,
        query_heads,
        key_heads,
        value_heads,
        same_image,
        log_total,
        attended,
        upper_proj,
        hidden,
    )
    return (output, saved_state)


def backward_pass(token_rows, grad_rows, full_weights, gains, saved_state):
    w_qkv, w_up, w_proj, w_down = full_weights
    norm_gain, query_gain, key_gain = gains
    (
        flat_rows,
        q_raw,
        k_raw,
        query_heads,
        key_heads,
        value_heads,
        same_image,
        log_total,
        attended,
        upper_proj,
        hidden,
    ) = saved_state
    seq_count, seq_length, head_count, head_size = query_heads.shape
    row_count, model_width = flat_rows.shape
    grad_full = lax.all_gather(grad_rows, "mp", axis=1, tiled=True)
    flat_grad = grad_full.reshape(row_count, model_width)
    grad_proj = inner_rows(attended, flat_grad)
    grad_down = inner_rows(hidden, flat_grad)
    d_attended = times_trans(flat_grad, w_proj).astype(jnp.bfloat16)
    d_hidden = times_trans(flat_grad, w_down)
    gelu_out, gelu_back = jax.vjp(gelu_tanh, upper_proj)
    d_upper = gelu_back(d_hidden)[0].astype(jnp.bfloat16)
    scores = score_block(query_heads, key_heads, same_image)
    attn_probs = jnp.exp(scores - log_total)
    d_heads = d_attended.reshape(seq_count, seq_length, head_count, head_size)
    d_probs = jnp.einsum(
        "sqhd,skhd->shqk", d_heads, value_heads, preferred_element_type=jnp.float32
    )
    d_scores = attn_probs * (d_probs - jnp.sum(d_probs * attn_probs, axis=-1, keepdims=True))
    d_scores = d_scores.astype(jnp.bfloat16)
    score_scale = head_size ** (-0.5)
    d_query = (
        jnp.einsum("shqk,skhd->sqhd", d_scores, key_heads, preferred_element_type=jnp.float32)
        * score_scale
    )
    d_key = (
        jnp.einsum("shqk,sqhd->skhd", d_scores, query_heads, preferred_element_type=jnp.float32)
        * score_scale
    )
    d_value = jnp.einsum(
        "shqk,sqhd->skhd",
        attn_probs.astype(jnp.bfloat16),
        d_heads,
        preferred_element_type=jnp.float32,
    )
    query_out, query_back = jax.vjp(norm_rows, q_raw, query_gain)
    d_q_raw, d_query_gain = query_back(d_query)
    key_out, key_back = jax.vjp(norm_rows, k_raw, key_gain)
    d_k_raw, d_key_gain = key_back(d_key)
    width_heads = head_count * head_size
    d_project = jnp.stack(
        [
            d_q_raw.reshape(row_count, width_heads),
            d_k_raw.reshape(row_count, width_heads),
            d_value.reshape(row_count, width_heads),
        ]
    ).astype(jnp.bfloat16)
    grad_qkv = jnp.einsum("rd,crh->cdh", flat_rows, d_project, preferred_element_type=jnp.float32)
    grad_up = inner_rows(flat_rows, d_upper)
    d_normed = jnp.einsum("crh,cdh->rd", d_project, w_qkv, preferred_element_type=jnp.float32)
    d_normed = d_normed + times_trans(d_upper, w_up)
    d_normed = lax.psum_scatter(
        d_normed.reshape(seq_count, seq_length, model_width).astype(jnp.bfloat16),
        "mp",
        scatter_dimension=1,
        tiled=True,
    ).astype(jnp.float32)
    norm_out, norm_back = jax.vjp(norm_rows, token_rows.astype(jnp.float32), norm_gain)
    d_tokens, d_norm_gain = norm_back(d_normed)
    input_grad = grad_rows.astype(jnp.float32) + d_tokens
    return (
        input_grad,
        (grad_qkv, grad_up, grad_proj, grad_down),
        (d_norm_gain, d_query_gain, d_key_gain),
    )


def body(
    tokens, w_qkv, w_up, w_proj, w_down, norm_gain, query_gain, key_gain, image_ids, cotangent
):
    gains = (norm_gain, query_gain, key_gain)
    outputs = []
    input_grads = []
    weight_totals = None
    gain_totals = None
    for micro_index in range(tokens.shape[0]):
        full_weights = (
            lax.all_gather(w_qkv, "dp", axis=1, tiled=True),
            lax.all_gather(w_up, "dp", axis=0, tiled=True),
            lax.all_gather(w_proj, "dp", axis=1, tiled=True),
            lax.all_gather(w_down, "dp", axis=1, tiled=True),
        )
        output, saved_state = forward_pass(
            tokens[micro_index], image_ids[micro_index], full_weights, gains
        )
        full_weights = (
            lax.all_gather(w_qkv, "dp", axis=1, tiled=True),
            lax.all_gather(w_up, "dp", axis=0, tiled=True),
            lax.all_gather(w_proj, "dp", axis=1, tiled=True),
            lax.all_gather(w_down, "dp", axis=1, tiled=True),
        )
        input_grad, weight_grads, gain_grads = backward_pass(
            tokens[micro_index], cotangent[micro_index], full_weights, gains, saved_state
        )
        weight_grads = (
            lax.psum_scatter(weight_grads[0], "dp", scatter_dimension=1, tiled=True),
            lax.psum_scatter(weight_grads[1], "dp", scatter_dimension=0, tiled=True),
            lax.psum_scatter(weight_grads[2], "dp", scatter_dimension=1, tiled=True),
            lax.psum_scatter(weight_grads[3], "dp", scatter_dimension=1, tiled=True),
        )
        if weight_totals is None:
            weight_totals = weight_grads
            gain_totals = gain_grads
        else:
            weight_totals = jax.tree.map(jnp.add, weight_totals, weight_grads)
            gain_totals = jax.tree.map(jnp.add, gain_totals, gain_grads)
        outputs.append(output)
        input_grads.append(input_grad)
    gain_totals = lax.psum(gain_totals, ("dp", "mp"))
    return (
        jnp.stack(outputs),
        jnp.stack(input_grads),
        weight_totals[0],
        weight_totals[1],
        weight_totals[2],
        weight_totals[3],
        gain_totals[0],
        gain_totals[1],
        gain_totals[2],
    )


def solution(mesh):
    placed = (
        P(None, "dp", "mp", None),
        P(None, "dp", "mp"),
        P("dp", "mp"),
        P("mp", "dp"),
        P("mp", "dp"),
        P(),
        P(),
        P(),
        P(None, "dp", None),
        P(None, "dp", "mp", None),
    )
    return jax.shard_map(
        body,
        mesh=mesh,
        in_specs=placed,
        out_specs=(
            P(None, "dp", "mp", None),
            P(None, "dp", "mp", None),
            P(None, "dp", "mp"),
            P("dp", "mp"),
            P("mp", "dp"),
            P("mp", "dp"),
            P(),
            P(),
            P(),
        ),
        check_vma=False,
    )
```

profile of v0, /device:TPU:0, one launch (start us, length us, event | category | flops | bytes accessed | tf_op | source)
XLA Modules:
  0.0 1266.9 jit_solution(9434480221717814295)
XLA Ops:
  7.2 2.6 convert_reduce_fusion.1
  10.0 2.7 fusion.43
  13.7 3.2 multiply_convert_fusion.9
  22.1 11.0 all_gather.18
  33.1 13.5 %all_gather.17 = bf16[3,768,192]{2,0,1:T(4,128)(2,1)S(1)} all-gather(bf16[3,96,192]{2,0,1:T(4,128)(2,1)S(1)} %copy.307), channel_id=1, replica_groups=mesh['dp'=8,'mp'=4] {'dp'}, dimensions={1}, use_global_device_ids=true | all-gather | bytes 995328 | tf_op jit(solution)/shard_map/all_gather | solution.py:180
  49.9 2.2 broadcast_compare_fusion
  52.1 27.1 %all-gather.15.cloned.1.call-done = bf16[2,944,768]{2,0,1:T(2,128)(2,1)} async-done(((bf16[2,236,768]{2,0,1:T(2,128)(2,1)}), bf16[2,944,768]{2,0,1:T(2,128)(2,1)}) %all-gather.15.cloned.1.call-update) | async-done | bytes 2899984 | tf_op jit(solution)/shard_map/all_gather | solution.py:44
  86.2 52.7 %all-gather.9.cloned.1.call-done = bf16[2,944,768]{2,0,1:T(2,128)(2,1)} async-done(((bf16[2,236,768]{2,0,1:T(2,128)(2,1)}), bf16[2,944,768]{2,0,1:T(2,128)(2,1)}) %all-gather.9.cloned.1.call-update) | async-done | bytes 2899984 | tf_op jit(solution)/shard_map/all_gather | solution.py:44
  144.6 54.7 %all-gather.17.cloned.1.call-done = bf16[1,2,944,768]{3,1,0,2:T(2,128)(2,1)} async-done(((bf16[1,2,236,768]{3,1,0,2:T(2,128)(2,1)}), bf16[1,2,944,768]{3,1,0,2:T(2,128)(2,1)}) %all-gather.17.cloned.1.call-update) | async-done | bytes 2899984 | tf_op jit(solution)/shard_map/all_gather | solution.py:107
  211.2 3.3 reshape_squeeze.12
  217.7 11.8 fusion
  229.5 10.9 exponential_reduce_fusion.1
  240.4 11.8 fusion.54
  252.3 12.1 fusion.52
  264.4 17.6 %multiply_reduce_fusion.1 = (f32[2,3,944]{2,1,0:T(4,128)}, f32[2,3,944,944]{2,3,1,0:T(8,128)}) fusion(f32[2,3,944,944]{2,3,1,0:T(8,128)} %get-tuple-element.121, f32[2,3,944]{2,1,0:T(4,128)S(1)} %log_add_fusion.1, pred[2,944,944]{1,2,0:T(8,128)(4,1)S(1)} %copy-done.17, bf16[2,944,3,64]{1,0,3,2:T(2,128)(2,1)} %convert_element_type.123, ...), kind=kOutput, calls=%fused_computation.3 | convolution fusion | flops 711120896 | bytes 46052096 | tf_op jit(solution)/shard_map/sqhd,skhd->shqk/dot_general | solution.py:118
  300.0 3.0 copy.319
  303.0 3.3 reshape.278
  306.3 2.8 fusion.111
  309.2 16.1 %multiply_convert_fusion.1 = bf16[2,3,944,944]{2,3,1,0:T(8,128)(2,1)S(1)} fusion(f32[2,3,944,944]{2,3,1,0:T(8,128)} %get-tuple-element.123, f32[2,3,944,944]{2,3,1,0:T(8,128)} %get-tuple-element.121, f32[2,3,944]{2,1,0:T(4,128)S(1)} %copy-done.85, f32[2,3,944]{2,1,0:T(4,128)S(1)} %copy-done.81, pred[2,944,944]{1,2,0:T(8,128)(4,1)S(1)} %copy-done.18), kind=kLoop, calls=%fused_computation.2 | loop fusion | flops 32080896 | bytes 55295744 | tf_op jit(solution)/shard_map/convert_element_type | solution.py:122
  325.3 6.6 fusion.30
  332.0 5.9 fusion.31
  338.1 10.4 fusion.1
  348.5 11.2 exponential_reduce_fusion
  359.7 10.8 fusion.53
  372.0 3.8 convolution_add_fusion.4
  378.1 17.4 %multiply_reduce_fusion = (f32[2,3,944]{2,1,0:T(4,128)}, f32[2,3,944,944]{2,3,1,0:T(8,128)}) fusion(f32[2,3,944,944]{2,3,1,0:T(8,128)} %get-tuple-element.117, f32[2,3,944]{2,1,0:T(4,128)S(1)} %log_add_fusion, pred[2,944,944]{1,2,0:T(8,128)(4,1)S(1)} %copy-done.14, bf16[2,944,3,64]{1,0,3,2:T(2,128)(2,1)} %convert_element_type.134, ...), kind=kOutput, calls=%fused_computation.1 | convolution fusion | flops 711120896 | bytes 46052096 | tf_op jit(solution)/shard_map/sqhd,skhd->shqk/dot_general | solution.py:118
  395.5 18.2 %multiply_convert_fusion = bf16[2,3,944,944]{2,3,1,0:T(8,128)(2,1)S(1)} fusion(f32[2,3,944,944]{2,3,1,0:T(8,128)} %get-tuple-element.119, f32[2,3,944,944]{2,3,1,0:T(8,128)} %get-tuple-element.117, f32[2,3,944]{2,1,0:T(4,128)} %get-tuple-element.118, f32[2,3,944]{2,1,0:T(4,128)} %copy-done.78, pred[2,944,944]{1,2,0:T(8,128)(4,1)} %broadcast_compare_fusion), kind=kLoop, calls=%fused_computation | loop fusion | flops 32080896 | bytes 55295744 | tf_op jit(solution)/shard_map/convert_element_type | solution.py:122
  413.8 5.7 fusion.27
  420.2 11.0 fusion.25
  432.8 4.0 fusion.24
  436.8 2.6 add_convert_fusion
  441.2 3.5 stack_reshape.28
  444.7 4.3 add_convert_fusion.1
  458.4 11.7 fusion.55
  474.4 6.2 fusion.105
  480.6 9.6 fusion.10
  490.2 2.5 fusion.106
  493.1 4.1 fusion.19
  502.6 5.8 copy.360
  509.4 3.6 add_bitcast_fusion
  513.0 2.7 copy.399
  515.7 5.0 reshape.301
  520.9 3.9 fusion.107
  524.8 6.9 fusion.17
  531.7 2.5 fusion.108
  534.2 4.3 fusion.18
  538.4 3.9 copy.385
  542.4 6.3 fusion.98
  549.7 6.9 copy.321
  556.7 6.1 fusion.96
  563.8 7.0 copy.339
  571.1 6.7 fusion.97
  577.9 7.2 convolution_add_fusion.2
  587.0 5.7 fusion.110
  592.7 4.2 convolution_add_fusion.3
  601.1 168.7 %all-reduce.12.cloned.1.call-done = (bf16[2,944,768]{2,0,1:T(2,128)(2,1)}, bf16[2,944,768]{2,0,1:T(2,128)(2,1)}) async-done(((bf16[2,944,768]{2,0,1:T(2,128)(2,1)}, bf16[2,944,768]{2,0,1:T(2,128)(2,1)}), (bf16[2,944,768]{2,0,1:T(2,128)(2,1)}, bf16[2,944,768]{2,0,1:T(2,128)(2,1)})) %all-reduce.12.cloned.1.call-update) | async-done | bytes 5799952
  769.9 7.3 fusion.46
  777.7 45.7 %all-reduce.4 = (f32[768]{0:T(1024)}, f32[64]{0:T(128)}, f32[64]{0:T(128)}) all-reduce(f32[768]{0:T(1024)S(1)} %add.199, f32[64]{0:T(128)S(1)} %add.200, f32[64]{0:T(128)S(1)} %add.201), channel_id=1, replica_groups=mesh['dp'=8,'mp'=4] {'dp','mp'}, use_global_device_ids=true, to_apply=%region_44.45 | all-reduce | flops 896 | bytes 7168 | tf_op jit(solution)/shard_map/psum | solution.py:211
  823.5 344.2 %all-reduce.10.cloned.1.call-done = (f32[2,944,768]{2,0,1:T(2,128)}, f32[2,944,768]{2,0,1:T(2,128)}) async-done(((f32[2,944,768]{2,0,1:T(2,128)}, f32[2,944,768]{2,0,1:T(2,128)}), (f32[2,944,768]{2,0,1:T(2,128)}, f32[2,944,768]{2,0,1:T(2,128)})) %all-reduce.10.cloned.1.call-update) | async-done | bytes 11599888
  1167.6 8.8 fusion.99
  1178.5 2.9 pad_maximum_fusion
  1181.4 3.2 pad_maximum_fusion.1
  1184.6 28.8 %reduce-scatter.11.cloned.1.call-done = f32[768,96]{0,1:T(8,128)} async-done(((f32[768,768]{0,1:T(8,128)}), f32[768,96]{0,1:T(8,128)}) %reduce-scatter.11.cloned.1.call-update) | async-done | bytes 294928 | tf_op jit(solution)/shard_map/reduce_scatter | solution.py:201
  1213.4 46.3 %reduce-scatter.9.cloned.1.call-done = f32[96,768]{1,0:T(8,128)} async-done(((f32[768,768]{1,0:T(8,128)}), f32[96,768]{1,0:T(8,128)}) %reduce-scatter.9.cloned.1.call-update) | async-done | bytes 294928 | tf_op jit(solution)/shard_map/reduce_scatter | solution.py:199
  (349 shorter events, 93.5 us)
Async XLA Ops:
  7.2 6.5 copy-start.87
  7.2 72.0 %all-gather.15.cloned.1.call-start = ((), (), s32[]{:S(2)}) async-start(), calls=%async_computation.7 | async-start | bytes 3624960 | tf_op jit(solution)/shard_map/all_gather | solution.py:44
  9.9 7.0 copy-start.49
  9.9 7.0 copy-start.51
  16.9 122.0 %all-gather.9.cloned.1.call-start = ((), (), s32[]{:S(2)}) async-start(), calls=%async_computation.4 | async-start | bytes 3624960 | tf_op jit(solution)/shard_map/all_gather | solution.py:44
  17.8 181.5 %all-gather.17.cloned.1.call-start = ((), (), s32[]{:S(2)}) async-start(), calls=%async_computation.8 | async-start | bytes 3624960 | tf_op jit(solution)/shard_map/all_gather | solution.py:107
  19.9 262.0 %all-gather.19.cloned.1.call-start = ((), (), s32[]{:S(2)}) async-start(), calls=%async_computation.9 | async-start | bytes 3624960 | tf_op jit(solution)/shard_map/all_gather | solution.py:107
  20.5 453.9 %all-gather.13.cloned.1.call-start = ((), (), s32[]{:S(2)}) async-start(), calls=%async_computation.6 | async-start | bytes 1327104 | tf_op jit(solution)/shard_map/all_gather | solution.py:183
  21.1 459.5 %all-gather.11.cloned.1.call-start = ((), (), s32[]{:S(2)}) async-start(), calls=%async_computation.5 | async-start | bytes 1327104 | tf_op jit(solution)/shard_map/all_gather | solution.py:181
  21.7 575.9 %reduce-scatter.15.cloned.1.call-start = ((), (), s32[]{:S(2)}) async-start(), calls=%async_computation.13 | async-start | bytes 884736
  33.1 251.1 %copy-start.32 = (bf16[192,768]{0,1:T(8,128)(2,1)}, bf16[192,768]{0,1:T(8,128)(2,1)S(1)}, u32[]{:S(2)}) copy-start(bf16[192,768]{0,1:T(8,128)(2,1)S(1)} %all_gather.18) | copy-start | bytes 884740
  47.6 93.5 %copy-start.69 = (bf16[3,768,192]{1,2,0:T(8,128)(2,1)}, bf16[3,768,192]{1,2,0:T(8,128)(2,1)S(1)}, u32[]{:S(2)}) copy-start(bf16[3,768,192]{1,2,0:T(8,128)(2,1)S(1)} %copy.308) | copy-start | bytes 2654212
  209.4 8.2 copy-start.3
  214.5 15.0 %copy-start.1 = (f32[2,944,3,64]{1,0,3,2:T(2,128)}, f32[2,944,3,64]{1,0,3,2:T(2,128)S(1)}, u32[]{:S(2)}) copy-start(f32[2,944,3,64]{1,0,3,2:T(2,128)S(1)} %reshape_squeeze.12) | copy-start | bytes 4349956
  216.5 13.0 %copy-start.41 = (f32[2,944,3]{1,2,0:T(4,128)}, f32[2,944,3]{1,2,0:T(4,128)S(1)}, u32[]{:S(2)}) copy-start(f32[2,944,3]{1,2,0:T(4,128)S(1)} %copy.309) | copy-start | bytes 67972
  217.6 11.9 copy-start.66
  217.6 11.9 copy-start.16
  229.5 10.9 copy-start.47
  240.4 24.0 %copy-start.80 = (f32[2,3,944]{2,1,0:T(4,128)}, f32[2,3,944]{2,1,0:T(4,128)S(1)}, u32[]{:S(2)}) copy-start(f32[2,3,944]{2,1,0:T(4,128)S(1)} %log_add_fusion.1) | copy-start | bytes 67972
  240.4 11.8 copy-start.48
  252.3 12.1 copy-start.17
  300.0 6.3 copy-start.22
  309.2 16.1 %copy-start.42 = (f32[2,944,3]{1,2,0:T(4,128)S(1)}, f32[2,944,3]{1,2,0:T(4,128)}, u32[]{:S(2)}) copy-start(f32[2,944,3]{1,2,0:T(4,128)} %copy-done.41) | copy-start | bytes 67972
  309.2 16.1 %copy-start.61 = (f32[2,944,3]{1,2,0:T(4,128)S(1)}, f32[2,944,3]{1,2,0:T(4,128)}, u32[]{:S(2)}) copy-start(f32[2,944,3]{1,2,0:T(4,128)} %copy-done.60) | copy-start | bytes 67972
  309.2 16.1 %copy-start.67 = (f32[2,944,3]{1,2,0:T(4,128)S(1)}, f32[2,944,3]{1,2,0:T(4,128)}, u32[]{:S(2)}) copy-start(f32[2,944,3]{1,2,0:T(4,128)} %copy-done.66) | copy-start | bytes 67972
  325.3 6.6 copy-start.68
  331.9 5.9 copy-start.77
  331.9 6.0 copy-start.75
  331.9 6.1 copy-start.6
  331.9 6.1 copy-start.9
  331.9 6.1 copy-start.13
  348.4 11.2 copy-start.46
  359.7 18.4 %copy-start.78 = (f32[2,3,944]{2,1,0:T(4,128)}, f32[2,3,944]{2,1,0:T(4,128)S(1)}, u32[]{:S(2)}) copy-start(f32[2,3,944]{2,1,0:T(4,128)S(1)} %log_add_fusion) | copy-start | bytes 67972
  372.0 6.1 copy-start.14
  395.5 18.2 %copy-start.2 = (f32[2,944,3,64]{1,0,3,2:T(2,128)S(1)}, f32[2,944,3,64]{1,0,3,2:T(2,128)}, u32[]{:S(2)}) copy-start(f32[2,944,3,64]{1,0,3,2:T(2,128)} %copy-done.1) | copy-start | bytes 4349956
  395.5 18.2 %copy-start.7 = (f32[2,944,3,64]{1,0,3,2:T(2,128)S(1)}, f32[2,944,3,64]{1,0,3,2:T(2,128)}, u32[]{:S(2)}) copy-start(f32[2,944,3,64]{1,0,3,2:T(2,128)} %copy-done.5) | copy-start | bytes 4349956
  395.5 18.2 %copy-start.10 = (f32[2,944,3,64]{1,0,3,2:T(2,128)S(1)}, f32[2,944,3,64]{1,0,3,2:T(2,128)}, u32[]{:S(2)}) copy-start(f32[2,944,3,64]{1,0,3,2:T(2,128)} %copy-done.8) | copy-start | bytes 4349956
  395.5 18.2 %copy-start.24 = (f32[2,3,64,944]{3,2,1,0:T(8,128)S(1)}, f32[2,3,64,944]{3,2,1,0:T(8,128)}, u32[]{:S(2)}) copy-start(f32[2,3,64,944]{3,2,1,0:T(8,128)} %get-tuple-element.125) | copy-start | bytes 4349956
  413.7 5.8 copy-start
  413.7 6.4 copy-start.4
  420.2 12.6 copy-start.25
  439.4 5.2 copy-start.84
  470.1 129.1 %reduce-scatter.13.cloned.1.call-start = ((), (), s32[]{:S(2)}) async-start(), calls=%async_computation.12 | async-start | bytes 2211840
  480.6 9.6 copy-start.100
  502.6 6.7 copy-start.29
  515.7 5.1 copy-start.20
  520.8 249.1 %all-reduce.12.cloned.1.call-start = ((), (), s32[]{:S(2)}) async-start(), calls=%async_computation.15 | async-start | bytes 11599872
  542.3 625.3 %all-reduce.10.cloned.1.call-start = ((), (), s32[]{:S(2)}) async-start(), calls=%async_computation.14 | async-start | bytes 23199744
  542.4 6.3 copy-start.33
  542.4 6.3 copy-start.36
  556.7 6.1 copy-start.35
  570.9 642.5 %reduce-scatter.11.cloned.1.call-start = ((), (), s32[]{:S(2)}) async-start(), calls=%async_computation.11 | async-start | bytes 2654208 | tf_op jit(solution)/shard_map/reduce_scatter | solution.py:201
  585.1 674.7 %reduce-scatter.9.cloned.1.call-start = ((), (), s32[]{:S(2)}) async-start(), calls=%async_computation.10 | async-start | bytes 2654208 | tf_op jit(solution)/shard_map/reduce_scatter | solution.py:199
  586.9 5.7 copy-start.31
  587.0 5.7 copy-start.57
  596.9 173.0 %copy-start.12 = (bf16[2,2,236,768]{3,1,2,0:T(2,128)(2,1)S(1)}, bf16[2,2,236,768]{3,1,2,0:T(2,128)(2,1)}, u32[]{:S(2)}) copy-start(bf16[2,2,236,768]{3,1,2,0:T(2,128)(2,1)} %param.10) | copy-start | bytes 4349956
  596.9 173.0 %copy-start.50 = (f32[2,236]{0,1:T(8,128)S(1)}, f32[2,236]{0,1:T(8,128)}, u32[]{:S(2)}) copy-start(f32[2,236]{0,1:T(8,128)} %copy-done.49) | copy-start | bytes 5668
  596.9 173.0 %copy-start.52 = (f32[2,236]{0,1:T(8,128)S(1)}, f32[2,236]{0,1:T(8,128)}, u32[]{:S(2)}) copy-start(f32[2,236]{0,1:T(8,128)} %copy-done.51) | copy-start | bytes 5668
  596.9 173.0 %copy-start.63 = (f32[2,236]{0,1:T(8,128)S(1)}, f32[2,236]{0,1:T(8,128)}, u32[]{:S(2)}) copy-start(f32[2,236]{0,1:T(8,128)} %copy-done.62) | copy-start | bytes 5668
  596.9 173.0 %copy-start.65 = (f32[2,236]{0,1:T(8,128)S(1)}, f32[2,236]{0,1:T(8,128)}, u32[]{:S(2)}) copy-start(f32[2,236]{0,1:T(8,128)} %copy-done.64) | copy-start | bytes 5668
  596.9 173.0 %copy-start.88 = (f32[768]{0:T(1024)S(1)}, f32[768]{0:T(1024)}, u32[]{:S(2)}) copy-start(f32[768]{0:T(1024)} %param.15) | copy-start | bytes 9220
  600.4 177.0 %copy-start.93 = (f32[2,236]{1,0:T(2,128)S(1)}, f32[2,236]{1,0:T(2,128)}, u32[]{:S(2)}) copy-start(f32[2,236]{1,0:T(2,128)} %copy-done.92) | copy-start | bytes 5668
  600.4 177.2 %copy-start.91 = (f32[2,236]{1,0:T(2,128)S(1)}, f32[2,236]{1,0:T(2,128)}, u32[]{:S(2)}) copy-start(f32[2,236]{1,0:T(2,128)} %copy-done.90) | copy-start | bytes 5668
  1167.6 8.9 copy-start.40
  (52 other events, 139.1 us)
Sparse Core Ops, SparseCore 0:
  17.1 62.1 all-gather.14
  80.8 58.1 all-gather.8
  141.1 58.1 all-gather.16
  200.7 58.1 all-gather.18
  260.6 22.7 all-gather.12
  285.1 24.0 all-gather.10
  470.2 33.6 reduce-scatter.14
  520.9 39.0 reduce-scatter.12
  562.6 207.2 all-reduce.11
  772.5 395.0 all-reduce.9
  1171.9 41.4 reduce-scatter.10
  1217.2 42.5 reduce-scatter.8
where the time goes:
time: 1270 us
  waiting for transfers between devices  725 us (57%)
  matrix products  229 us (18%)
  local copies, waits for them, and re-layouts  113 us (9%)
  other arithmetic  112 us (9%)
  blocking collectives  70.3 us (6%)
  between operations  16.9 us (1%)
    unnamed x16, waiting for transfers between devices  515 us
    all_gather x2, waiting for transfers between devices, forward_pass(): gathered = lax.all_gather(normed, 'mp', axis=1, tiled=True)  79.9 us
    all_gather x2, waiting for transfers between devices, backward_pass(): grad_full = lax.all_gather(grad_rows, 'mp', axis=1, tiled=True)  54.7 us
    reduce_scatter x1, waiting for transfers between devices, body(): lax.psum_scatter(weight_grads[1], 'dp', scatter_dimension=0, tiled=True)  46.3 us
    psum x1, blocking collectives, body(): gain_totals = lax.psum(gain_totals, ('dp', 'mp'))  45.7 us
    dot_general x2, matrix products, backward_pass(): jnp.einsum('sqhd,skhd->shqk', d_heads, value_heads, preferred_element_typ...  35 us
    convert_element_type x2, other arithmetic, backward_pass(): d_scores = d_scores.astype(jnp.bfloat16)  34.3 us
    dot_general x6, matrix products, inner_rows(): lax.dot_general(left, right, (((0,), (0,)), ((), ())), preferred_element_...  30.5 us
  transfers between devices with their start and end apart: 12, of which 7 were waited for; matrix products, arithmetic and copies ran while one was open for 35% of the time, Pallas kernels for 0%

commit v1 on v0

v1 whole, which is shorter than its diff:
```python
import functools

import jax
import jax.numpy as jnp
from jax import lax
from jax.experimental import pallas as pl
from jax.experimental.pallas import tpu as pltpu
from jax.sharding import PartitionSpec as P

HD = 64
MOST = 709
IMAGES = 8
PIECE = 240
BIG = 768
REST = 256
ROWS = BIG + REST
VMEM = 60 * 1024 * 1024
F32 = jnp.float32
BF16 = jnp.bfloat16


def nn(left, right):
    return lax.dot_general(left, right, (((1,), (0,)), ((), ())), preferred_element_type=F32)


def nt(left, right):
    return lax.dot_general(left, right, (((1,), (1,)), ((), ())), preferred_element_type=F32)


def norm_kernel(place, tok, cot, gain, normed, grads, send1, send2, send3):
    step = pl.program_id(0)
    part = tok.shape[1]
    x = tok[0].astype(F32)
    centered = x - jnp.mean(x, axis=-1, keepdims=True)
    spread = lax.rsqrt(jnp.mean(centered * centered, axis=-1, keepdims=True) + 1e-6)
    value = (centered * spread * gain[...]).astype(BF16)
    normed[...] = jnp.zeros_like(normed)
    grads[...] = jnp.zeros_like(grads)
    normed[0, :part] = value
    grads[0, :part] = cot[0]
    for index, send in ((1, send1), (2, send2), (3, send3)):

        @pl.when(step == index)
        def _():
            send[0] = normed[0]
            send[1] = grads[0]


def norm_call(place, tokens, cotangent, gain):
    count, part, width = tokens.shape
    block = lambda k, place: (lax.rem(place[0] + k, count), 0, 0)
    fixed = lambda k, place: (0, 0, 0)
    return pl.pallas_call(
        norm_kernel,
        grid_spec=pltpu.PrefetchScalarGridSpec(
            num_scalar_prefetch=1,
            grid=(count,),
            in_specs=[
                pl.BlockSpec((1, part, width), block),
                pl.BlockSpec((1, part, width), block),
                pl.BlockSpec((1, width), lambda k, place: (0, 0)),
            ],
            out_specs=[pl.BlockSpec((1, PIECE, width), lambda k, place: (k, 0, 0))] * 2
            + [pl.BlockSpec((2, PIECE, width), fixed)] * 3,
        ),
        out_shape=[jax.ShapeDtypeStruct((count, PIECE, width), BF16)] * 2
        + [jax.ShapeDtypeStruct((2, PIECE, width), BF16)] * 3,
        compiler_params=pltpu.CompilerParams(vmem_limit_bytes=VMEM),
        name="norm_rows",
    )(place, tokens, cotangent, gain)


def feed_kernel(normed, grads, w_up, w_down, branch, d_normed, g_up, g_down, xt, dt):
    step = pl.program_id(0)
    x = normed[...]
    dy = grads[...]

    @pl.when(step == 0)
    def _():
        xt[...] = x.T
        dt[...] = dy.T

    up = nn(x, w_up[0])
    inner = 0.7978845608028654 * (up + 0.044715 * up * up * up)
    th = jnp.tanh(inner)
    half = 0.5 * (1.0 + th)
    hidden = (up * half).astype(BF16)
    slope = half + 0.5 * up * (1.0 - th * th) * (
        0.7978845608028654 * (1.0 + 3 * 0.044715 * up * up)
    )
    d_up = (nn(dy, w_down[0]) * slope).astype(BF16)
    g_up[0] = nn(xt[...], d_up).astype(BF16)
    g_down[0] = nn(dt[...], hidden).astype(BF16)
    out = nt(hidden, w_down[0])
    back = nt(d_up, w_up[0])

    @pl.when(step == 0)
    def _():
        branch[...] = out
        d_normed[...] = back

    @pl.when(step > 0)
    def _():
        branch[...] += out
        d_normed[...] += back


def feed_call(normed, grads, w_up, w_down):
    rows, width = normed.shape
    chunks, _, hidden = w_up.shape
    whole = pl.BlockSpec((rows, width), lambda m: (0, 0))
    chunk = pl.BlockSpec((1, width, hidden), lambda m: (m, 0, 0))
    return pl.pallas_call(
        feed_kernel,
        grid=(chunks,),
        in_specs=[whole, whole, chunk, chunk],
        out_specs=[whole, whole, chunk, chunk],
        out_shape=[jax.ShapeDtypeStruct((rows, width), F32)] * 2
        + [jax.ShapeDtypeStruct(w_up.shape, BF16)] * 2,
        scratch_shapes=[pltpu.VMEM((width, rows), BF16)] * 2,
        compiler_params=pltpu.CompilerParams(vmem_limit_bytes=VMEM),
        cost_estimate=pl.CostEstimate(
            flops=12 * rows * width * hidden * chunks,
            bytes_accessed=4 * chunks * width * hidden * 2,
            transcendentals=rows * hidden * chunks,
        ),
        name="feed_forward",
    )(normed, grads, w_up, w_down)


def iota(shape, axis):
    return lax.broadcasted_iota(jnp.int32, shape, axis)


def source_of(index, start, total):
    rest = index - BIG
    other = jnp.where(rest < start, rest, rest + MOST)
    held = jnp.where(index < MOST, start + index, -1)
    return jnp.where((rest >= 0) & (rest < total - MOST), other, held)


def attention_kernel(
    part, place, own_x, own_dy, in1, in2, in3, ids, gains, weights,
    out0, out1, out2, out3, g_weights, g_gains,
    x_ref, dy_ref, xt, dt, feat_q, feat_k, pt, raw, d_raw, d_att, att, d_normed, branch,
):
    step = pl.program_id(0)
    mp = ids.shape[1]
    total = mp * part
    me = place[0]
    lane = iota((1, 128), 1)

    @pl.when(step == 0)
    def _():
        numbers = ids[0]
        start = jnp.zeros((1, 1), jnp.int32)
        for image in range(IMAGES):
            count = jnp.sum(
                (numbers == image).astype(F32), axis=(0, 1), keepdims=True
            )
            ahead = jnp.sum(
                ((numbers >= 0) & (numbers < image)).astype(F32), axis=(0, 1), keepdims=True
            )
            start = start + jnp.where(count == MOST, ahead, 0.0).astype(jnp.int32)
        column = source_of(iota((ROWS, 1), 0), start, total)
        line = source_of(iota((1, ROWS), 1), start, total)
        x_sum, dy_sum, feats = 0.0, 0.0, 0.0
        pieces = ((own_x, own_dy), (in1,), (in2,), (in3,))
        for k, piece in enumerate(pieces):
            chunk = lax.rem(me - k + mp, mp)
            offset = iota((1, PIECE), 1)
            pos = jnp.where(offset < part, chunk * part + offset, -2)
            pick = (column == pos).astype(F32).astype(BF16)
            offset = iota((PIECE, 1), 0)
            pos = jnp.where(offset < part, chunk * part + offset, -2)
            pt[k] = (line == pos).astype(F32).astype(BF16)
            x_piece = piece[0][0]
            dy_piece = piece[1][0] if k == 0 else piece[0][1]
            x_sum = x_sum + nn(pick, x_piece)
            dy_sum = dy_sum + nn(pick, dy_piece)
            marks = (iota((128, 1), 0) - HD == ids[0, pl.ds(chunk, 1), :]).astype(F32)
            feats = feats + nt(pick, marks.astype(BF16))
        x = x_sum.astype(BF16)
        dy = dy_sum.astype(BF16)
        x_ref[...] = x
        dy_ref[...] = dy
        xt[...] = x.T
        dt[...] = dy.T
        feat_q[...] = (feats * 128.0).astype(BF16)
        marked = (lane >= HD) & (lane < HD + IMAGES)
        feat_k[...] = jnp.where(marked, (feats - 1.0) * 256.0, 0.0).astype(BF16)
        d_normed[...] = jnp.zeros_like(d_normed)
        branch[...] = jnp.zeros_like(branch)
        g_gains[...] = jnp.zeros_like(g_gains)

    raw[...] = nn(x_ref[...], weights[0, :, :640])
    d_att[...] = nn(dy_ref[...], weights[0, :, 512:])
    low = lane < HD
    same = (iota((128, 128), 0) // HD == iota((128, 128), 1) // HD).astype(F32)
    mean_of = (same * (1.0 / HD)).astype(BF16)
    gain = gains[...]

    def half_mean(value):
        return nn(value.astype(BF16), mean_of)

    d_gain = jnp.zeros((1, 128), F32)
    for head in range(3):
        qk = raw[:, 128 * head:128 * head + 128]
        high = qk.astype(BF16)
        mean = nn(high, mean_of) + half_mean(qk - high.astype(F32))
        centered = qk - mean
        spread = lax.rsqrt(half_mean(centered * centered) + 1e-6)
        unit = centered * spread
        rounded = (unit * gain).astype(BF16).astype(F32)
        q_aug = jnp.where(low, rounded * 0.125, feat_q[...].astype(F32)).astype(BF16)
        k_aug = jnp.where(low, pltpu.roll(rounded, HD, 1), feat_k[...].astype(F32)).astype(BF16)
        v_tile = 384 + 128 * (head // 2)
        v = raw[:, v_tile:v_tile + 128]
        if head == 1:
            v = pltpu.roll(v, HD, 1)
        one = ((lane == HD) | (lane == HD + 1)).astype(F32)
        v_aug = jnp.where(low, v, one).astype(BF16)
        a_tile = 128 * ((head + 1) // 2)
        da = d_att[:, a_tile:a_tile + 128]
        if head != 1:
            da = pltpu.roll(da, HD, 1)
        q_t = q_aug.astype(F32).T.astype(BF16)
        d_queries, attended, d_keys, d_values = [], [], [], []
        for base, count in ((0, BIG), (BIG, REST)):
            keys = k_aug[base:base + count]
            values = v_aug[base:base + count]
            dk_t = jnp.zeros((128, count), F32)
            dv_t = jnp.zeros((128, count), F32)
            for row in range(base, base + count, 256):
                rows = slice(row, row + 256)
                prob = jnp.exp(nt(q_aug[rows], keys))
                prob_low = prob.astype(BF16)
                gathered = nn(prob_low, values)
                inverse = 1.0 / gathered[:, HD:HD + 1]
                out = jnp.where(low, gathered * inverse, 0.0)
                attended.append(out)
                scaled = jnp.where(low, da[rows] * inverse, 0.0).astype(BF16).astype(F32)
                dot = jnp.sum(scaled * out, axis=-1, keepdims=True)
                dot_high = dot.astype(BF16).astype(F32)
                d_aug = jnp.where(
                    lane == HD, -dot_high, jnp.where(lane == HD + 1, dot_high - dot, scaled)
                )
                d_low = d_aug.astype(BF16)
                d_score = (prob * nt(d_low, values)).astype(BF16)
                d_queries.append(nn(d_score, keys))
                dk_t = dk_t + nn(q_t[:, rows], d_score)
                dv_t = dv_t + nn(d_aug.T.astype(BF16), prob_low)
            d_keys.append(dk_t.T)
            d_values.append(dv_t.T)
        d_query = jnp.concatenate(d_queries, axis=0) * 0.125
        d_key = jnp.concatenate(d_keys, axis=0)
        d_value = jnp.concatenate(d_values, axis=0)
        attend = jnp.concatenate(attended, axis=0)
        d_qk = jnp.where(low, d_query, pltpu.roll(d_key, HD, 1))
        d_gain = d_gain + jnp.sum(d_qk * unit, axis=0, keepdims=True)
        scaled = d_qk * gain
        d_qk = spread * (scaled - half_mean(scaled) - unit * half_mean(scaled * unit))
        d_raw[:, 128 * head:128 * head + 128] = d_qk.astype(BF16)
        if head == 0:
            first_value = d_value
            att[:, 0:128] = jnp.where(low, 0.0, pltpu.roll(attend, HD, 1)).astype(BF16)
        elif head == 1:
            both = jnp.where(low, first_value, pltpu.roll(d_value, HD, 1))
            d_raw[:, 384:512] = both.astype(BF16)
            first_att = attend
        else:
            d_raw[:, 512:640] = jnp.where(low, d_value, 0.0).astype(BF16)
            both = jnp.where(low, first_att, pltpu.roll(attend, HD, 1))
            att[:, 128:256] = both.astype(BF16)
    g_gains[...] += d_gain
    d_projected = d_raw[...]
    attended = att[...]
    d_normed[...] += nt(d_projected, weights[0, :, :640])
    branch[...] += nt(attended, weights[0, :, 512:])
    left = nn(xt[...], d_projected)
    right = nn(dt[...], attended)
    g_weights[0, :, :512] = left[:, :512].astype(BF16)
    g_weights[0, :, 512:640] = (left[:, 512:] + right[:, :128]).astype(BF16)
    g_weights[0, :, 640:] = right[:, 128:].astype(BF16)

    @pl.when(step == pl.num_programs(0) - 1)
    def _():
        d_rows = d_normed[...].astype(BF16)
        b_rows = branch[...].astype(BF16)
        for k, out in enumerate((out0, out1, out2, out3)):
            out[0] = nn(pt[k], d_rows).astype(BF16)
            out[1] = nn(pt[k], b_rows).astype(BF16)


def attention_call(place, part, normed, grads, received, ids, gains, weights):
    width = normed.shape[-1]
    chunks = weights.shape[0]
    mp = ids.shape[1]
    own = pl.BlockSpec((1, PIECE, width), lambda m, place: (0, 0, 0))
    pair = pl.BlockSpec((2, PIECE, width), lambda m, place: (0, 0, 0))
    chunk = pl.BlockSpec((1, width, width), lambda m, place: (m, 0, 0))
    line = pl.BlockSpec((1, 128), lambda m, place: (0, 0))
    return pl.pallas_call(
        functools.partial(attention_kernel, part),
        grid_spec=pltpu.PrefetchScalarGridSpec(
            num_scalar_prefetch=1,
            grid=(chunks,),
            in_specs=[own, own, pair, pair, pair,
                      pl.BlockSpec((1, mp, PIECE), lambda m, place: (place[0], 0, 0)),
                      line, chunk],
            out_specs=[pair] * 4 + [chunk, line],
            scratch_shapes=[
                pltpu.VMEM((ROWS, width), BF16),
                pltpu.VMEM((ROWS, width), BF16),
                pltpu.VMEM((width, ROWS), BF16),
                pltpu.VMEM((width, ROWS), BF16),
                pltpu.VMEM((ROWS, 128), BF16),
                pltpu.VMEM((ROWS, 128), BF16),
                pltpu.VMEM((mp, PIECE, ROWS), BF16),
                pltpu.VMEM((ROWS, 640), F32),
                pltpu.VMEM((ROWS, 640), BF16),
                pltpu.VMEM((ROWS, 256), F32),
                pltpu.VMEM((ROWS, 256), BF16),
                pltpu.VMEM((ROWS, width), F32),
                pltpu.VMEM((ROWS, width), F32),
            ],
        ),
        out_shape=[jax.ShapeDtypeStruct((2, PIECE, width), BF16)] * 4
        + [jax.ShapeDtypeStruct(weights.shape, BF16), jax.ShapeDtypeStruct((1, 128), F32)],
        compiler_params=pltpu.CompilerParams(vmem_limit_bytes=VMEM),
        cost_estimate=pl.CostEstimate(
            flops=60_000_000_000, bytes_accessed=4 * chunks * width * width,
            transcendentals=ROWS * ROWS * 12,
        ),
        name="attention",
    )(place, normed, grads, *received, ids, gains, weights)


def finish_kernel(
    place, tok, cot, gain, branch, d_ff, ret0, ret1, ret2, ret3, output, input_grad, g_gain
):
    step = pl.program_id(0)
    part = tok.shape[1]

    @pl.when(step == 0)
    def _():
        g_gain[...] = jnp.zeros_like(g_gain)

    for index, back in enumerate((ret0, ret1, ret2, ret3)):

        @pl.when(step == index)
        def _():
            x = tok[0].astype(F32)
            output[0] = (x + (branch[0] + back[1].astype(F32))[:part]).astype(BF16)
            d_normed = (d_ff[0] + back[0].astype(F32))[:part]
            centered = x - jnp.mean(x, axis=-1, keepdims=True)
            spread = lax.rsqrt(jnp.mean(centered * centered, axis=-1, keepdims=True) + 1e-6)
            unit = centered * spread
            g_gain[...] += jnp.sum(d_normed * unit, axis=0, keepdims=True)
            scaled = d_normed * gain[...]
            d_x = spread * (
                scaled
                - jnp.mean(scaled, axis=-1, keepdims=True)
                - unit * jnp.mean(scaled * unit, axis=-1, keepdims=True)
            )
            input_grad[0] = cot[0].astype(F32) + d_x


def finish_call(place, tokens, cotangent, gain, branch, d_ff, returned):
    count, part, width = tokens.shape
    block = pl.BlockSpec(
        (1, part, width), lambda k, place: (lax.rem(place[0] + k, count), 0, 0)
    )
    padded = pl.BlockSpec((1, PIECE, width), lambda k, place: (k, 0, 0))
    pair = pl.BlockSpec((2, PIECE, width), lambda k, place: (0, 0, 0))
    line = pl.BlockSpec((1, width), lambda k, place: (0, 0))
    return pl.pallas_call(
        finish_kernel,
        grid_spec=pltpu.PrefetchScalarGridSpec(
            num_scalar_prefetch=1,
            grid=(count,),
            in_specs=[block, block, line, padded, padded] + [pair] * 4,
            out_specs=[block, block, line],
        ),
        out_shape=[
            jax.ShapeDtypeStruct(tokens.shape, BF16),
            jax.ShapeDtypeStruct(tokens.shape, F32),
            jax.ShapeDtypeStruct((1, width), F32),
        ],
        compiler_params=pltpu.CompilerParams(vmem_limit_bytes=VMEM),
        name="finish",
    )(place, tokens, cotangent, gain, branch, d_ff, *returned)


def pack_attention(w_qkv, w_proj):
    rows, wide = w_qkv.shape[1:]
    heads = wide // HD
    qk = w_qkv[:2].reshape(2, rows, heads, HD).transpose(1, 2, 0, 3).reshape(rows, 2 * wide)
    return jnp.concatenate([qk, w_qkv[2], w_proj.T], axis=1)


def unpack_attention(grad, wide):
    rows = grad.shape[0]
    heads = wide // HD
    qk = grad[:, :2 * wide].reshape(rows, heads, 2, HD).transpose(2, 0, 1, 3)
    qk = qk.reshape(2, rows, wide)
    g_qkv = jnp.concatenate([qk, grad[None, :, 2 * wide:3 * wide]], axis=0)
    return g_qkv, grad[:, 3 * wide:].T


def body(
    mp, tokens, w_qkv, w_up, w_proj, w_down, norm_gain, query_gain, key_gain, image_ids, cotangent
):
    micro, seqs, part, width = tokens.shape
    count = micro * seqs
    shard = w_up.shape[0]
    me = lax.axis_index("mp")
    place = me.astype(jnp.int32)[None]
    both = ("mp", "dp")
    w_attn = lax.all_gather(pack_attention(w_qkv, w_proj), both).reshape(mp, width, width)
    w_ff = lax.all_gather(jnp.stack([w_up, w_down.T]), both)
    w_ff = w_ff.reshape(mp, -1, 2, shard, width)
    w_upper = w_ff[:, :, 0].reshape(mp, width, width)
    w_lower = w_ff[:, :, 1].reshape(mp, width, width)

    tok = tokens.reshape(count, part, width)
    cot = cotangent.reshape(count, part, width)
    gain = norm_gain.reshape(1, width)
    normed, grads, *sends = norm_call(place, tok, cot, gain)
    received = [
        lax.ppermute(send, "mp", [(i, (i + k) % mp) for i in range(mp)])
        for k, send in enumerate(sends, 1)
    ]
    ids = image_ids.reshape(count, mp, part)
    ids = jnp.pad(ids, ((0, 0), (0, 0), (0, PIECE - part)), constant_values=-1)
    gains = jnp.concatenate([query_gain, key_gain]).reshape(1, 2 * HD)
    *outs, g_attn, g_gains = attention_call(
        place, part, normed, grads, received, ids, gains, w_attn
    )
    returned = [outs[0]] + [
        lax.ppermute(out, "mp", [(i, (i - k) % mp) for i in range(mp)])
        for k, out in enumerate(outs[1:], 1)
    ]
    branch, d_ff, g_up, g_down = feed_call(
        normed.reshape(count * PIECE, width), grads.reshape(count * PIECE, width), w_upper, w_lower
    )
    output, input_grad, g_norm = finish_call(
        place, tok, cot, gain,
        branch.reshape(count, PIECE, width), d_ff.reshape(count, PIECE, width), returned,
    )

    def scatter(grad):
        grad = grad.reshape(-1, shard, width)
        return lax.psum_scatter(grad, both, scatter_dimension=0).astype(F32)

    g_attn, g_up, g_down = scatter(g_attn), scatter(g_up), scatter(g_down)
    g_qkv, g_proj = unpack_attention(g_attn, w_qkv.shape[2])
    g_norm, g_gains = lax.psum((g_norm[0], g_gains[0]), ("dp", "mp"))
    return (
        output.reshape(tokens.shape),
        input_grad.reshape(tokens.shape),
        g_qkv,
        g_up,
        g_proj,
        g_down.T,
        g_norm,
        g_gains[:HD],
        g_gains[HD:],
    )


def solution(mesh):
    rows = P(None, "dp", "mp", None)
    weights = (P(None, "dp", "mp"), P("dp", "mp"), P("mp", "dp"), P("mp", "dp"))
    gains = (P(), P(), P())
    return jax.shard_map(
        functools.partial(body, mesh.shape["mp"]),
        mesh=mesh,
        in_specs=(rows,) + weights + gains + (P(None, "dp", None), rows),
        out_specs=(rows, rows) + weights + gains,
        check_vma=False,
    )
```

time: 1270 us -> 619 us (0.49)
  waiting for transfers between devices: 725 us -> 361 us
  matrix products: 229 us -> 0 us
  Pallas kernels: 0 us -> 136 us
  other arithmetic: 112 us -> 7.43 us
  local copies, waits for them, and re-layouts: 113 us -> 35.8 us
  blocking collectives: 70.3 us -> 40.4 us
    unnamed x16 -> x5, waiting for transfers between devices: 515 us -> 0.6 us
    dot_general x34 -> x0, matrix products: 225 us -> none  [the longest x2 35 us: backward_pass(): jnp.einsum('sqhd,skhd->shqk', d_heads, value_heads, preferred_element_typ...]
    reduce_scatter x2 -> x3, waiting for transfers between devices: 75.1 us -> 267 us  [scatter(): return lax.psum_scatter(grad, both, scatter_dimension=0).astype(F32)]
    pallas_call x0 -> x4, Pallas kernels: none -> 136 us  [the longest x1 83.2 us: attention_call(): pl.pallas_call(functools.partial(attention_kernel, part), grid_spec=pltpu...]
    all_gather x6 -> x2, waiting for transfers between devices: 135 us -> 42.1 us  [the longest x1 42.1 us: body(): lax.all_gather(pack_attention(w_qkv, w_proj), both)]
    reduce_sum x15 -> x0, other arithmetic: 52.3 us -> none  [the longest x2 22 us: forward_pass(): row_total = jnp.sum(jnp.exp(scores - row_peak), axis=-1, keepdims=True)]
    ppermute x0 -> x6, waiting for transfers between devices: none -> 52.2 us  [the longest x3 52.2 us: body(): lax.ppermute(send, 'mp', [(i, (i + k) % mp) for i in range(mp)])]
    convert_element_type x3 -> x2, other arithmetic: 37.4 us -> 2.6 us  [scatter(): return lax.psum_scatter(grad, both, scatter_dimension=0).astype(F32)]
  transfers between devices with their start and end apart: 12 -> 11, of which waited for: 7 -> 6; matrix products, arithmetic and copies ran while one was open for 35% -> 6% of each run, Pallas kernels for 0% -> 22%
where the time goes in v1:
time: 619 us; the launch traced here: 606 us
  waiting for transfers between devices  361 us (58%)
  Pallas kernels  136 us (22%)
  blocking collectives  40.4 us (7%)
  local copies, waits for them, and re-layouts  35.8 us (6%)
  between operations  14.2 us (2%)
  starting transfers between devices  11.4 us (2%)
  other arithmetic  7.43 us (1%)
    reduce_scatter x3, waiting for transfers between devices, scatter(): return lax.psum_scatter(grad, both, scatter_dimension=0).astype(F32)  267 us
    pallas_call x1, Pallas kernels, attention_call(): pl.pallas_call(functools.partial(attention_kernel, part), grid_spec=pltpu...  83.2 us
    ppermute x3, waiting for transfers between devices, body(): lax.ppermute(send, 'mp', [(i, (i + k) % mp) for i in range(mp)])  52.2 us
    all_gather x1, waiting for transfers between devices, body(): lax.all_gather(pack_attention(w_qkv, w_proj), both)  42.1 us
    psum x1, blocking collectives, body(): g_norm, g_gains = lax.psum((g_norm[0], g_gains[0]), ('dp', 'mp'))  40.4 us
    pallas_call x1, Pallas kernels, feed_call(): pl.pallas_call(feed_kernel, grid=(chunks,), in_specs=[whole, whole, chunk...  39 us
    unnamed x37, local copies, waits for them, and re-layouts  14.5 us
  transfers between devices with their start and end apart: 11, of which 6 were waited for; matrix products, arithmetic and copies ran while one was open for 6% of the time, Pallas kernels for 22%

profile of v1, /device:TPU:0, one launch (start us, length us, event | category | flops | bytes accessed | tf_op | source)
XLA Modules:
  0.0 606.4 jit_solution(9448021387070683526)
XLA Ops:
  7.2 0.0 all-gather.7.cloned.1.call-start
  7.2 1.0 slice.30
  8.2 0.9 slice.29
  9.1 0.1 copy.59
  9.2 0.1 copy.58
  9.4 0.8 pad_maximum_fusion.2
  10.2 0.8 copy.50
  11.0 0.0 all-gather.7.cloned.1.call-update
  11.0 0.0 all-gather.5.cloned.1.call-start
  11.1 1.7 pad_maximum_fusion
  12.8 0.0 all-gather.5.cloned.1.call-update
  12.8 0.0 copy-start.6
  12.8 0.0 reduce-scatter.4.cloned.1.call-start
  12.9 1.3 copy.43
  14.2 1.3 copy.44
  15.5 0.6 reshape.86.gain
  16.1 5.4 norm_rows.1
  21.5 3.1 collective-permute-start
  24.6 2.6 collective-permute-start.1
  27.2 1.3 collective-permute-start.2
  28.5 0.1 reshape.92
  28.6 0.6 pad.4.ids
  29.2 0.0 copy-done.13
  29.3 0.6 maximum_bitcast_fusion.gains
  29.8 16.7 %collective-permute-done.in1 = bf16[2,240,768]{2,1,0:T(8,128)(2,1)S(1)} collective-permute-done((bf16[2,240,768]{2,1,0:T(8,128)(2,1)}, bf16[2,240,768]{2,1,0:T(8,128)(2,1)S(1)}, u32[]{:S(2)}, u32[]{:S(2)}) %collective-permute-start) | collective-permute-done | bytes 737312 | tf_op jit(solution)/shard_map/ppermute | solution.py:431
  46.5 35.5 %collective-permute-done.1.in2 = bf16[2,240,768]{2,1,0:T(8,128)(2,1)S(1)} collective-permute-done((bf16[2,240,768]{2,1,0:T(8,128)(2,1)}, bf16[2,240,768]{2,1,0:T(8,128)(2,1)S(1)}, u32[]{:S(2)}, u32[]{:S(2)}) %collective-permute-start.1) | collective-permute-done | bytes 737312 | tf_op jit(solution)/shard_map/ppermute | solution.py:431
  82.0 0.0 collective-permute-done.2.in3
  82.0 42.1 %all-gather.7.cloned.1.call-done = bf16[3072,768]{1,0:T(8,128)(2,1)} async-done(((bf16[96,768]{1,0:T(8,128)(2,1)}), bf16[3072,768]{1,0:T(8,128)(2,1)}) %all-gather.7.cloned.1.call-update) | async-done | bytes 4718608 | tf_op jit(solution)/shard_map/all_gather | solution.py:420
  124.1 0.0 copy-done.11
  124.1 83.2 %attention.1 = (bf16[2,240,768]{2,1,0:T(8,128)(2,1)}, bf16[2,240,768]{2,1,0:T(8,128)(2,1)}, bf16[2,240,768]{2,1,0:T(8,128)(2,1)}, bf16[2,240,768]{2,1,0:T(8,128)...) custom-call(s32[1]{0:T(128)} %bitcast.place, bf16[4,240,768]{2,1,0:T(8,128)(2,1)} %get-tuple-element.27.own_x, ...), custom_call_target="tpu_custom_call" | custom-call | flops 60000002048 | bytes 9437184 | tf_op jit(solution)/shard_map/attention/pallas_call | solution.py:303
  207.3 8.0 %copy.51 = bf16[32,96,768]{1,2,0:T(8,128)(2,1)} copy(bf16[32,96,768]{2,1,0:T(8,128)(2,1)} %bitcast.59) | data formatting | bytes 9437184 | tf_op jit(solution)/shard_map/reshape | solution.py:453
  215.3 0.0 reduce-scatter.4.cloned.1.call-update
  215.3 0.0 reduce-scatter.6.cloned.1.call-start
  215.3 0.0 all-gather.5.cloned.1.call-done
  215.4 8.1 %fusion = (bf16[4,8,1,96,768]{4,3,2,1,0:T(8,128)(2,1)}, bf16[4,8,1,96,768]{4,3,2,1,0:T(8,128)(2,1)}) fusion(bf16[4,8,2,96,768]{4,3,2,1,0:T(8,128)(2,1)} %bitcast.56), kind=kLoop, calls=%fused_computation.9 | loop fusion | bytes 18874368 | tf_op jit(solution)/shard_map/slice | solution.py:424
  223.5 39.0 %feed_forward.1 = (f32[960,768]{1,0:T(8,128)}, f32[960,768]{1,0:T(8,128)}, bf16[4,768,768]{2,1,0:T(8,128)(2,1)}, bf16[4,768,768]{2,1,0:T(8,128)(2,1)}) custom-call(bf16[960,768]{1,0:T(8,128)(2,1)} %bitcast.76, bf16[960,768]{1,0:T(8,128)(2,1)} %bitcast.77, bf16[4,768,768]{2,1,0:T(8,128)(2,1)} %bitcast.61, bf16[4,768,768]{2,1,0:T(8,128)(2,1)} %bitcast.60), custom_call_target="tpu_custom_call" | custom-call | flops 27179089920 | bytes 18874368 | tf_op jit(solution)/shard_map/feed_forward/pallas_call | solution.py:113
  262.5 0.0 reduce-scatter.6.cloned.1.call-update
  262.5 0.0 copy-start.9
  262.5 0.0 reduce-scatter.8.cloned.1.call-start
  262.5 0.5 reduce-scatter.8.cloned.1.call-update
  263.1 2.2 collective-permute-start.3
  265.2 1.2 collective-permute-start.4
  266.5 0.0 copy-done.9
  266.5 0.8 collective-permute-start.5
  267.3 106.2 %reduce-scatter.4.cloned.1.call-done = bf16[1,96,768]{1,2,0:T(8,128)(2,1)} async-done(((bf16[32,96,768]{1,2,0:T(8,128)(2,1)}), bf16[1,96,768]{1,2,0:T(8,128)(2,1)}) %reduce-scatter.4.cloned.1.call-update) | async-done | bytes 147472 | tf_op jit(solution)/shard_map/reduce_scatter | solution.py:454
  373.4 1.0 bitcast_convert_fusion
  374.4 0.7 slice_bitcast_fusion
  375.1 0.9 copy.55
  376.0 0.0 collective-permute-done.3.ret1
  376.0 0.0 collective-permute-done.4.ret2
  376.0 0.0 collective-permute-done.5.ret3
  376.0 0.0 copy-start.4
  376.0 0.8 copy-done.2
  376.9 0.3 copy-done.3
  377.1 0.2 copy-done.4
  377.3 8.2 %finish.1 = (bf16[4,236,768]{2,1,0:T(8,128)(2,1)}, f32[4,236,768]{2,1,0:T(8,128)}, f32[1,768]{1,0:T(1,128)}) custom-call(s32[1]{0:T(128)} %bitcast.place, bf16[4,236,768]{2,1,0:T(8,128)(2,1)} %bitcast.53, bf16[4,236,768]{2,1,0:T(8,128)(2,1)} %bitcast.55, f32[1,768]{1,0:T(1,128)} %reshape.86.gain, f32[4,240,768]{2,1,0:T(8,128)} %bitcast.62, ...), custom_call_target="tpu_custom_call" | custom-call | tf_op jit(solution)/shard_map/finish/pallas_call | solution.py:377
  385.5 3.6 copy.53
  389.2 5.8 copy.54
  395.0 40.4 %all-reduce.1 = (f32[768]{0:T(1024)}, f32[128]{0:T(128)S(1)}) all-reduce(f32[768]{0:T(1024)S(1)} %reduce, f32[128]{0:T(128)S(1)} %bitcast.74), channel_id=1, replica_groups=mesh['dp'=8,'mp'=4] {'dp','mp'}, use_global_device_ids=true, to_apply=%region_3.4 | all-reduce | flops 896 | bytes 7168 | tf_op jit(solution)/shard_map/psum | solution.py:458
  435.3 0.6 fusion.1
  435.9 50.7 %reduce-scatter.6.cloned.1.call-done = bf16[1,96,768]{2,1,0:T(8,128)(2,1)} async-done(((bf16[32,96,768]{2,1,0:T(8,128)(2,1)}), bf16[1,96,768]{2,1,0:T(8,128)(2,1)}) %reduce-scatter.6.cloned.1.call-update) | async-done | bytes 147472 | tf_op jit(solution)/shard_map/reduce_scatter | solution.py:454
  486.6 1.6 bitcast_convert_fusion.1
  488.2 109.8 %reduce-scatter.8.cloned.1.call-done = bf16[1,96,768]{2,1,0:T(8,128)(2,1)} async-done(((bf16[32,96,768]{2,1,0:T(8,128)(2,1)}), bf16[1,96,768]{2,1,0:T(8,128)(2,1)}) %reduce-scatter.8.cloned.1.call-update) | async-done | bytes 147472 | tf_op jit(solution)/shard_map/reduce_scatter | solution.py:454
  598.0 1.6 convert_bitcast_fusion
  (26 shorter events, 0.1 us)
Async XLA Ops:
  7.2 5.7 copy-start
  7.2 7.0 %copy-start.1 = (bf16[2,2,236,768]{3,1,2,0:T(2,128)(2,1)S(1)}, bf16[2,2,236,768]{3,1,2,0:T(2,128)(2,1)}, u32[]{:S(2)}) copy-start(bf16[2,2,236,768]{3,1,2,0:T(2,128)(2,1)} %param.19) | copy-start | bytes 4349956
  7.2 116.9 %all-gather.7.cloned.1.call-start = ((), (), s32[]{:S(2)}) async-start(), calls=%async_computation.7 | async-start | bytes 4866048 | tf_op jit(solution)/shard_map/all_gather | solution.py:420
  11.0 204.3 %all-gather.5.cloned.1.call-start = ((), (), s32[]{:S(2)}) async-start(), calls=%async_computation.6 | async-start | bytes 9732096 | tf_op jit(solution)/shard_map/all_gather | solution.py:421
  12.8 2.7 copy-start.6
  12.8 360.6 %reduce-scatter.4.cloned.1.call-start = ((), (), s32[]{:S(2)}) async-start(), calls=%async_computation.3 | async-start | bytes 6488064 | tf_op jit(solution)/shard_map/reduce_scatter | solution.py:454
  14.2 14.3 %copy-start.5 = (s32[2,2,944]{2,1,0:T(2,128)S(1)}, s32[2,2,944]{2,1,0:T(2,128)}, u32[]{:S(2)}) copy-start(s32[2,2,944]{2,1,0:T(2,128)} %param.18) | copy-start | bytes 45316
  14.2 15.1 %copy-start.13 = (f32[64]{0:T(128)S(1)}, f32[64]{0:T(128)}, u32[]{:S(2)}) copy-start(f32[64]{0:T(128)} %param.17) | copy-start | bytes 772
  14.2 15.1 %copy-start.14 = (f32[64]{0:T(128)S(1)}, f32[64]{0:T(128)}, u32[]{:S(2)}) copy-start(f32[64]{0:T(128)} %param.16) | copy-start | bytes 772
  21.5 25.0 %collective-permute-start = (bf16[2,240,768]{2,1,0:T(8,128)(2,1)}, bf16[2,240,768]{2,1,0:T(8,128)(2,1)S(1)}, u32[]{:S(2)}, u32[]{:S(2)}) collective-permute-start(bf16[2,240,768]{2,1,0:T(8,128)(2,1)} %get-tuple-element.31), channel_id=1, source_target_pairs={{0,1},{1,2},{2,3},{3,0},{4,5},{5,6},{6,7},{7,4},{8,9},{9,10},{10,1... | collective-permute-start | bytes 2211848 | tf_op jit(solution)/shard_map/ppermute | solution.py:431
  24.6 57.4 %collective-permute-start.1 = (bf16[2,240,768]{2,1,0:T(8,128)(2,1)}, bf16[2,240,768]{2,1,0:T(8,128)(2,1)S(1)}, u32[]{:S(2)}, u32[]{:S(2)}) collective-permute-start(bf16[2,240,768]{2,1,0:T(8,128)(2,1)} %get-tuple-element.32), channel_id=1, source_target_pairs={{0,2},{1,3},{2,0},{3,1},{4,6},{5,7},{6,4},{7,5},{8,10},{9,11},{10,... | collective-permute-start | bytes 2211848 | tf_op jit(solution)/shard_map/ppermute | solution.py:431
  27.2 54.8 %collective-permute-start.2 = (bf16[2,240,768]{2,1,0:T(8,128)(2,1)}, bf16[2,240,768]{2,1,0:T(8,128)(2,1)S(1)}, u32[]{:S(2)}, u32[]{:S(2)}) collective-permute-start(bf16[2,240,768]{2,1,0:T(8,128)(2,1)} %get-tuple-element.33), channel_id=1, source_target_pairs={{0,3},{1,0},{2,1},{3,2},{4,7},{5,4},{6,5},{7,6},{8,11},{9,8},{10,9... | collective-permute-start | bytes 2211848 | tf_op jit(solution)/shard_map/ppermute | solution.py:431
  46.5 77.6 %copy-start.10 = (bf16[2,240,768]{2,1,0:T(8,128)(2,1)}, bf16[2,240,768]{2,1,0:T(8,128)(2,1)S(1)}, u32[]{:S(2)}) copy-start(bf16[2,240,768]{2,1,0:T(8,128)(2,1)S(1)} %collective-permute-done.in1) | copy-start | bytes 2211844
  82.0 42.1 %copy-start.11 = (bf16[2,240,768]{2,1,0:T(8,128)(2,1)}, bf16[2,240,768]{2,1,0:T(8,128)(2,1)S(1)}, u32[]{:S(2)}) copy-start(bf16[2,240,768]{2,1,0:T(8,128)(2,1)S(1)} %collective-permute-done.1.in2) | copy-start | bytes 2211844
  82.0 42.1 %copy-start.12 = (bf16[2,240,768]{2,1,0:T(8,128)(2,1)}, bf16[2,240,768]{2,1,0:T(8,128)(2,1)S(1)}, u32[]{:S(2)}) copy-start(bf16[2,240,768]{2,1,0:T(8,128)(2,1)S(1)} %collective-permute-done.2.in3) | copy-start | bytes 2211844
  215.3 271.3 %reduce-scatter.6.cloned.1.call-start = ((), (), s32[]{:S(2)}) async-start(), calls=%async_computation.4 | async-start | bytes 4866048 | tf_op jit(solution)/shard_map/reduce_scatter | solution.py:454
  262.5 4.0 copy-start.9
  262.5 335.5 %reduce-scatter.8.cloned.1.call-start = ((), (), s32[]{:S(2)}) async-start(), calls=%async_computation.5 | async-start | bytes 4866048 | tf_op jit(solution)/shard_map/reduce_scatter | solution.py:454
  263.1 112.9 %collective-permute-start.3 = (bf16[2,240,768]{2,1,0:T(8,128)(2,1)}, bf16[2,240,768]{2,1,0:T(8,128)(2,1)S(1)}, u32[]{:S(2)}, u32[]{:S(2)}) collective-permute-start(bf16[2,240,768]{2,1,0:T(8,128)(2,1)} %get-tuple-element.35), channel_id=1, source_target_pairs={{0,3},{1,0},{2,1},{3,2},{4,7},{5,4},{6,5},{7,6},{8,11},{9,8},{10,9... | collective-permute-start | bytes 2211848 | tf_op jit(solution)/shard_map/ppermute | solution.py:441
  265.2 110.8 %collective-permute-start.4 = (bf16[2,240,768]{2,1,0:T(8,128)(2,1)}, bf16[2,240,768]{2,1,0:T(8,128)(2,1)S(1)}, u32[]{:S(2)}, u32[]{:S(2)}) collective-permute-start(bf16[2,240,768]{2,1,0:T(8,128)(2,1)} %get-tuple-element.36), channel_id=1, source_target_pairs={{0,2},{1,3},{2,0},{3,1},{4,6},{5,7},{6,4},{7,5},{8,10},{9,11},{10,... | collective-permute-start | bytes 2211848 | tf_op jit(solution)/shard_map/ppermute | solution.py:441
  266.5 109.6 %collective-permute-start.5 = (bf16[2,240,768]{2,1,0:T(8,128)(2,1)S(1)}, bf16[2,240,768]{2,1,0:T(8,128)(2,1)S(1)}, u32[]{:S(2)}, u32[]{:S(2)}) collective-permute-start(bf16[2,240,768]{2,1,0:T(8,128)(2,1)S(1)} %copy-done.9), channel_id=1, source_target_pairs={{0,1},{1,2},{2,3},{3,0},{4,5},{5,6},{6,7},{7,4},{8,9},{9,10},{10,1... | collective-permute-start | bytes 2211848 | tf_op jit(solution)/shard_map/ppermute | solution.py:441
  376.0 0.9 copy-start.2
  376.0 1.1 copy-start.3
  376.0 1.3 copy-start.4
  389.2 5.8 copy-start.7
  389.2 5.8 copy-start.8
Sparse Core Ops, SparseCore 0:
  11.5 112.5 all-gather.6
  127.6 80.8 all-gather.4
  215.4 157.9 reduce-scatter.3
  379.7 106.8 reduce-scatter.5
  491.9 106.0 reduce-scatter.7

commit v2 on v1

--- a/solution.py
+++ b/solution.py
@@ -81,13 +81,8 @@
         dt[...] = dy.T
 
     up = nn(x, w_up[0])
-    inner = 0.7978845608028654 * (up + 0.044715 * up * up * up)
-    th = jnp.tanh(inner)
-    half = 0.5 * (1.0 + th)
-    hidden = (up * half).astype(BF16)
-    slope = half + 0.5 * up * (1.0 - th * th) * (
-        0.7978845608028654 * (1.0 + 3 * 0.044715 * up * up)
-    )
+    value, slope = gelu_parts(up)
+    hidden = value.astype(BF16)
     d_up = (nn(dy, w_down[0]) * slope).astype(BF16)
     g_up[0] = nn(xt[...], d_up).astype(BF16)
     g_down[0] = nn(dt[...], hidden).astype(BF16)
@@ -128,6 +123,300 @@
     )(normed, grads, w_up, w_down)
 
 
+def gelu_parts(up):
+    inner = 0.7978845608028654 * (up + 0.044715 * up * up * up)
+    th = jnp.tanh(inner)
+    half = 0.5 * (1.0 + th)
+    slope = half + 0.5 * up * (1.0 - th * th) * (
+        0.7978845608028654 * (1.0 + 3 * 0.044715 * up * up)
+    )
+    return up * half, slope
+
+
+def feed_remote_kernel(
+    x_ref, dy_ref, w_hbm, g_attn, gain, gains_in,
+    branch, d_normed, out_attn, out_up, out_down, out_gains,
+    xt, dt, w_buf, g_ff, got_core, got_first, got_second, got_z, sums, got_sums, z_sums,
+    w_sem, send_sem, recv_sem, z_send, z_recv, sum_send, sum_recv,
+):
+    width = x_ref.shape[1]
+    steps, shard = w_hbm.shape[0], w_hbm.shape[3]
+    d = lax.axis_index("dp")
+    z = lax.axis_index("mp")
+    core, x, y = d % 2, (d // 2) % 2, d // 4
+    sibling, beside, above = d + 1 - 2 * core, d + 2 - 4 * x, d + 4 - 8 * y
+    half = width // 2
+    items = ((0, slice(0, half), True), (0, slice(half, width), False),
+             (1, slice(0, width), True), (2, slice(0, width), False))
+
+    def part_of(step):
+        return lax.rem(z + 1 + step, steps)
+
+    barrier = pltpu.get_barrier_semaphore()
+    for other in (sibling, beside, above):
+        pl.semaphore_signal(barrier, 1, device_id={"dp": other, "mp": z},
+                            device_id_type=pl.DeviceIdType.MESH)
+    for k in range(1, steps):
+        pl.semaphore_signal(barrier, 1, device_id={"dp": d, "mp": lax.rem(z + k, steps)},
+                            device_id_type=pl.DeviceIdType.MESH)
+    pl.semaphore_wait(barrier, steps + 2)
+
+    def remote(src, dst, send, recv, dp_to, z_to):
+        return pltpu.make_async_remote_copy(
+            src_ref=src, dst_ref=dst, send_sem=send, recv_sem=recv,
+            device_id={"dp": dp_to, "mp": z_to}, device_id_type=pl.DeviceIdType.MESH,
+        )
+
+    def core_copy(step, item):
+        kind, cols, _ = items[item]
+        if kind == 0:
+            src = g_attn.at[part_of(step), :, :, 1 - core, :, cols]
+        else:
+            src = g_ff.at[step, kind - 1, :, :, 1 - core, :, cols]
+        dst = got_core.at[step, kind, :, :, :, cols]
+        sem = (0, item, step)
+        return remote(src, dst, send_sem.at[sem], recv_sem.at[sem], sibling, z)
+
+    def first_copy(step, item):
+        kind, cols, x_first = items[item]
+        dst = got_first.at[step, kind, :, :, cols]
+        sem = (1, item, step)
+        if x_first:
+            src = got_core.at[step, kind, :, 1 - x, :, cols]
+        else:
+            src = got_core.at[step, kind, 1 - y, :, :, cols]
+        return remote(src, dst, send_sem.at[sem], recv_sem.at[sem], beside if x_first else above, z)
+
+    def second_copy(step, item):
+        kind, cols, x_first = items[item]
+        src = got_first.at[step, kind, 1 - y if x_first else 1 - x, :, cols]
+        dst = got_second.at[step, kind, :, cols]
+        sem = (2, item, step)
+        return remote(src, dst, send_sem.at[sem], recv_sem.at[sem], above if x_first else beside, z)
+
+    def z_copy(step, kind):
+        return remote(got_second.at[step, kind], got_z.at[kind, step],
+                      z_send.at[kind, step], z_recv.at[kind, step], d, part_of(step))
+
+    def after_core(step, chosen):
+        for item in chosen:
+            kind, cols, _ = items[item]
+            core_copy(step, item).wait_recv()
+            for row in ((0, 0), (0, 1), (1, 0), (1, 1)):
+                if kind == 0:
+                    own = g_attn[(part_of(step), *row, core, slice(None), cols)]
+                else:
+                    own = g_ff[(step, kind - 1, *row, core, slice(None), cols)]
+                place = (step, kind, *row, slice(None), cols)
+                got_core[place] = (own.astype(F32) + got_core[place].astype(F32)).astype(BF16)
+            first_copy(step, item).start()
+
+    def after_first(step, chosen):
+        for item in chosen:
+            kind, cols, x_first = items[item]
+            first_copy(step, item).wait_recv()
+            for row in range(2):
+                if x_first:
+                    own = got_core[step, kind, row, x, :, cols]
+                else:
+                    own = got_core[step, kind, y, row, :, cols]
+                total = own.astype(F32) + got_first[step, kind, row, :, cols].astype(F32)
+                got_first[step, kind, row, :, cols] = total.astype(BF16)
+            second_copy(step, item).start()
+
+    def second_sum(step, item):
+        kind, cols, x_first = items[item]
+        second_copy(step, item).wait_recv()
+        own = got_first[step, kind, y if x_first else x, :, cols]
+        return own.astype(F32) + got_second[step, kind, :, cols].astype(F32)
+
+    def after_second(step, chosen):
+        for item in chosen:
+            kind, cols, _ = items[item]
+            got_second[step, kind, :, cols] = second_sum(step, item).astype(BF16)
+        for kind in sorted({items[item][0] for item in chosen}):
+            z_copy(step, kind).start()
+
+    def finish_sum(chosen, out):
+        step = steps - 1
+        for item in chosen:
+            kind, cols, _ = items[item]
+            total = second_sum(step, item)
+            for slot in range(steps - 1):
+                total = total + got_z[kind, slot, :, cols].astype(F32)
+            out[:, cols] = total
+
+    def w_copy(step, kind):
+        slot = lax.rem(step, 2)
+        return pltpu.make_async_copy(
+            w_hbm.at[part_of(step), :, kind], w_buf.at[slot, kind], w_sem.at[slot, kind]
+        )
+
+    def feed_half(step, index):
+        cols = slice(half * index, half * index + half)
+        slot = lax.rem(step, 2)
+        upper = w_buf[slot, 0, :, :, cols].reshape(width, half)
+        lower = w_buf[slot, 1, :, :, cols].reshape(width, half)
+        value, slope = gelu_parts(nn(x_ref[...], upper))
+        hidden = value.astype(BF16)
+        d_up = (nn(dy_ref[...], lower) * slope).astype(BF16)
+        split = (2, 2, 2, shard, half)
+        g_ff[step, 0, :, :, :, :, cols] = nn(xt[...], d_up).astype(BF16).reshape(split)
+        g_ff[step, 1, :, :, :, :, cols] = nn(dt[...], hidden).astype(BF16).reshape(split)
+        branch[...] += nt(hidden, lower)
+        d_normed[...] += nt(d_up, upper)
+
+    attn, feed = (0, 1), (2, 3)
+    for step in range(steps):
+        for item in attn:
+            core_copy(step, item).start()
+    for kind in range(2):
+        w_copy(0, kind).start()
+    xt[...] = x_ref[...].T
+    dt[...] = dy_ref[...].T
+    branch[...] = jnp.zeros_like(branch)
+    d_normed[...] = jnp.zeros_like(d_normed)
+
+    def one_step(step, carry):
+        for kind in range(2):
+            w_copy(step, kind).wait()
+
+        @pl.when(step + 1 < steps)
+        def _():
+            for kind in range(2):
+                w_copy(step + 1, kind).start()
+
+        feed_half(step, 0)
+
+        @pl.when(step >= 1)
+        def _():
+            after_core(step - 1, feed)
+
+        after_core(step, attn)
+
+        @pl.when(step >= 2)
+        def _():
+            after_second(step - 2, feed)
+
+        feed_half(step, 1)
+        for item in feed:
+            core_copy(step, item).start()
+
+        @pl.when(step >= 1)
+        def _():
+            after_first(step - 1, feed)
+
+        after_first(step, attn)
+
+        @pl.when(step >= 1)
+        def _():
+            after_second(step - 1, attn)
+
+        return carry
+
+    lax.fori_loop(0, steps, one_step, 0)
+    last = steps - 1
+
+    sums[0] = gains_in[...]
+    store_gain(sums.at[0], d_normed[...], x_ref[...], gain[...])
+
+    def sum_copy(stage):
+        to = (sibling, beside, above)[stage]
+        return remote(sums.at[stage], got_sums.at[stage], sum_send.at[stage], sum_recv.at[stage],
+                      to, z)
+
+    def sum_z_copy(k):
+        return remote(sums.at[3], z_sums.at[z], sum_send.at[2 + k], sum_recv.at[2 + k],
+                      d, lax.rem(z + k, steps))
+
+    def next_sum(stage):
+        sum_copy(stage).wait_recv()
+        sums[stage + 1] = sums[stage] + got_sums[stage]
+
+    sum_copy(0).start()
+    after_core(last, feed)
+    next_sum(0)
+    sum_copy(1).start()
+    after_second(last - 1, feed)
+    next_sum(1)
+    sum_copy(2).start()
+    after_first(last, feed)
+    next_sum(2)
+    for k in range(1, steps):
+        sum_z_copy(k).start()
+    z_sums[z] = sums[3]
+    for step in range(last):
+        z_copy(step, 0).wait_recv()
+    finish_sum(attn, out_attn)
+    for step in range(last):
+        z_copy(step, 1).wait_recv()
+        z_copy(step, 2).wait_recv()
+    finish_sum(feed[:1], out_up)
+    finish_sum(feed[1:], out_down)
+    for k in range(1, steps):
+        sum_z_copy(k).wait_recv()
+    total = z_sums[0]
+    for k in range(1, steps):
+        total = total + z_sums[k]
+    out_gains[...] = total
+
+    for step in range(steps):
+        for item in range(4):
+            core_copy(step, item).wait_send()
+            first_copy(step, item).wait_send()
+            second_copy(step, item).wait_send()
+    for step in range(last):
+        for kind in range(3):
+            z_copy(step, kind).wait_send()
+    for stage in range(3):
+        sum_copy(stage).wait_send()
+    for k in range(1, steps):
+        sum_z_copy(k).wait_send()
+
+
+def feed_remote_call(normed, grads, w_ff, g_attn, gain, gains):
+    rows, width = normed.shape
+    steps, _, _, shard, _ = w_ff.shape
+    vmem = pl.BlockSpec(memory_space=pltpu.VMEM)
+    return pl.pallas_call(
+        feed_remote_kernel,
+        in_specs=[vmem, vmem, pl.BlockSpec(memory_space=pl.ANY), vmem, vmem, vmem],
+        out_specs=[vmem] * 6,
+        out_shape=[jax.ShapeDtypeStruct((rows, width), F32)] * 2
+        + [jax.ShapeDtypeStruct((shard, width), F32)] * 3
+        + [jax.ShapeDtypeStruct((8, 128), F32)],
+        scratch_shapes=[
+            pltpu.VMEM((width, rows), BF16),
+            pltpu.VMEM((width, rows), BF16),
+            pltpu.VMEM((2, 2, 8, shard, width), BF16),
+            pltpu.VMEM((steps, 2, 2, 2, 2, shard, width), BF16),
+            pltpu.VMEM((steps, 3, 2, 2, shard, width), BF16),
+            pltpu.VMEM((steps, 3, 2, shard, width), BF16),
+            pltpu.VMEM((steps, 3, shard, width), BF16),
+            pltpu.VMEM((3, steps - 1, shard, width), BF16),
+            pltpu.VMEM((4, 8, 128), F32),
+            pltpu.VMEM((3, 8, 128), F32),
+            pltpu.VMEM((steps, 8, 128), F32),
+            pltpu.SemaphoreType.DMA((2, 2)),
+            pltpu.SemaphoreType.DMA((3, 4, steps)),
+            pltpu.SemaphoreType.DMA((3, 4, steps)),
+            pltpu.SemaphoreType.DMA((3, steps - 1)),
+            pltpu.SemaphoreType.DMA((3, steps - 1)),
+            pltpu.SemaphoreType.DMA((6,)),
+            pltpu.SemaphoreType.DMA((6,)),
+        ],
+        compiler_params=pltpu.CompilerParams(
+            collective_id=0, has_side_effects=True, vmem_limit_bytes=VMEM
+        ),
+        cost_estimate=pl.CostEstimate(
+            flops=12 * rows * width * width * steps,
+            bytes_accessed=4 * steps * width * width * 2,
+            transcendentals=rows * width * steps,
+        ),
+        name="feed_forward_scatter",
+    )(normed, grads, w_ff, g_attn, gain, gains)
+
+
 def iota(shape, axis):
     return lax.broadcasted_iota(jnp.int32, shape, axis)
 
@@ -139,8 +428,14 @@
     return jnp.where((rest >= 0) & (rest < total - MOST), other, held)
 
 
+def store_gain(out, d_normed, normed, gain):
+    total = jnp.sum(d_normed * normed.astype(F32), axis=0, keepdims=True) / gain
+    for row in range(total.shape[1] // 128):
+        out[row:row + 1] += total[:, 128 * row:128 * row + 128]
+
+
 def attention_kernel(
-    part, place, own_x, own_dy, in1, in2, in3, ids, gains, weights,
+    part, place, own_x, own_dy, in1, in2, in3, ids, gains, norm_gain, weights,
     out0, out1, out2, out3, g_weights, g_gains,
     x_ref, dy_ref, xt, dt, feat_q, feat_k, pt, raw, d_raw, d_att, att, d_normed, branch,
 ):
@@ -272,7 +567,7 @@
             d_raw[:, 512:640] = jnp.where(low, d_value, 0.0).astype(BF16)
             both = jnp.where(low, first_att, pltpu.roll(attend, HD, 1))
             att[:, 128:256] = both.astype(BF16)
-    g_gains[...] += d_gain
+    g_gains[6:7] += d_gain
     d_projected = d_raw[...]
     attended = att[...]
     d_normed[...] += nt(d_projected, weights[0, :, :640])
@@ -285,6 +580,7 @@
 
     @pl.when(step == pl.num_programs(0) - 1)
     def _():
+        store_gain(g_gains, d_normed[...], x_ref[...], norm_gain[...])
         d_rows = d_normed[...].astype(BF16)
         b_rows = branch[...].astype(BF16)
         for k, out in enumerate((out0, out1, out2, out3)):
@@ -292,7 +588,7 @@
             out[1] = nn(pt[k], b_rows).astype(BF16)
 
 
-def attention_call(place, part, normed, grads, received, ids, gains, weights):
+def attention_call(place, part, normed, grads, received, ids, gains, norm_gain, weights):
     width = normed.shape[-1]
     chunks = weights.shape[0]
     mp = ids.shape[1]
@@ -307,8 +603,8 @@
             grid=(chunks,),
             in_specs=[own, own, pair, pair, pair,
                       pl.BlockSpec((1, mp, PIECE), lambda m, place: (place[0], 0, 0)),
-                      line, chunk],
-            out_specs=[pair] * 4 + [chunk, line],
+                      line, pl.BlockSpec((1, width), lambda m, place: (0, 0)), chunk],
+            out_specs=[pair] * 4 + [chunk, pl.BlockSpec((8, 128), lambda m, place: (0, 0))],
             scratch_shapes=[
                 pltpu.VMEM((ROWS, width), BF16),
                 pltpu.VMEM((ROWS, width), BF16),
@@ -326,25 +622,21 @@
             ],
         ),
         out_shape=[jax.ShapeDtypeStruct((2, PIECE, width), BF16)] * 4
-        + [jax.ShapeDtypeStruct(weights.shape, BF16), jax.ShapeDtypeStruct((1, 128), F32)],
+        + [jax.ShapeDtypeStruct(weights.shape, BF16), jax.ShapeDtypeStruct((8, 128), F32)],
         compiler_params=pltpu.CompilerParams(vmem_limit_bytes=VMEM),
         cost_estimate=pl.CostEstimate(
             flops=60_000_000_000, bytes_accessed=4 * chunks * width * width,
             transcendentals=ROWS * ROWS * 12,
         ),
         name="attention",
-    )(place, normed, grads, *received, ids, gains, weights)
+    )(place, normed, grads, *received, ids, gains, norm_gain, weights)
 
 
 def finish_kernel(
-    place, tok, cot, gain, branch, d_ff, ret0, ret1, ret2, ret3, output, input_grad, g_gain
+    place, tok, cot, gain, branch, d_ff, ret0, ret1, ret2, ret3, output, input_grad
 ):
     step = pl.program_id(0)
     part = tok.shape[1]
-
-    @pl.when(step == 0)
-    def _():
-        g_gain[...] = jnp.zeros_like(g_gain)
 
     for index, back in enumerate((ret0, ret1, ret2, ret3)):
 
@@ -356,7 +648,6 @@
             centered = x - jnp.mean(x, axis=-1, keepdims=True)
             spread = lax.rsqrt(jnp.mean(centered * centered, axis=-1, keepdims=True) + 1e-6)
             unit = centered * spread
-            g_gain[...] += jnp.sum(d_normed * unit, axis=0, keepdims=True)
             scaled = d_normed * gain[...]
             d_x = spread * (
                 scaled
@@ -380,12 +671,11 @@
             num_scalar_prefetch=1,
             grid=(count,),
             in_specs=[block, block, line, padded, padded] + [pair] * 4,
-            out_specs=[block, block, line],
+            out_specs=[block, block],
         ),
         out_shape=[
             jax.ShapeDtypeStruct(tokens.shape, BF16),
             jax.ShapeDtypeStruct(tokens.shape, F32),
-            jax.ShapeDtypeStruct((1, width), F32),
         ],
         compiler_params=pltpu.CompilerParams(vmem_limit_bytes=VMEM),
         name="finish",
@@ -409,7 +699,7 @@
 
 
 def body(
-    mp, tokens, w_qkv, w_up, w_proj, w_down, norm_gain, query_gain, key_gain, image_ids, cotangent
+    dp, mp, tokens, w_qkv, w_up, w_proj, w_down, norm_gain, query_gain, key_gain, image_ids, cotangent
 ):
     micro, seqs, part, width = tokens.shape
     count = micro * seqs
@@ -418,10 +708,6 @@
     place = me.astype(jnp.int32)[None]
     both = ("mp", "dp")
     w_attn = lax.all_gather(pack_attention(w_qkv, w_proj), both).reshape(mp, width, width)
-    w_ff = lax.all_gather(jnp.stack([w_up, w_down.T]), both)
-    w_ff = w_ff.reshape(mp, -1, 2, shard, width)
-    w_upper = w_ff[:, :, 0].reshape(mp, width, width)
-    w_lower = w_ff[:, :, 1].reshape(mp, width, width)
 
     tok = tokens.reshape(count, part, width)
     cot = cotangent.reshape(count, part, width)
@@ -434,28 +720,42 @@
     ids = image_ids.reshape(count, mp, part)
     ids = jnp.pad(ids, ((0, 0), (0, 0), (0, PIECE - part)), constant_values=-1)
     gains = jnp.concatenate([query_gain, key_gain]).reshape(1, 2 * HD)
+    w_ff, received = lax.optimization_barrier((jnp.stack([w_up, w_down.T]), received))
+    w_ff = lax.all_gather(w_ff, both).reshape(mp, dp, 2, shard, width)
     *outs, g_attn, g_gains = attention_call(
-        place, part, normed, grads, received, ids, gains, w_attn
+        place, part, normed, grads, received, ids, gains, gain, w_attn
     )
     returned = [outs[0]] + [
         lax.ppermute(out, "mp", [(i, (i - k) % mp) for i in range(mp)])
         for k, out in enumerate(outs[1:], 1)
     ]
-    branch, d_ff, g_up, g_down = feed_call(
-        normed.reshape(count * PIECE, width), grads.reshape(count * PIECE, width), w_upper, w_lower
-    )
-    output, input_grad, g_norm = finish_call(
+    flat_normed = normed.reshape(count * PIECE, width)
+    flat_grads = grads.reshape(count * PIECE, width)
+    if (dp, mp) == (8, 4):
+        branch, d_ff, g_attn, g_up, g_down, g_gains = feed_remote_call(
+            flat_normed, flat_grads, w_ff, g_attn.reshape(mp, 2, 2, 2, shard, width), gain, g_gains
+        )
+    else:
+        branch, d_ff, g_up, g_down = feed_call(
+            flat_normed, flat_grads,
+            w_ff[:, :, 0].reshape(mp, width, width), w_ff[:, :, 1].reshape(mp, width, width),
+        )
+        g_attn, g_up, g_down = (
+            lax.psum_scatter(
+                grad.reshape(-1, shard, width), both, scatter_dimension=0
+            ).astype(F32)
+            for grad in (g_attn, g_up, g_down)
+        )
+        own = jnp.sum(d_ff * flat_normed.astype(F32), axis=0) / norm_gain
+        g_gains = g_gains.at[:width // 128].add(own.reshape(-1, 128))
+        g_gains = lax.psum(g_gains, ("dp", "mp"))
+    output, input_grad = finish_call(
         place, tok, cot, gain,
         branch.reshape(count, PIECE, width), d_ff.reshape(count, PIECE, width), returned,
     )
-
-    def scatter(grad):
-        grad = grad.reshape(-1, shard, width)
-        return lax.psum_scatter(grad, both, scatter_dimension=0).astype(F32)
-
-    g_attn, g_up, g_down = scatter(g_attn), scatter(g_up), scatter(g_down)
     g_qkv, g_proj = unpack_attention(g_attn, w_qkv.shape[2])
-    g_norm, g_gains = lax.psum((g_norm[0], g_gains[0]), ("dp", "mp"))
+    g_norm = g_gains[:width // 128].reshape(width)
+    g_gains = g_gains[6]
     return (
         output.reshape(tokens.shape),
         input_grad.reshape(tokens.shape),
@@ -474,7 +774,7 @@
     weights = (P(None, "dp", "mp"), P("dp", "mp"), P("mp", "dp"), P("mp", "dp"))
     gains = (P(), P(), P())
     return jax.shard_map(
-        functools.partial(body, mesh.shape["mp"]),
+        functools.partial(body, mesh.shape["dp"], mesh.shape["mp"]),
         mesh=mesh,
         in_specs=(rows,) + weights + gains + (P(None, "dp", None), rows),
         out_specs=(rows, rows) + weights + gains,

time: 619 us -> 357 us (0.58); the launches traced: 606 us -> 357 us
  waiting for transfers between devices: 361 us -> 94.4 us
  Pallas kernels: 136 us -> 211 us
  blocking collectives: 40.4 us -> 0 us
  local copies, waits for them, and re-layouts: 35.8 us -> 22.8 us
    reduce_scatter x3 -> x0, waiting for transfers between devices: 267 us -> none  [scatter(): return lax.psum_scatter(grad, both, scatter_dimension=0).astype(F32)]
    pallas_call x1, Pallas kernels: 39 us -> 106 us  [feed_remote_call(): pl.pallas_call(feed_remote_kernel, in_specs=[vmem, vmem, pl.BlockSpec(mem...]
    psum x1 -> x0, blocking collectives: 40.4 us -> none  [body(): g_norm, g_gains = lax.psum((g_norm[0], g_gains[0]), ('dp', 'mp'))]
    pallas_call x1, Pallas kernels: 83.2 us -> 92 us  [attention_call(): pl.pallas_call(functools.partial(attention_kernel, part), grid_spec=pltpu...]
    slice x1 -> x0, local copies, waits for them, and re-layouts: 8.13 us -> none  [body(): w_lower = w_ff[:, :, 1].reshape(mp, width, width)]
    reshape x2 -> x1, local copies, waits for them, and re-layouts: 8.01 us -> 0.59 us  [body(): g_norm = g_gains[:width // 128].reshape(width)]
    unnamed x37 -> x46, local copies, waits for them, and re-layouts: 14.5 us -> 15.3 us
  transfers between devices with their start and end apart: 11 -> 8, of which waited for: 6 -> 3; matrix products, arithmetic and copies ran while one was open for 6% -> 3% of each run, Pallas kernels for 22% -> 57%
where the time goes in v2:
time: 357 us
  Pallas kernels  211 us (59%)
  waiting for transfers between devices  94.4 us (26%)
  local copies, waits for them, and re-layouts  22.8 us (6%)
  between operations  14.5 us (4%)
  starting transfers between devices  11.3 us (3%)
    pallas_call x1, Pallas kernels, feed_remote_call(): pl.pallas_call(feed_remote_kernel, in_specs=[vmem, vmem, pl.BlockSpec(mem...  106 us
    pallas_call x1, Pallas kernels, attention_call(): pl.pallas_call(functools.partial(attention_kernel, part), grid_spec=pltpu...  92 us
    ppermute x3, waiting for transfers between devices, body(): lax.ppermute(send, 'mp', [(i, (i + k) % mp) for i in range(mp)])  52.7 us
    all_gather x1, waiting for transfers between devices, body(): lax.all_gather(pack_attention(w_qkv, w_proj), both)  41.6 us
    unnamed x46, local copies, waits for them, and re-layouts  15.3 us
    pallas_call x1, Pallas kernels, finish_call(): pl.pallas_call(finish_kernel, grid_spec=pltpu.PrefetchScalarGridSpec(num_...  8.08 us
  transfers between devices with their start and end apart: 8, of which 3 were waited for; matrix products, arithmetic and copies ran while one was open for 3% of the time, Pallas kernels for 57%

profile of v2, /device:TPU:0, one launch (start us, length us, event | category | flops | bytes accessed | tf_op | source)
XLA Modules:
  0.0 356.6 jit_solution(382784053958701807)
XLA Ops:
  7.2 0.0 copy-start.12
  7.2 0.0 copy-start.1
  7.2 0.0 all-gather.7.cloned.1.call-start
  7.2 1.0 slice.33
  8.2 0.8 slice.34
  9.0 0.1 copy.53
  9.2 0.1 copy.54
  9.3 0.8 pad_maximum_fusion.2
  10.1 0.8 copy.45
  10.9 0.0 all-gather.7.cloned.1.call-update
  11.0 0.0 copy-start.2
  11.0 0.0 all-gather.5.cloned.1.call-start
  11.0 0.0 copy-done.12
  11.0 0.6 reshape.79.gain.norm_gain
  11.6 0.0 copy-done.1
  11.6 1.3 copy.40
  12.9 0.0 copy-done.2
  12.9 1.3 copy.41
  14.3 0.0 copy-start.17
  14.3 5.5 %norm_rows.1 = (bf16[4,240,768]{2,1,0:T(8,128)(2,1)}, bf16[4,240,768]{2,1,0:T(8,128)(2,1)}, bf16[2,240,768]{2,1,0:T(8,128)(2,1)}, bf16[2,240,768]{2,1,0:T(8,128)(2,1)}, bf16[2,240,768]{2,1,0:T(8,128)(2,1)}) custom-call(s32[1]{0:T(128)} %bitcast.place, bf16[4,236,768]{2,1,0:T(8,128)(2,1)} %bitcast.39, bf16[4,236,768]{2,1,0:T(8,128)(2,1)} %bitcast.41, ...), custom_call_target="tpu_custom_call" | custom-call | tf_op jit(solution)/shard_map/norm_rows/pallas_call | solution.py:53
  19.9 3.1 collective-permute-start
  22.9 2.6 collective-permute-start.1
  25.5 1.3 collective-permute-start.2
  26.9 0.0 copy-done.8
  26.9 0.0 copy-done.9
  26.9 0.7 pad_maximum_fusion
  27.6 18.0 %collective-permute-done.in1 = bf16[2,240,768]{2,1,0:T(8,128)(2,1)S(1)} collective-permute-done((bf16[2,240,768]{2,1,0:T(8,128)(2,1)}, bf16[2,240,768]{2,1,0:T(8,128)(2,1)S(1)}, u32[]{:S(2)}, u32[]{:S(2)}) %collective-permute-start) | collective-permute-done | bytes 737312 | tf_op jit(solution)/shard_map/ppermute | solution.py:717
  45.6 34.7 %collective-permute-done.1.in2 = bf16[2,240,768]{2,1,0:T(8,128)(2,1)S(1)} collective-permute-done((bf16[2,240,768]{2,1,0:T(8,128)(2,1)}, bf16[2,240,768]{2,1,0:T(8,128)(2,1)S(1)}, u32[]{:S(2)}, u32[]{:S(2)}) %collective-permute-start.1) | collective-permute-done | bytes 737312 | tf_op jit(solution)/shard_map/ppermute | solution.py:717
  80.3 0.0 collective-permute-done.2.in3
  80.3 0.0 all-gather.5.cloned.1.call-update
  80.4 0.0 copy-done.10
  80.4 0.1 reshape.83
  80.5 0.8 pad.4.ids
  81.3 0.0 copy-done.16
  81.3 0.0 copy-done.17
  81.3 0.6 maximum_bitcast_fusion.gains
  81.9 41.6 %all-gather.7.cloned.1.call-done = bf16[3072,768]{1,0:T(8,128)(2,1)} async-done(((bf16[96,768]{1,0:T(8,128)(2,1)}), bf16[3072,768]{1,0:T(8,128)(2,1)}) %all-gather.7.cloned.1.call-update) | async-done | bytes 4718608 | tf_op jit(solution)/shard_map/all_gather | solution.py:710
  123.5 0.0 copy-done.13
  123.5 0.0 copy-done.14
  123.5 0.0 copy-done.15
  123.5 92.0 %attention.1 = (bf16[2,240,768]{2,1,0:T(8,128)(2,1)}, bf16[2,240,768]{2,1,0:T(8,128)(2,1)}, bf16[2,240,768]{2,1,0:T(8,128)(2,1)}, bf16[2,240,768]{2,1,0:T(8,128)...) custom-call(s32[1]{0:T(128)} %bitcast.place, bf16[4,240,768]{2,1,0:T(8,128)(2,1)} %get-tuple-element.32.own_x, ...), custom_call_target="tpu_custom_call" | custom-call | flops 60000002048 | bytes 9437184 | tf_op jit(solution)/shard_map/attention/pallas_call | solution.py:599
  215.5 2.2 collective-permute-start.3
  217.6 1.2 collective-permute-start.4
  218.8 0.8 collective-permute-start.5
  219.6 105.8 %feed_forward_scatter.1 = (f32[960,768]{1,0:T(8,128)}, f32[960,768]{1,0:T(8,128)}, f32[96,768]{1,0:T(8,128)}, f32[96,768]{1,0:T(8,128)}, f32[96,768]{1,0:T(8,128)}, /*index=5*/f32[8,128]{1,0:T(8,128)}) custom-call(bf16[960,768]{1,0:T(8,128)(2,1)} %bitcast.58, bf16[960,768]{1,0:T(8,128)(2,1)} %bitcast.59, bf16[4,8,2,96,768]{4,3,2,1,0:T(8,128)(2,1)} %bitcast.56, ...), custom_call_target="tpu_custom_call" | custom-call | flops 27179089920 | bytes 18874368 | tf_op jit(solution)/shard_map/feed_forward_scatter/pallas_call | solution.py:381
  325.5 0.9 slice.35
  326.4 0.1 copy.46
  326.6 1.1 slice_bitcast_fusion
  327.6 0.1 copy.48
  327.8 0.9 copy.51
  328.6 0.6 slice_bitcast_fusion.3
  329.2 0.6 slice_bitcast_fusion.2
  329.8 0.0 collective-permute-done.3.ret1
  329.8 0.0 collective-permute-done.4.ret2
  329.8 0.0 collective-permute-done.5.ret3
  329.8 0.8 copy-done.3
  330.7 0.2 copy-done.4
  330.9 0.3 copy-done.5
  331.2 8.1 %finish.1 = (bf16[4,236,768]{2,1,0:T(8,128)(2,1)}, f32[4,236,768]{2,1,0:T(8,128)}) custom-call(s32[1]{0:T(128)} %bitcast.place, bf16[4,236,768]{2,1,0:T(8,128)(2,1)} %bitcast.40, bf16[4,236,768]{2,1,0:T(8,128)(2,1)} %bitcast.42, f32[1,768]{1,0:T(1,128)} %reshape.79.gain.norm_gain, f32[4,240,768]{2,1,0:T(8,128)} %bitcast.43, f32[4,240,768]{2,1,0:T(8,128)} %bitcast.44, ...), custom_call_target="tpu_custom_call" | custom-call | tf_op jit(solution)/shard_map/finish/pallas_call | solution.py:668
  339.3 5.8 %copy.50 = f32[2,2,236,768]{3,1,2,0:T(2,128)} copy(f32[2,2,236,768]{3,2,1,0:T(8,128)} %bitcast.45) | data formatting | bytes 5799936
  345.1 2.2 copy.49
  347.3 0.7 copy.52
  348.0 0.7 copy.57
  348.7 0.7 copy.58
  (22 shorter events, 0.1 us)
Async XLA Ops:
  7.2 3.9 %copy-start.12 = (f32[768]{0:T(1024)S(1)}, f32[768]{0:T(1024)}, u32[]{:S(2)}) copy-start(f32[768]{0:T(1024)} %param.15) | copy-start | bytes 9220
  7.2 4.5 %copy-start.1 = (bf16[2,2,236,768]{3,1,2,0:T(2,128)(2,1)S(1)}, bf16[2,2,236,768]{3,1,2,0:T(2,128)(2,1)}, u32[]{:S(2)}) copy-start(bf16[2,2,236,768]{3,1,2,0:T(2,128)(2,1)} %param.10) | copy-start | bytes 4349956
  7.2 116.3 %all-gather.7.cloned.1.call-start = ((), (), s32[]{:S(2)}) async-start(), calls=%async_computation.1 | async-start | bytes 4866048 | tf_op jit(solution)/shard_map/all_gather | solution.py:710
  11.0 2.0 copy-start.2
  11.0 208.7 %all-gather.5.cloned.1.call-start = ((), (), s32[]{:S(2)}) async-start(), calls=%async_computation | async-start | bytes 9732096 | tf_op jit(solution)/shard_map/all_gather | solution.py:724
  14.3 12.6 %copy-start.8 = (bf16[768,96]{0,1:T(8,128)(2,1)S(1)}, bf16[768,96]{0,1:T(8,128)(2,1)}, u32[]{:S(2)}) copy-start(bf16[768,96]{0,1:T(8,128)(2,1)} %param.14) | copy-start | bytes 442372
  14.3 12.6 %copy-start.9 = (bf16[96,768]{1,0:T(8,128)(2,1)S(1)}, bf16[96,768]{1,0:T(8,128)(2,1)}, u32[]{:S(2)}) copy-start(bf16[96,768]{1,0:T(8,128)(2,1)} %param.12) | copy-start | bytes 442372
  14.3 66.1 %copy-start.10 = (s32[2,2,944]{2,1,0:T(2,128)S(1)}, s32[2,2,944]{2,1,0:T(2,128)}, u32[]{:S(2)}) copy-start(s32[2,2,944]{2,1,0:T(2,128)} %param.18) | copy-start | bytes 45316
  14.3 67.0 %copy-start.16 = (f32[64]{0:T(128)S(1)}, f32[64]{0:T(128)}, u32[]{:S(2)}) copy-start(f32[64]{0:T(128)} %param.17) | copy-start | bytes 772
  14.3 67.0 %copy-start.17 = (f32[64]{0:T(128)S(1)}, f32[64]{0:T(128)}, u32[]{:S(2)}) copy-start(f32[64]{0:T(128)} %param.16) | copy-start | bytes 772
  19.9 25.8 %collective-permute-start = (bf16[2,240,768]{2,1,0:T(8,128)(2,1)}, bf16[2,240,768]{2,1,0:T(8,128)(2,1)S(1)}, u32[]{:S(2)}, u32[]{:S(2)}) collective-permute-start(bf16[2,240,768]{2,1,0:T(8,128)(2,1)} %get-tuple-element.34), channel_id=1, source_target_pairs={{0,1},{1,2},{2,3},{3,0},{4,5},{5,6},{6,7},{7,4},{8,9},{9,10},{10,1... | collective-permute-start | bytes 2211848 | tf_op jit(solution)/shard_map/ppermute | solution.py:717
  22.9 57.4 %collective-permute-start.1 = (bf16[2,240,768]{2,1,0:T(8,128)(2,1)}, bf16[2,240,768]{2,1,0:T(8,128)(2,1)S(1)}, u32[]{:S(2)}, u32[]{:S(2)}) collective-permute-start(bf16[2,240,768]{2,1,0:T(8,128)(2,1)} %get-tuple-element.35), channel_id=1, source_target_pairs={{0,2},{1,3},{2,0},{3,1},{4,6},{5,7},{6,4},{7,5},{8,10},{9,11},{10,... | collective-permute-start | bytes 2211848 | tf_op jit(solution)/shard_map/ppermute | solution.py:717
  25.5 54.8 %collective-permute-start.2 = (bf16[2,240,768]{2,1,0:T(8,128)(2,1)}, bf16[2,240,768]{2,1,0:T(8,128)(2,1)S(1)}, u32[]{:S(2)}, u32[]{:S(2)}) collective-permute-start(bf16[2,240,768]{2,1,0:T(8,128)(2,1)} %get-tuple-element.36), channel_id=1, source_target_pairs={{0,3},{1,0},{2,1},{3,2},{4,7},{5,4},{6,5},{7,6},{8,11},{9,8},{10,9... | collective-permute-start | bytes 2211848 | tf_op jit(solution)/shard_map/ppermute | solution.py:717
  45.6 77.8 %copy-start.13 = (bf16[2,240,768]{2,1,0:T(8,128)(2,1)}, bf16[2,240,768]{2,1,0:T(8,128)(2,1)S(1)}, u32[]{:S(2)}) copy-start(bf16[2,240,768]{2,1,0:T(8,128)(2,1)S(1)} %collective-permute-done.in1) | copy-start | bytes 2211844
  80.3 43.1 %copy-start.14 = (bf16[2,240,768]{2,1,0:T(8,128)(2,1)}, bf16[2,240,768]{2,1,0:T(8,128)(2,1)S(1)}, u32[]{:S(2)}) copy-start(bf16[2,240,768]{2,1,0:T(8,128)(2,1)S(1)} %collective-permute-done.1.in2) | copy-start | bytes 2211844
  80.3 43.1 %copy-start.15 = (bf16[2,240,768]{2,1,0:T(8,128)(2,1)}, bf16[2,240,768]{2,1,0:T(8,128)(2,1)S(1)}, u32[]{:S(2)}) copy-start(bf16[2,240,768]{2,1,0:T(8,128)(2,1)S(1)} %collective-permute-done.2.in3) | copy-start | bytes 2211844
  215.5 114.4 %collective-permute-start.3 = (bf16[2,240,768]{2,1,0:T(8,128)(2,1)}, bf16[2,240,768]{2,1,0:T(8,128)(2,1)S(1)}, u32[]{:S(2)}, u32[]{:S(2)}) collective-permute-start(bf16[2,240,768]{2,1,0:T(8,128)(2,1)} %get-tuple-element.46), channel_id=1, source_target_pairs={{0,3},{1,0},{2,1},{3,2},{4,7},{5,4},{6,5},{7,6},{8,11},{9,8},{10,9... | collective-permute-start | bytes 2211848 | tf_op jit(solution)/shard_map/ppermute | solution.py:729
  217.6 112.2 %collective-permute-start.4 = (bf16[2,240,768]{2,1,0:T(8,128)(2,1)}, bf16[2,240,768]{2,1,0:T(8,128)(2,1)S(1)}, u32[]{:S(2)}, u32[]{:S(2)}) collective-permute-start(bf16[2,240,768]{2,1,0:T(8,128)(2,1)} %get-tuple-element.47), channel_id=1, source_target_pairs={{0,2},{1,3},{2,0},{3,1},{4,6},{5,7},{6,4},{7,5},{8,10},{9,11},{10,... | collective-permute-start | bytes 2211848 | tf_op jit(solution)/shard_map/ppermute | solution.py:729
  218.8 111.0 %collective-permute-start.5 = (bf16[2,240,768]{2,1,0:T(8,128)(2,1)}, bf16[2,240,768]{2,1,0:T(8,128)(2,1)S(1)}, u32[]{:S(2)}, u32[]{:S(2)}) collective-permute-start(bf16[2,240,768]{2,1,0:T(8,128)(2,1)} %get-tuple-element.48), channel_id=1, source_target_pairs={{0,1},{1,2},{2,3},{3,0},{4,5},{5,6},{6,7},{7,4},{8,9},{9,10},{10,1... | collective-permute-start | bytes 2211848 | tf_op jit(solution)/shard_map/ppermute | solution.py:729
  325.5 3.2 copy-start.11
  329.8 0.9 copy-start.3
  329.8 1.1 copy-start.4
  329.8 1.4 copy-start.5
  339.3 5.8 %copy-start = (bf16[4,236,768]{2,1,0:T(8,128)(2,1)S(1)}, bf16[4,236,768]{2,1,0:T(8,128)(2,1)}, u32[]{:S(2)}) copy-start(bf16[4,236,768]{2,1,0:T(8,128)(2,1)} %get-tuple-element.49) | copy-start | bytes 4349956
  345.0 3.0 copy-start.7
  345.0 3.7 %copy-start.6 = (f32[96,768]{1,0:T(8,128)S(1)}, f32[96,768]{1,0:T(8,128)}, u32[]{:S(2)}) copy-start(f32[96,768]{1,0:T(8,128)} %get-tuple-element.53) | copy-start | bytes 884740
Sparse Core Ops, SparseCore 0:
  11.5 111.9 all-gather.6
  126.9 80.8 all-gather.4

commit v3 on v2

--- a/solution.py
+++ b/solution.py
@@ -123,6 +123,171 @@
     )(normed, grads, w_up, w_down)
 
 
+class Place:
+    def __init__(self, planes):
+        d = lax.axis_index("dp")
+        self.z = lax.axis_index("mp")
+        self.d, self.planes = d, planes
+        self.core, self.x, self.y = d % 2, (d // 2) % 2, d // 4
+        self.sibling = d + 1 - 2 * self.core
+        self.beside = d + 2 - 4 * self.x
+        self.above = d + 4 - 8 * self.y
+
+    def along(self, k):
+        return lax.rem(self.z + k + self.planes, self.planes)
+
+    def copy(self, src, dst, send, recv, dp=None, mp=None):
+        return pltpu.make_async_remote_copy(
+            src_ref=src, dst_ref=dst, send_sem=send, recv_sem=recv,
+            device_id={"dp": self.d if dp is None else dp, "mp": self.z if mp is None else mp},
+            device_id_type=pl.DeviceIdType.MESH,
+        )
+
+    def greet(self):
+        barrier = pltpu.get_barrier_semaphore()
+        for other in (self.sibling, self.beside, self.above):
+            pl.semaphore_signal(barrier, 1, device_id={"dp": other, "mp": self.z},
+                                device_id_type=pl.DeviceIdType.MESH)
+        for k in range(1, self.planes):
+            pl.semaphore_signal(barrier, 1, device_id={"dp": self.d, "mp": self.along(k)},
+                                device_id_type=pl.DeviceIdType.MESH)
+        pl.semaphore_wait(barrier, self.planes + 2)
+
+
+class Scatter:
+    def __init__(self, at, items, src, got_core, got_first, got_second, send_sem, recv_sem):
+        self.at, self.items, self.src = at, items, src
+        self.got_core, self.got_first, self.got_second = got_core, got_first, got_second
+        self.send_sem, self.recv_sem = send_sem, recv_sem
+
+    def copy(self, stage, step, item):
+        at = self.at
+        kind, cols, x_first = self.items[item]
+        if stage == 0:
+            src = self.src.at[step, kind, :, :, 1 - at.core, :, cols]
+            dst = self.got_core.at[step, kind, :, :, :, cols]
+            to = at.sibling
+        elif stage == 1:
+            if x_first:
+                src = self.got_core.at[step, kind, :, 1 - at.x, :, cols]
+            else:
+                src = self.got_core.at[step, kind, 1 - at.y, :, :, cols]
+            dst = self.got_first.at[step, kind, :, :, cols]
+            to = at.beside if x_first else at.above
+        else:
+            src = self.got_first.at[step, kind, 1 - at.y if x_first else 1 - at.x, :, cols]
+            dst = self.got_second.at[step, kind, :, cols]
+            to = at.above if x_first else at.beside
+        sem = (stage, item, step)
+        return at.copy(src, dst, self.send_sem.at[sem], self.recv_sem.at[sem], dp=to)
+
+    def start(self, step):
+        for item in range(len(self.items)):
+            self.copy(0, step, item).start()
+
+    def after_core(self, step):
+        for item, (kind, cols, _) in enumerate(self.items):
+            self.copy(0, step, item).wait_recv()
+            for row in ((0, 0), (0, 1), (1, 0), (1, 1)):
+                own = self.src[(step, kind, *row, self.at.core, slice(None), cols)]
+                to = (step, kind, *row, slice(None), cols)
+                total = own.astype(F32) + self.got_core[to].astype(F32)
+                self.got_core[to] = total.astype(BF16)
+            self.copy(1, step, item).start()
+
+    def after_first(self, step):
+        for item, (kind, cols, x_first) in enumerate(self.items):
+            self.copy(1, step, item).wait_recv()
+            for row in range(2):
+                if x_first:
+                    own = self.got_core[step, kind, row, self.at.x, :, cols]
+                else:
+                    own = self.got_core[step, kind, self.at.y, row, :, cols]
+                total = own.astype(F32) + self.got_first[step, kind, row, :, cols].astype(F32)
+                self.got_first[step, kind, row, :, cols] = total.astype(BF16)
+            self.copy(2, step, item).start()
+
+    def total(self, step, item):
+        kind, cols, x_first = self.items[item]
+        self.copy(2, step, item).wait_recv()
+        own = self.got_first[step, kind, self.at.y if x_first else self.at.x, :, cols]
+        return own.astype(F32) + self.got_second[step, kind, :, cols].astype(F32)
+
+    def after_second(self, step):
+        for item, (kind, cols, _) in enumerate(self.items):
+            self.got_second[step, kind, :, cols] = self.total(step, item).astype(BF16)
+
+    def wait_send(self, step):
+        for item in range(len(self.items)):
+            for stage in range(3):
+                self.copy(stage, step, item).wait_send()
+
+
+class Gather:
+    def __init__(self, at, shard, full, send_sem, recv_sem):
+        self.at, self.shard, self.full = at, shard, full
+        self.send_sem, self.recv_sem = send_sem, recv_sem
+
+    def piece(self, k, y=False, x=False, core=False):
+        at = self.at
+        return self.full.at[at.along(-k), 1 - at.y if y else at.y, 1 - at.x if x else at.x,
+                            1 - at.core if core else at.core]
+
+    def move(self, kind, k, src, **to):
+        sem = (kind, k)
+        self.at.copy(src, src, self.send_sem.at[sem], self.recv_sem.at[sem], **to).start()
+
+    def arrived(self, kind, k, ref):
+        sem = (kind, k)
+        self.at.copy(ref, ref, self.send_sem.at[sem], self.recv_sem.at[sem],
+                     dp=self.at.sibling).wait_recv()
+
+    def start(self):
+        for k in range(1, self.at.planes):
+            sem = (0, k)
+            self.at.copy(self.shard, self.piece(0), self.send_sem.at[sem], self.recv_sem.at[sem],
+                         mp=self.at.along(k)).start()
+
+    def spread(self, k):
+        at = self.at
+        src = self.piece(k)
+        if k:
+            self.arrived(0, k, src)
+        self.move(1, k, src, dp=at.beside)
+        self.move(2, k, src, dp=at.above)
+        self.move(3, k, src, dp=at.sibling)
+
+    def forward(self, k):
+        at = self.at
+        from_x, from_y = self.piece(k, x=True), self.piece(k, y=True)
+        self.arrived(1, k, from_x)
+        if k % 2 == 0:
+            self.move(5, k, from_x, dp=at.above)
+        self.move(4, k, from_x, dp=at.sibling)
+        self.arrived(2, k, from_y)
+        if k % 2 == 1:
+            self.move(5, k, from_y, dp=at.beside)
+        self.move(6, k, from_y, dp=at.sibling)
+
+    def across(self, k):
+        src = self.piece(k, y=True, x=True)
+        self.arrived(5, k, src)
+        self.move(7, k, src, dp=self.at.sibling)
+
+    def last(self, k):
+        self.arrived(3, k, self.piece(k, core=True))
+        self.arrived(4, k, self.piece(k, x=True, core=True))
+        self.arrived(6, k, self.piece(k, y=True, core=True))
+        self.arrived(7, k, self.piece(k, y=True, x=True, core=True))
+
+    def wait_send(self):
+        for k in range(self.at.planes):
+            for kind in range(0 if k else 1, 8):
+                sem = (kind, k)
+                self.at.copy(self.piece(k), self.piece(k), self.send_sem.at[sem],
+                             self.recv_sem.at[sem], dp=self.at.sibling).wait_send()
+
+
 def gelu_parts(up):
     inner = 0.7978845608028654 * (up + 0.044715 * up * up * up)
     th = jnp.tanh(inner)
@@ -133,123 +298,40 @@
     return up * half, slope
 
 
+def halves(width):
+    return (0, slice(0, width // 2), True), (0, slice(width // 2, width), False)
+
+
 def feed_remote_kernel(
-    x_ref, dy_ref, w_hbm, g_attn, gain, gains_in,
+    x_ref, dy_ref, w_hbm, g_attn, z_attn, gain, gains_in,
     branch, d_normed, out_attn, out_up, out_down, out_gains,
-    xt, dt, w_buf, g_ff, got_core, got_first, got_second, got_z, sums, got_sums, z_sums,
-    w_sem, send_sem, recv_sem, z_send, z_recv, sum_send, sum_recv,
+    xt, dt, w_buf, g_ff, ff_core, ff_first, ff_second, at_core, at_first, at_second, got_z,
+    sums, got_sums, z_sums,
+    w_sem, ff_send, ff_recv, at_send, at_recv, z_send, z_recv, sum_send, sum_recv,
 ):
     width = x_ref.shape[1]
     steps, shard = w_hbm.shape[0], w_hbm.shape[3]
-    d = lax.axis_index("dp")
-    z = lax.axis_index("mp")
-    core, x, y = d % 2, (d // 2) % 2, d // 4
-    sibling, beside, above = d + 1 - 2 * core, d + 2 - 4 * x, d + 4 - 8 * y
     half = width // 2
-    items = ((0, slice(0, half), True), (0, slice(half, width), False),
-             (1, slice(0, width), True), (2, slice(0, width), False))
-
-    def part_of(step):
-        return lax.rem(z + 1 + step, steps)
-
-    barrier = pltpu.get_barrier_semaphore()
-    for other in (sibling, beside, above):
-        pl.semaphore_signal(barrier, 1, device_id={"dp": other, "mp": z},
-                            device_id_type=pl.DeviceIdType.MESH)
-    for k in range(1, steps):
-        pl.semaphore_signal(barrier, 1, device_id={"dp": d, "mp": lax.rem(z + k, steps)},
-                            device_id_type=pl.DeviceIdType.MESH)
-    pl.semaphore_wait(barrier, steps + 2)
-
-    def remote(src, dst, send, recv, dp_to, z_to):
-        return pltpu.make_async_remote_copy(
-            src_ref=src, dst_ref=dst, send_sem=send, recv_sem=recv,
-            device_id={"dp": dp_to, "mp": z_to}, device_id_type=pl.DeviceIdType.MESH,
-        )
-
-    def core_copy(step, item):
-        kind, cols, _ = items[item]
-        if kind == 0:
-            src = g_attn.at[part_of(step), :, :, 1 - core, :, cols]
-        else:
-            src = g_ff.at[step, kind - 1, :, :, 1 - core, :, cols]
-        dst = got_core.at[step, kind, :, :, :, cols]
-        sem = (0, item, step)
-        return remote(src, dst, send_sem.at[sem], recv_sem.at[sem], sibling, z)
-
-    def first_copy(step, item):
-        kind, cols, x_first = items[item]
-        dst = got_first.at[step, kind, :, :, cols]
-        sem = (1, item, step)
-        if x_first:
-            src = got_core.at[step, kind, :, 1 - x, :, cols]
-        else:
-            src = got_core.at[step, kind, 1 - y, :, :, cols]
-        return remote(src, dst, send_sem.at[sem], recv_sem.at[sem], beside if x_first else above, z)
-
-    def second_copy(step, item):
-        kind, cols, x_first = items[item]
-        src = got_first.at[step, kind, 1 - y if x_first else 1 - x, :, cols]
-        dst = got_second.at[step, kind, :, cols]
-        sem = (2, item, step)
-        return remote(src, dst, send_sem.at[sem], recv_sem.at[sem], above if x_first else beside, z)
+    at = Place(steps)
+    at.greet()
+    attn = Scatter(at, halves(width), g_attn, at_core, at_first, at_second, at_send, at_recv)
+    both = (0, slice(0, width), True), (1, slice(0, width), False)
+    feed = Scatter(at, both, g_ff, ff_core, ff_first, ff_second, ff_send, ff_recv)
+    last = steps - 1
 
     def z_copy(step, kind):
-        return remote(got_second.at[step, kind], got_z.at[kind, step],
-                      z_send.at[kind, step], z_recv.at[kind, step], d, part_of(step))
-
-    def after_core(step, chosen):
-        for item in chosen:
-            kind, cols, _ = items[item]
-            core_copy(step, item).wait_recv()
-            for row in ((0, 0), (0, 1), (1, 0), (1, 1)):
-                if kind == 0:
-                    own = g_attn[(part_of(step), *row, core, slice(None), cols)]
-                else:
-                    own = g_ff[(step, kind - 1, *row, core, slice(None), cols)]
-                place = (step, kind, *row, slice(None), cols)
-                got_core[place] = (own.astype(F32) + got_core[place].astype(F32)).astype(BF16)
-            first_copy(step, item).start()
-
-    def after_first(step, chosen):
-        for item in chosen:
-            kind, cols, x_first = items[item]
-            first_copy(step, item).wait_recv()
-            for row in range(2):
-                if x_first:
-                    own = got_core[step, kind, row, x, :, cols]
-                else:
-                    own = got_core[step, kind, y, row, :, cols]
-                total = own.astype(F32) + got_first[step, kind, row, :, cols].astype(F32)
-                got_first[step, kind, row, :, cols] = total.astype(BF16)
-            second_copy(step, item).start()
-
-    def second_sum(step, item):
-        kind, cols, x_first = items[item]
-        second_copy(step, item).wait_recv()
-        own = got_first[step, kind, y if x_first else x, :, cols]
-        return own.astype(F32) + got_second[step, kind, :, cols].astype(F32)
-
-    def after_second(step, chosen):
-        for item in chosen:
-            kind, cols, _ = items[item]
-            got_second[step, kind, :, cols] = second_sum(step, item).astype(BF16)
-        for kind in sorted({items[item][0] for item in chosen}):
+        return at.copy(ff_second.at[step, kind], got_z.at[kind, step],
+                       z_send.at[kind, step], z_recv.at[kind, step], mp=at.along(1 + step))
+
+    def to_z(step):
+        feed.after_second(step)
+        for kind in range(2):
             z_copy(step, kind).start()
-
-    def finish_sum(chosen, out):
-        step = steps - 1
-        for item in chosen:
-            kind, cols, _ = items[item]
-            total = second_sum(step, item)
-            for slot in range(steps - 1):
-                total = total + got_z[kind, slot, :, cols].astype(F32)
-            out[:, cols] = total
 
     def w_copy(step, kind):
         slot = lax.rem(step, 2)
         return pltpu.make_async_copy(
-            w_hbm.at[part_of(step), :, kind], w_buf.at[slot, kind], w_sem.at[slot, kind]
+            w_hbm.at[at.along(1 + step), :, kind], w_buf.at[slot, kind], w_sem.at[slot, kind]
         )
 
     def feed_half(step, index):
@@ -266,10 +348,7 @@
         branch[...] += nt(hidden, lower)
         d_normed[...] += nt(d_up, upper)
 
-    attn, feed = (0, 1), (2, 3)
-    for step in range(steps):
-        for item in attn:
-            core_copy(step, item).start()
+    attn.start(0)
     for kind in range(2):
         w_copy(0, kind).start()
     xt[...] = x_ref[...].T
@@ -288,71 +367,70 @@
 
         feed_half(step, 0)
 
+        @pl.when(step == 0)
+        def _():
+            attn.after_core(0)
+
         @pl.when(step >= 1)
         def _():
-            after_core(step - 1, feed)
-
-        after_core(step, attn)
+            feed.after_core(step - 1)
 
         @pl.when(step >= 2)
         def _():
-            after_second(step - 2, feed)
+            to_z(step - 2)
 
         feed_half(step, 1)
-        for item in feed:
-            core_copy(step, item).start()
+        feed.start(step)
+
+        @pl.when(step == 0)
+        def _():
+            attn.after_first(0)
 
         @pl.when(step >= 1)
         def _():
-            after_first(step - 1, feed)
-
-        after_first(step, attn)
-
-        @pl.when(step >= 1)
-        def _():
-            after_second(step - 1, attn)
+            feed.after_first(step - 1)
 
         return carry
 
     lax.fori_loop(0, steps, one_step, 0)
-    last = steps - 1
 
     sums[0] = gains_in[...]
     store_gain(sums.at[0], d_normed[...], x_ref[...], gain[...])
 
     def sum_copy(stage):
-        to = (sibling, beside, above)[stage]
-        return remote(sums.at[stage], got_sums.at[stage], sum_send.at[stage], sum_recv.at[stage],
-                      to, z)
+        to = (at.sibling, at.beside, at.above)[stage]
+        return at.copy(sums.at[stage], got_sums.at[stage], sum_send.at[stage],
+                       sum_recv.at[stage], dp=to)
 
     def sum_z_copy(k):
-        return remote(sums.at[3], z_sums.at[z], sum_send.at[2 + k], sum_recv.at[2 + k],
-                      d, lax.rem(z + k, steps))
+        return at.copy(sums.at[3], z_sums.at[at.z], sum_send.at[2 + k], sum_recv.at[2 + k],
+                       mp=at.along(k))
 
     def next_sum(stage):
         sum_copy(stage).wait_recv()
         sums[stage + 1] = sums[stage] + got_sums[stage]
 
     sum_copy(0).start()
-    after_core(last, feed)
+    feed.after_core(last)
     next_sum(0)
     sum_copy(1).start()
-    after_second(last - 1, feed)
+    to_z(last - 1)
     next_sum(1)
     sum_copy(2).start()
-    after_first(last, feed)
+    for item in range(2):
+        cols = attn.items[item][1]
+        out_attn[:, cols] = attn.total(0, item) + z_attn[:, cols]
+    feed.after_first(last)
     next_sum(2)
     for k in range(1, steps):
         sum_z_copy(k).start()
-    z_sums[z] = sums[3]
-    for step in range(last):
-        z_copy(step, 0).wait_recv()
-    finish_sum(attn, out_attn)
-    for step in range(last):
-        z_copy(step, 1).wait_recv()
-        z_copy(step, 2).wait_recv()
-    finish_sum(feed[:1], out_up)
-    finish_sum(feed[1:], out_down)
+    z_sums[at.z] = sums[3]
+    for kind, out in enumerate((out_up, out_down)):
+        total = feed.total(last, kind)
+        for step in range(last):
+            z_copy(step, kind).wait_recv()
+            total = total + got_z[kind, step].astype(F32)
+        out[...] = total
     for k in range(1, steps):
         sum_z_copy(k).wait_recv()
     total = z_sums[0]
@@ -360,13 +438,11 @@
         total = total + z_sums[k]
     out_gains[...] = total
 
+    attn.wait_send(0)
     for step in range(steps):
-        for item in range(4):
-            core_copy(step, item).wait_send()
-            first_copy(step, item).wait_send()
-            second_copy(step, item).wait_send()
+        feed.wait_send(step)
     for step in range(last):
-        for kind in range(3):
+        for kind in range(2):
             z_copy(step, kind).wait_send()
     for stage in range(3):
         sum_copy(stage).wait_send()
@@ -374,13 +450,13 @@
         sum_z_copy(k).wait_send()
 
 
-def feed_remote_call(normed, grads, w_ff, g_attn, gain, gains):
+def feed_remote_call(normed, grads, w_ff, g_attn, z_attn, gain, gains):
     rows, width = normed.shape
     steps, _, _, shard, _ = w_ff.shape
     vmem = pl.BlockSpec(memory_space=pltpu.VMEM)
     return pl.pallas_call(
         feed_remote_kernel,
-        in_specs=[vmem, vmem, pl.BlockSpec(memory_space=pl.ANY), vmem, vmem, vmem],
+        in_specs=[vmem, vmem, pl.BlockSpec(memory_space=pl.ANY)] + [vmem] * 4,
         out_specs=[vmem] * 6,
         out_shape=[jax.ShapeDtypeStruct((rows, width), F32)] * 2
         + [jax.ShapeDtypeStruct((shard, width), F32)] * 3
@@ -390,18 +466,23 @@
             pltpu.VMEM((width, rows), BF16),
             pltpu.VMEM((2, 2, 8, shard, width), BF16),
             pltpu.VMEM((steps, 2, 2, 2, 2, shard, width), BF16),
-            pltpu.VMEM((steps, 3, 2, 2, shard, width), BF16),
-            pltpu.VMEM((steps, 3, 2, shard, width), BF16),
-            pltpu.VMEM((steps, 3, shard, width), BF16),
-            pltpu.VMEM((3, steps - 1, shard, width), BF16),
+            pltpu.VMEM((steps, 2, 2, 2, shard, width), BF16),
+            pltpu.VMEM((steps, 2, 2, shard, width), BF16),
+            pltpu.VMEM((steps, 2, shard, width), BF16),
+            pltpu.VMEM((1, 1, 2, 2, shard, width), BF16),
+            pltpu.VMEM((1, 1, 2, shard, width), BF16),
+            pltpu.VMEM((1, 1, shard, width), BF16),
+            pltpu.VMEM((2, steps - 1, shard, width), BF16),
             pltpu.VMEM((4, 8, 128), F32),
             pltpu.VMEM((3, 8, 128), F32),
             pltpu.VMEM((steps, 8, 128), F32),
             pltpu.SemaphoreType.DMA((2, 2)),
-            pltpu.SemaphoreType.DMA((3, 4, steps)),
-            pltpu.SemaphoreType.DMA((3, 4, steps)),
-            pltpu.SemaphoreType.DMA((3, steps - 1)),
-            pltpu.SemaphoreType.DMA((3, steps - 1)),
+            pltpu.SemaphoreType.DMA((3, 2, steps)),
+            pltpu.SemaphoreType.DMA((3, 2, steps)),
+            pltpu.SemaphoreType.DMA((3, 2, 1)),
+            pltpu.SemaphoreType.DMA((3, 2, 1)),
+            pltpu.SemaphoreType.DMA((2, steps - 1)),
+            pltpu.SemaphoreType.DMA((2, steps - 1)),
             pltpu.SemaphoreType.DMA((6,)),
             pltpu.SemaphoreType.DMA((6,)),
         ],
@@ -414,7 +495,7 @@
             transcendentals=rows * width * steps,
         ),
         name="feed_forward_scatter",
-    )(normed, grads, w_ff, g_attn, gain, gains)
+    )(normed, grads, w_ff, g_attn, z_attn, gain, gains)
 
 
 def iota(shape, axis):
@@ -434,66 +515,59 @@
         out[row:row + 1] += total[:, 128 * row:128 * row + 128]
 
 
-def attention_kernel(
-    part, place, own_x, own_dy, in1, in2, in3, ids, gains, norm_gain, weights,
-    out0, out1, out2, out3, g_weights, g_gains,
-    x_ref, dy_ref, xt, dt, feat_q, feat_k, pt, raw, d_raw, d_att, att, d_normed, branch,
+def prepare(
+    me, part, ids, pieces, x_ref, dy_ref, xt, dt, feat_q, feat_k, pt, d_normed, branch, g_gains
 ):
-    step = pl.program_id(0)
     mp = ids.shape[1]
     total = mp * part
-    me = place[0]
+    numbers = ids[me]
+    start = jnp.zeros((1, 1), jnp.int32)
+    for image in range(IMAGES):
+        count = jnp.sum((numbers == image).astype(F32), axis=(0, 1), keepdims=True)
+        ahead = jnp.sum(
+            ((numbers >= 0) & (numbers < image)).astype(F32), axis=(0, 1), keepdims=True
+        )
+        start = start + jnp.where(count == MOST, ahead, 0.0).astype(jnp.int32)
+    column = source_of(iota((ROWS, 1), 0), start, total)
+    line = source_of(iota((1, ROWS), 1), start, total)
+    x_sum, dy_sum, feats = 0.0, 0.0, 0.0
+    for k, piece in enumerate(pieces):
+        chunk = lax.rem(me - k + mp, mp)
+        offset = iota((1, PIECE), 1)
+        pos = jnp.where(offset < part, chunk * part + offset, -2)
+        pick = (column == pos).astype(F32).astype(BF16)
+        offset = iota((PIECE, 1), 0)
+        pos = jnp.where(offset < part, chunk * part + offset, -2)
+        pt[k] = (line == pos).astype(F32).astype(BF16)
+        x_sum = x_sum + nn(pick, piece[0][...])
+        dy_sum = dy_sum + nn(pick, piece[1][...])
+        marks = (iota((128, 1), 0) - HD == ids[me, pl.ds(chunk, 1), :]).astype(F32)
+        feats = feats + nt(pick, marks.astype(BF16))
+    x = x_sum.astype(BF16)
+    dy = dy_sum.astype(BF16)
+    x_ref[...] = x
+    dy_ref[...] = dy
+    xt[...] = x.T
+    dt[...] = dy.T
     lane = iota((1, 128), 1)
-
-    @pl.when(step == 0)
-    def _():
-        numbers = ids[0]
-        start = jnp.zeros((1, 1), jnp.int32)
-        for image in range(IMAGES):
-            count = jnp.sum(
-                (numbers == image).astype(F32), axis=(0, 1), keepdims=True
-            )
-            ahead = jnp.sum(
-                ((numbers >= 0) & (numbers < image)).astype(F32), axis=(0, 1), keepdims=True
-            )
-            start = start + jnp.where(count == MOST, ahead, 0.0).astype(jnp.int32)
-        column = source_of(iota((ROWS, 1), 0), start, total)
-        line = source_of(iota((1, ROWS), 1), start, total)
-        x_sum, dy_sum, feats = 0.0, 0.0, 0.0
-        pieces = ((own_x, own_dy), (in1,), (in2,), (in3,))
-        for k, piece in enumerate(pieces):
-            chunk = lax.rem(me - k + mp, mp)
-            offset = iota((1, PIECE), 1)
-            pos = jnp.where(offset < part, chunk * part + offset, -2)
-            pick = (column == pos).astype(F32).astype(BF16)
-            offset = iota((PIECE, 1), 0)
-            pos = jnp.where(offset < part, chunk * part + offset, -2)
-            pt[k] = (line == pos).astype(F32).astype(BF16)
-            x_piece = piece[0][0]
-            dy_piece = piece[1][0] if k == 0 else piece[0][1]
-            x_sum = x_sum + nn(pick, x_piece)
-            dy_sum = dy_sum + nn(pick, dy_piece)
-            marks = (iota((128, 1), 0) - HD == ids[0, pl.ds(chunk, 1), :]).astype(F32)
-            feats = feats + nt(pick, marks.astype(BF16))
-        x = x_sum.astype(BF16)
-        dy = dy_sum.astype(BF16)
-        x_ref[...] = x
-        dy_ref[...] = dy
-        xt[...] = x.T
-        dt[...] = dy.T
-        feat_q[...] = (feats * 128.0).astype(BF16)
-        marked = (lane >= HD) & (lane < HD + IMAGES)
-        feat_k[...] = jnp.where(marked, (feats - 1.0) * 256.0, 0.0).astype(BF16)
-        d_normed[...] = jnp.zeros_like(d_normed)
-        branch[...] = jnp.zeros_like(branch)
-        g_gains[...] = jnp.zeros_like(g_gains)
-
-    raw[...] = nn(x_ref[...], weights[0, :, :640])
-    d_att[...] = nn(dy_ref[...], weights[0, :, 512:])
+    feat_q[...] = (feats * 128.0).astype(BF16)
+    marked = (lane >= HD) & (lane < HD + IMAGES)
+    feat_k[...] = jnp.where(marked, (feats - 1.0) * 256.0, 0.0).astype(BF16)
+    d_normed[...] = jnp.zeros_like(d_normed)
+    branch[...] = jnp.zeros_like(branch)
+    g_gains[...] = jnp.zeros_like(g_gains)
+
+
+def attention_chunk(
+    weights, gain, x_ref, dy_ref, xt, dt, feat_q, feat_k, raw, d_raw, d_att, att,
+    d_normed, branch, g_gains, store, poll,
+):
+    raw[...] = nn(x_ref[...], weights(slice(0, 640)))
+    d_att[...] = nn(dy_ref[...], weights(slice(512, 768)))
+    lane = iota((1, 128), 1)
     low = lane < HD
     same = (iota((128, 128), 0) // HD == iota((128, 128), 1) // HD).astype(F32)
     mean_of = (same * (1.0 / HD)).astype(BF16)
-    gain = gains[...]
 
     def half_mean(value):
         return nn(value.astype(BF16), mean_of)
@@ -567,25 +641,52 @@
             d_raw[:, 512:640] = jnp.where(low, d_value, 0.0).astype(BF16)
             both = jnp.where(low, first_att, pltpu.roll(attend, HD, 1))
             att[:, 128:256] = both.astype(BF16)
+        poll(head)
     g_gains[6:7] += d_gain
     d_projected = d_raw[...]
     attended = att[...]
-    d_normed[...] += nt(d_projected, weights[0, :, :640])
-    branch[...] += nt(attended, weights[0, :, 512:])
+    d_normed[...] += nt(d_projected, weights(slice(0, 640)))
+    branch[...] += nt(attended, weights(slice(512, 768)))
     left = nn(xt[...], d_projected)
     right = nn(dt[...], attended)
-    g_weights[0, :, :512] = left[:, :512].astype(BF16)
-    g_weights[0, :, 512:640] = (left[:, 512:] + right[:, :128]).astype(BF16)
-    g_weights[0, :, 640:] = right[:, 128:].astype(BF16)
+    store(slice(0, 512), left[:, :512].astype(BF16))
+    store(slice(512, 640), (left[:, 512:] + right[:, :128]).astype(BF16))
+    store(slice(640, 768), right[:, 128:].astype(BF16))
+
+
+def take_back(outs, pt, x_ref, norm_gain, d_normed, branch, g_gains):
+    store_gain(g_gains, d_normed[...], x_ref[...], norm_gain[...])
+    d_rows = d_normed[...].astype(BF16)
+    b_rows = branch[...].astype(BF16)
+    for k, out in enumerate(outs):
+        out[0] = nn(pt[k], d_rows).astype(BF16)
+        out[1] = nn(pt[k], b_rows).astype(BF16)
+
+
+def attention_kernel(
+    part, place, own_x, own_dy, in1, in2, in3, ids, gains, norm_gain, weights,
+    out0, out1, out2, out3, g_weights, g_gains,
+    x_ref, dy_ref, xt, dt, feat_q, feat_k, pt, raw, d_raw, d_att, att, d_normed, branch,
+):
+    step = pl.program_id(0)
+
+    @pl.when(step == 0)
+    def _():
+        pieces = [(own_x.at[0], own_dy.at[0])] + [(got.at[0], got.at[1]) for got in (in1, in2, in3)]
+        prepare(place[0], part, ids, pieces, x_ref, dy_ref, xt, dt, feat_q, feat_k, pt,
+                d_normed, branch, g_gains)
+
+    def store(cols, value):
+        g_weights[0, :, cols] = value
+
+    attention_chunk(
+        lambda cols: weights[0, :, cols], gains[...], x_ref, dy_ref, xt, dt, feat_q, feat_k,
+        raw, d_raw, d_att, att, d_normed, branch, g_gains, store, lambda head: None,
+    )
 
     @pl.when(step == pl.num_programs(0) - 1)
     def _():
-        store_gain(g_gains, d_normed[...], x_ref[...], norm_gain[...])
-        d_rows = d_normed[...].astype(BF16)
-        b_rows = branch[...].astype(BF16)
-        for k, out in enumerate((out0, out1, out2, out3)):
-            out[0] = nn(pt[k], d_rows).astype(BF16)
-            out[1] = nn(pt[k], b_rows).astype(BF16)
+        take_back((out0, out1, out2, out3), pt, x_ref, norm_gain, d_normed, branch, g_gains)
 
 
 def attention_call(place, part, normed, grads, received, ids, gains, norm_gain, weights):
@@ -602,7 +703,7 @@
             num_scalar_prefetch=1,
             grid=(chunks,),
             in_specs=[own, own, pair, pair, pair,
-                      pl.BlockSpec((1, mp, PIECE), lambda m, place: (place[0], 0, 0)),
+                      pl.BlockSpec(ids.shape, lambda m, place: (0, 0, 0)),
                       line, pl.BlockSpec((1, width), lambda m, place: (0, 0)), chunk],
             out_specs=[pair] * 4 + [chunk, pl.BlockSpec((8, 128), lambda m, place: (0, 0))],
             scratch_shapes=[
@@ -632,6 +733,210 @@
     )(place, normed, grads, *received, ids, gains, norm_gain, weights)
 
 
+def front_kernel(
+    tok, cot, ids, gains, norm_gain, w_attn, w_feed,
+    normed, grads, out0, out1, out2, out3, w_ff, g_last, z_attn, g_gains,
+    got_rows, w_full, g_buf, at_core, at_first, at_second, got_z,
+    x_ref, dy_ref, xt, dt, feat_q, feat_k, pt, raw, d_raw, d_att, att, d_normed, branch,
+    row_send, row_recv, wa_send, wa_recv, wf_send, wf_recv, own_sem, at_send, at_recv,
+    z_send, z_recv,
+):
+    count, part, width = tok.shape
+    shard = w_attn.shape[0]
+    at = Place(count)
+    at.greet()
+    gather = Gather(at, w_attn, w_full, wa_send, wa_recv)
+    gather_ff = Gather(at, w_feed, w_ff, wf_send, wf_recv)
+    scatter = Scatter(at, halves(width), g_buf, at_core, at_first, at_second, at_send, at_recv)
+    own_ff = pltpu.make_async_copy(w_feed, gather_ff.piece(0), own_sem)
+
+    def row_copy(kind, k):
+        src = (normed, grads)[kind].at[k]
+        return at.copy(src, got_rows.at[k - 1, kind], row_send.at[kind, k - 1],
+                       row_recv.at[kind, k - 1], mp=at.along(k))
+
+    gather.start()
+    own_ff.start()
+    w_full[at.z, at.y, at.x, at.core] = w_attn[...]
+    gather.spread(0)
+    gain = norm_gain[...]
+    for k in (1, 3, 2, 0):
+        sequence = at.along(k)
+        x = tok[sequence].astype(F32)
+        centered = x - jnp.mean(x, axis=-1, keepdims=True)
+        spread = lax.rsqrt(jnp.mean(centered * centered, axis=-1, keepdims=True) + 1e-6)
+        pad = jnp.zeros((PIECE - part, width), BF16)
+        normed[k, :part] = (centered * spread * gain).astype(BF16)
+        normed[k, part:] = pad
+        if k:
+            row_copy(0, k).start()
+        grads[k, :part] = cot[sequence]
+        grads[k, part:] = pad
+    gather.spread(1)
+    gather.spread(3)
+    gather.forward(0)
+    gather.spread(2)
+    own_ff.wait()
+    gather_ff.spread(0)
+    gather.forward(1)
+    gather.across(0)
+    gather.forward(3)
+    for k in (1, 3, 2):
+        row_copy(0, k).wait_recv()
+    for k in (1, 3, 2):
+        row_copy(1, k).start()
+    gather_ff.start()
+    gather.across(1)
+    gather.forward(2)
+    gather.across(3)
+    gather.across(2)
+    for k in range(count):
+        gather.last(k)
+    for k in (1, 3, 2):
+        row_copy(1, k).wait_recv()
+    pieces = [(normed.at[0], grads.at[0])]
+    pieces += [(got_rows.at[k, 0], got_rows.at[k, 1]) for k in range(count - 1)]
+    prepare(at.z, part, ids, pieces, x_ref, dy_ref, xt, dt, feat_q, feat_k, pt,
+            d_normed, branch, g_gains)
+
+    def z_copy(step):
+        return at.copy(at_second.at[step, 0], got_z.at[step], z_send.at[step], z_recv.at[step],
+                       mp=at.along(1 + step))
+
+    def one_step(step, carry):
+        chunk = at.along(1 + step)
+
+        def weights(cols):
+            return w_full[chunk, :, :, :, :, cols].reshape(width, cols.stop - cols.start)
+
+        def store(cols, value):
+            split = (2, 2, 2, shard, cols.stop - cols.start)
+            g_buf[step, 0, :, :, :, :, cols] = value.reshape(split)
+
+        def poll(head):
+            @pl.when(step >= 1)
+            def _():
+                if head == 0:
+                    scatter.after_core(step - 1)
+                elif head == 1:
+                    scatter.after_first(step - 1)
+                else:
+                    scatter.after_second(step - 1)
+                    z_copy(step - 1).start()
+
+            @pl.when(step == 0)
+            def _():
+                if head == 0:
+                    gather_ff.spread(1)
+                    gather_ff.forward(0)
+                elif head == 1:
+                    gather_ff.spread(3)
+                    gather_ff.across(0)
+                else:
+                    gather_ff.spread(2)
+                    gather_ff.forward(1)
+
+            @pl.when(step == 1)
+            def _():
+                if head == 0:
+                    gather_ff.forward(3)
+                    gather_ff.across(1)
+                elif head == 1:
+                    gather_ff.forward(2)
+                    gather_ff.across(3)
+                else:
+                    gather_ff.across(2)
+
+        attention_chunk(
+            weights, gains[...], x_ref, dy_ref, xt, dt, feat_q, feat_k,
+            raw, d_raw, d_att, att, d_normed, branch, g_gains, store, poll,
+        )
+
+        @pl.when(step < count - 1)
+        def _():
+            scatter.start(step)
+
+        return carry
+
+    lax.fori_loop(0, count, one_step, 0)
+    take_back((out0, out1, out2, out3), pt, x_ref, norm_gain, d_normed, branch, g_gains)
+    g_last[...] = g_buf[count - 1:]
+    total = 0.0
+    for step in range(count - 1):
+        z_copy(step).wait_recv()
+        total = total + got_z[step].astype(F32)
+    z_attn[...] = total
+    for k in range(count):
+        gather_ff.last(k)
+
+    gather.wait_send()
+    gather_ff.wait_send()
+    for k in range(1, count):
+        for kind in range(2):
+            row_copy(kind, k).wait_send()
+    for step in range(count - 1):
+        scatter.wait_send(step)
+        z_copy(step).wait_send()
+
+
+def front_call(tokens, cotangent, ids, gains, norm_gain, w_attn, w_feed):
+    count, part, width = tokens.shape
+    shard = w_attn.shape[0]
+    vmem = pl.BlockSpec(memory_space=pltpu.VMEM)
+    hbm = pl.BlockSpec(memory_space=pl.ANY)
+    rows = jax.ShapeDtypeStruct((count, PIECE, width), BF16)
+    return pl.pallas_call(
+        front_kernel,
+        in_specs=[vmem] * 6 + [hbm],
+        out_specs=[vmem] * 6 + [hbm] + [vmem] * 3,
+        out_shape=[rows, rows]
+        + [jax.ShapeDtypeStruct((2, PIECE, width), BF16)] * 4
+        + [
+            jax.ShapeDtypeStruct((count, 2, 2, 2, 2, shard, width), BF16),
+            jax.ShapeDtypeStruct((1, 1, 2, 2, 2, shard, width), BF16),
+            jax.ShapeDtypeStruct((shard, width), F32),
+            jax.ShapeDtypeStruct((8, 128), F32),
+        ],
+        scratch_shapes=[
+            pltpu.VMEM((count - 1, 2, PIECE, width), BF16),
+            pltpu.VMEM((count, 2, 2, 2, shard, width), BF16),
+            pltpu.VMEM((count, 1, 2, 2, 2, shard, width), BF16),
+            pltpu.VMEM((count - 1, 1, 2, 2, shard, width), BF16),
+            pltpu.VMEM((count - 1, 1, 2, shard, width), BF16),
+            pltpu.VMEM((count - 1, 1, shard, width), BF16),
+            pltpu.VMEM((count - 1, shard, width), BF16),
+            pltpu.VMEM((ROWS, width), BF16),
+            pltpu.VMEM((ROWS, width), BF16),
+            pltpu.VMEM((width, ROWS), BF16),
+            pltpu.VMEM((width, ROWS), BF16),
+            pltpu.VMEM((ROWS, 128), BF16),
+            pltpu.VMEM((ROWS, 128), BF16),
+            pltpu.VMEM((count, PIECE, ROWS), BF16),
+            pltpu.VMEM((ROWS, 640), F32),
+            pltpu.VMEM((ROWS, 640), BF16),
+            pltpu.VMEM((ROWS, 256), F32),
+            pltpu.VMEM((ROWS, 256), BF16),
+            pltpu.VMEM((ROWS, width), F32),
+            pltpu.VMEM((ROWS, width), F32),
+            pltpu.SemaphoreType.DMA((2, count - 1)),
+            pltpu.SemaphoreType.DMA((2, count - 1)),
+            pltpu.SemaphoreType.DMA((8, count)),
+            pltpu.SemaphoreType.DMA((8, count)),
+            pltpu.SemaphoreType.DMA((8, count)),
+            pltpu.SemaphoreType.DMA((8, count)),
+            pltpu.SemaphoreType.DMA,
+            pltpu.SemaphoreType.DMA((3, 2, count - 1)),
+            pltpu.SemaphoreType.DMA((3, 2, count - 1)),
+            pltpu.SemaphoreType.DMA((count - 1,)),
+            pltpu.SemaphoreType.DMA((count - 1,)),
+        ],
+        compiler_params=pltpu.CompilerParams(
+            collective_id=1, has_side_effects=True, vmem_limit_bytes=VMEM
+        ),
+        name="front",
+    )(tokens, cotangent, ids, gains, norm_gain, w_attn, w_feed)
+
+
 def finish_kernel(
     place, tok, cot, gain, branch, d_ff, ret0, ret1, ret2, ret3, output, input_grad
 ):
@@ -707,37 +1012,45 @@
     me = lax.axis_index("mp")
     place = me.astype(jnp.int32)[None]
     both = ("mp", "dp")
-    w_attn = lax.all_gather(pack_attention(w_qkv, w_proj), both).reshape(mp, width, width)
-
     tok = tokens.reshape(count, part, width)
     cot = cotangent.reshape(count, part, width)
     gain = norm_gain.reshape(1, width)
-    normed, grads, *sends = norm_call(place, tok, cot, gain)
-    received = [
-        lax.ppermute(send, "mp", [(i, (i + k) % mp) for i in range(mp)])
-        for k, send in enumerate(sends, 1)
-    ]
     ids = image_ids.reshape(count, mp, part)
     ids = jnp.pad(ids, ((0, 0), (0, 0), (0, PIECE - part)), constant_values=-1)
     gains = jnp.concatenate([query_gain, key_gain]).reshape(1, 2 * HD)
-    w_ff, received = lax.optimization_barrier((jnp.stack([w_up, w_down.T]), received))
-    w_ff = lax.all_gather(w_ff, both).reshape(mp, dp, 2, shard, width)
-    *outs, g_attn, g_gains = attention_call(
-        place, part, normed, grads, received, ids, gains, gain, w_attn
-    )
-    returned = [outs[0]] + [
-        lax.ppermute(out, "mp", [(i, (i - k) % mp) for i in range(mp)])
-        for k, out in enumerate(outs[1:], 1)
-    ]
-    flat_normed = normed.reshape(count * PIECE, width)
-    flat_grads = grads.reshape(count * PIECE, width)
+    w_attn = pack_attention(w_qkv, w_proj)
+    w_ff = jnp.stack([w_up, w_down.T])
+
+    def send_back(outs):
+        return [outs[0]] + [
+            lax.ppermute(out, "mp", [(i, (i - k) % mp) for i in range(mp)])
+            for k, out in enumerate(outs[1:], 1)
+        ]
+
     if (dp, mp) == (8, 4):
+        normed, grads, *outs, w_ff, g_attn, z_attn, g_gains = front_call(
+            tok, cot, ids, gains, gain, w_attn, w_ff
+        )
+        returned = send_back(outs)
         branch, d_ff, g_attn, g_up, g_down, g_gains = feed_remote_call(
-            flat_normed, flat_grads, w_ff, g_attn.reshape(mp, 2, 2, 2, shard, width), gain, g_gains
+            normed.reshape(count * PIECE, width), grads.reshape(count * PIECE, width),
+            w_ff.reshape(mp, dp, 2, shard, width), g_attn, z_attn, gain, g_gains,
         )
     else:
+        w_attn = lax.all_gather(w_attn, both).reshape(mp, width, width)
+        w_ff = lax.all_gather(w_ff, both).reshape(mp, dp, 2, shard, width)
+        normed, grads, *sends = norm_call(place, tok, cot, gain)
+        received = [
+            lax.ppermute(send, "mp", [(i, (i + k) % mp) for i in range(mp)])
+            for k, send in enumerate(sends, 1)
+        ]
+        *outs, g_attn, g_gains = attention_call(
+            place, part, normed, grads, received, ids, gains, gain, w_attn
+        )
+        returned = send_back(outs)
+        flat_normed = normed.reshape(count * PIECE, width)
         branch, d_ff, g_up, g_down = feed_call(
-            flat_normed, flat_grads,
+            flat_normed, grads.reshape(count * PIECE, width),
             w_ff[:, :, 0].reshape(mp, width, width), w_ff[:, :, 1].reshape(mp, width, width),
         )
         g_attn, g_up, g_down = (
@@ -748,7 +1061,7 @@
         )
         own = jnp.sum(d_ff * flat_normed.astype(F32), axis=0) / norm_gain
         g_gains = g_gains.at[:width // 128].add(own.reshape(-1, 128))
-        g_gains = lax.psum(g_gains, ("dp", "mp"))
+        g_gains = lax.psum(g_gains, both)
     output, input_grad = finish_call(
         place, tok, cot, gain,
         branch.reshape(count, PIECE, width), d_ff.reshape(count, PIECE, width), returned,

time: 357 us -> 340 us (0.952); the launches traced: 357 us -> 335 us
  Pallas kernels: 211 us -> 307 us
  waiting for transfers between devices: 94.4 us -> 0.01 us
  between operations: 14.5 us -> 1.09 us
  starting transfers between devices: 11.3 us -> 2.07 us
    pallas_call x2 -> x1, Pallas kernels: 97.5 us -> 217 us  [front_call(): pl.pallas_call(front_kernel, in_specs=[vmem] * 6 + [hbm], out_specs=[vmem...]
    ppermute x6 -> x3, waiting for transfers between devices: 52.7 us -> 0.01 us  [send_back(): lax.ppermute(out, 'mp', [(i, (i - k) % mp) for i in range(mp)])]
    all_gather x2 -> x0, waiting for transfers between devices: 41.6 us -> none  [the longest x1 41.6 us: body(): lax.all_gather(pack_attention(w_qkv, w_proj), both)]
    pallas_call x1, Pallas kernels: 106 us -> 81.5 us  [feed_remote_call(): pl.pallas_call(feed_remote_kernel, in_specs=[vmem, vmem, pl.BlockSpec(mem...]
    ppermute x6 -> x3, starting transfers between devices: 11.2 us -> 2.07 us  [send_back(): lax.ppermute(out, 'mp', [(i, (i - k) % mp) for i in range(mp)])]
    unnamed x46 -> x38, local copies, waits for them, and re-layouts: 15.3 us -> 16.6 us
  transfers between devices with their start and end apart: 8 -> 3, of which waited for: 3 -> 0; matrix products, arithmetic and copies ran while one was open for 3% -> 2% of each run, Pallas kernels for 57% -> 24%
where the time goes in v3:
time: 340 us; the launch traced here: 335 us
  Pallas kernels  307 us (90%)
  local copies, waits for them, and re-layouts  23 us (7%)
    pallas_call x1, Pallas kernels, front_call(): pl.pallas_call(front_kernel, in_specs=[vmem] * 6 + [hbm], out_specs=[vmem...  217 us
    pallas_call x1, Pallas kernels, feed_remote_call(): pl.pallas_call(feed_remote_kernel, in_specs=[vmem, vmem, pl.BlockSpec(mem...  81.5 us
    unnamed x38, local copies, waits for them, and re-layouts  16.6 us
    pallas_call x1, Pallas kernels, finish_call(): pl.pallas_call(finish_kernel, grid_spec=pltpu.PrefetchScalarGridSpec(num_...  7.95 us
  transfers between devices with their start and end apart: 3, of which 0 were waited for; matrix products, arithmetic and copies ran while one was open for 2% of the time, Pallas kernels for 24%

profile of v3, /device:TPU:0, one launch (start us, length us, event | category | flops | bytes accessed | tf_op | source)
XLA Modules:
  0.0 335.0 jit_solution(7355018700460088951)
XLA Ops:
  0.6 0.8 slice_bitcast_fusion.2
  1.4 0.0 copy-start.1
  1.4 1.4 reshape.73.norm_gain.gain
  2.8 2.7 copy.27
  5.5 0.0 copy-done.1
  5.5 0.0 slice-start
  5.5 0.0 copy-start.9
  5.5 0.0 copy-start.10
  5.5 0.0 copy-start.7
  5.5 0.0 copy-start.8
  5.5 0.0 copy-start.12
  5.5 0.0 copy-start.13
  5.5 1.3 copy.28
  6.8 0.0 slice-done
  6.8 0.1 copy.40
  7.0 0.1 copy.32
  7.1 0.0 copy-done.9
  7.1 0.1 copy.31
  7.2 0.0 copy-done.10
  7.2 0.1 reshape.74
  7.3 0.0 copy-done.7
  7.3 0.0 copy-done.8
  7.3 0.7 pad_maximum_fusion.w_feed
  8.1 0.6 pad.4.ids
  8.7 0.0 copy-done.12
  8.7 0.0 copy-done.13
  8.7 0.6 maximum_bitcast_fusion.gains
  9.3 0.7 pad_maximum_fusion.2.w_attn
  10.0 217.3 %front.1 = (bf16[4,240,768]{2,1,0:T(8,128)(2,1)}, bf16[4,240,768]{2,1,0:T(8,128)(2,1)}, bf16[2,240,768]{2,1,0:T(8,128)(2,1)}, bf16[2,240,768]{2,1,0:T(8,128)(2,1...) custom-call(bf16[4,236,768]{2,1,0:T(8,128)(2,1)} %bitcast.38, ...), custom_call_target="tpu_custom_call" | custom-call | tf_op jit(solution)/shard_map/front/pallas_call | solution.py:888
  227.4 0.1 collective-permute-start
  227.4 0.1 collective-permute-start.1
  227.5 1.9 collective-permute-start.2
  229.5 81.5 %feed_forward_scatter.1 = (f32[960,768]{1,0:T(8,128)}, f32[960,768]{1,0:T(8,128)}, f32[96,768]{1,0:T(8,128)}, f32[96,768]{1,0:T(8,128)}, f32[96,768]{1,0:T(8,128)}, /*index=5*/f32[8,128]{1,0:T(8,128)}) custom-call(bf16[960,768]{1,0:T(8,128)(2,1)} %bitcast.55, bf16[960,768]{1,0:T(8,128)(2,1)} %bitcast.56, bf16[4,8,2,96,768]{4,3,2,1,0:T(8,128)(2,1)} %bitcast.54, ...), custom_call_target="tpu_custom_call" | custom-call | flops 27179089920 | bytes 18874368 | tf_op jit(solution)/shard_map/feed_forward_scatter/pallas_call | solution.py:457
  310.9 0.0 copy-start.11
  310.9 0.9 slice.35
  311.9 1.1 slice_bitcast_fusion
  312.9 0.1 copy.35
  313.0 0.1 copy.33
  313.2 0.9 copy.38
  314.1 0.7 copy.39
  314.8 0.0 copy-done.11
  314.8 0.6 slice_bitcast_fusion.4
  315.4 0.6 slice_bitcast_fusion.3
  316.0 0.0 collective-permute-done.ret1
  316.0 0.0 copy-start.2
  316.0 0.0 collective-permute-done.1.ret2
  316.0 0.0 copy-start.3
  316.0 0.0 collective-permute-done.2.ret3
  316.0 0.0 copy-start.4
  316.1 0.8 copy-done.2
  316.9 0.3 copy-done.3
  317.1 0.3 copy-done.4
  317.4 8.0 %finish.1 = (bf16[4,236,768]{2,1,0:T(8,128)(2,1)}, f32[4,236,768]{2,1,0:T(8,128)}) custom-call(s32[1]{0:T(128)} %bitcast.place, bf16[4,236,768]{2,1,0:T(8,128)(2,1)} %bitcast.39, bf16[4,236,768]{2,1,0:T(8,128)(2,1)} %bitcast.41, f32[1,768]{1,0:T(1,128)} %reshape.73.norm_gain.gain, f32[4,240,768]{2,1,0:T(8,128)} %bitcast.42, f32[4,240,768]{2,1,0:T(8,128)} %bitcast.43, ...), custom_call_target="tpu_custom_call" | custom-call | tf_op jit(solution)/shard_map/finish/pallas_call | solution.py:973
  325.3 0.0 copy-start
  325.3 5.8 %copy.37 = f32[2,2,236,768]{3,1,2,0:T(2,128)} copy(f32[2,2,236,768]{3,2,1,0:T(8,128)} %bitcast.44) | data formatting | bytes 5799936
  331.1 0.0 copy-start.6
  331.1 0.0 copy-done
  331.1 0.0 copy-start.5
  331.1 2.2 copy.36
  333.3 0.0 copy-done.6
  333.3 0.7 copy.43
  334.1 0.0 copy-done.5
  334.1 0.7 copy.44
  (3 shorter events, 0.1 us)
Async XLA Ops:
  1.4 4.0 %copy-start.1 = (bf16[2,2,236,768]{3,1,2,0:T(2,128)(2,1)S(1)}, bf16[2,2,236,768]{3,1,2,0:T(2,128)(2,1)}, u32[]{:S(2)}) copy-start(bf16[2,2,236,768]{3,1,2,0:T(2,128)(2,1)} %param.19) | copy-start | bytes 4349956
  5.5 1.4 slice-start
  5.5 1.6 copy-start.9
  5.5 1.7 copy-start.10
  5.5 1.8 copy-start.7
  5.5 1.8 copy-start.8
  5.5 3.2 copy-start.12
  5.5 3.2 copy-start.13
  227.4 88.6 %collective-permute-start = (bf16[2,240,768]{2,1,0:T(8,128)(2,1)}, bf16[2,240,768]{2,1,0:T(8,128)(2,1)S(1)}, u32[]{:S(2)}, u32[]{:S(2)}) collective-permute-start(bf16[2,240,768]{2,1,0:T(8,128)(2,1)} %get-tuple-element.36), channel_id=1, source_target_pairs={{0,3},{1,0},{2,1},{3,2},{4,7},{5,4},{6,5},{7,6},{8,11},{9,8},{10,9... | collective-permute-start | bytes 2211848 | tf_op jit(solution)/shard_map/ppermute | solution.py:1026
  227.4 88.6 %collective-permute-start.1 = (bf16[2,240,768]{2,1,0:T(8,128)(2,1)}, bf16[2,240,768]{2,1,0:T(8,128)(2,1)S(1)}, u32[]{:S(2)}, u32[]{:S(2)}) collective-permute-start(bf16[2,240,768]{2,1,0:T(8,128)(2,1)} %get-tuple-element.37), channel_id=1, source_target_pairs={{0,2},{1,3},{2,0},{3,1},{4,6},{5,7},{6,4},{7,5},{8,10},{9,11},{10,... | collective-permute-start | bytes 2211848 | tf_op jit(solution)/shard_map/ppermute | solution.py:1026
  227.5 88.5 %collective-permute-start.2 = (bf16[2,240,768]{2,1,0:T(8,128)(2,1)}, bf16[2,240,768]{2,1,0:T(8,128)(2,1)S(1)}, u32[]{:S(2)}, u32[]{:S(2)}) collective-permute-start(bf16[2,240,768]{2,1,0:T(8,128)(2,1)} %get-tuple-element.38), channel_id=1, source_target_pairs={{0,1},{1,2},{2,3},{3,0},{4,5},{5,6},{6,7},{7,4},{8,9},{9,10},{10,1... | collective-permute-start | bytes 2211848 | tf_op jit(solution)/shard_map/ppermute | solution.py:1026
  310.9 3.9 %copy-start.11 = (f32[8,128]{1,0:T(8,128)S(1)}, f32[8,128]{1,0:T(8,128)}, u32[]{:S(2)}) copy-start(f32[8,128]{1,0:T(8,128)} %get-tuple-element.44) | copy-start | bytes 12292
  316.0 0.9 copy-start.2
  316.0 1.1 copy-start.3
  316.0 1.3 copy-start.4
  325.3 5.8 %copy-start = (bf16[4,236,768]{2,1,0:T(8,128)(2,1)S(1)}, bf16[4,236,768]{2,1,0:T(8,128)(2,1)}, u32[]{:S(2)}) copy-start(bf16[4,236,768]{2,1,0:T(8,128)(2,1)} %get-tuple-element.39) | copy-start | bytes 4349956
  331.1 2.2 copy-start.6
  331.1 2.9 copy-start.5

commit v4 on v3

--- a/solution.py
+++ b/solution.py
@@ -785,7 +785,6 @@
         row_copy(0, k).wait_recv()
     for k in (1, 3, 2):
         row_copy(1, k).start()
-    gather_ff.start()
     gather.across(1)
     gather.forward(2)
     gather.across(3)
@@ -794,6 +793,7 @@
         gather.last(k)
     for k in (1, 3, 2):
         row_copy(1, k).wait_recv()
+    gather_ff.start()
     pieces = [(normed.at[0], grads.at[0])]
     pieces += [(got_rows.at[k, 0], got_rows.at[k, 1]) for k in range(count - 1)]
     prepare(at.z, part, ids, pieces, x_ref, dy_ref, xt, dt, feat_q, feat_k, pt,

time: 340 us -> 334 us (0.982); the launches traced: 335 us -> 333 us
    pallas_call x1, Pallas kernels: 217 us -> 205 us  [front_call(): pl.pallas_call(front_kernel, in_specs=[vmem] * 6 + [hbm], out_specs=[vmem...]
    pallas_call x1, Pallas kernels: 81.5 us -> 90.9 us  [feed_remote_call(): pl.pallas_call(feed_remote_kernel, in_specs=[vmem, vmem, pl.BlockSpec(mem...]
  transfers between devices with their start and end apart: 3 -> 3, of which waited for: 0 -> 0; matrix products, arithmetic and copies ran while one was open for 2% -> 2% of each run, Pallas kernels for 24% -> 27%
where the time goes in v4:
time: 334 us; the launch traced here: 333 us
  Pallas kernels  304 us (91%)
  local copies, waits for them, and re-layouts  23 us (7%)
  starting transfers between devices  3.75 us (1%)
    pallas_call x1, Pallas kernels, front_call(): pl.pallas_call(front_kernel, in_specs=[vmem] * 6 + [hbm], out_specs=[vmem...  205 us
    pallas_call x1, Pallas kernels, feed_remote_call(): pl.pallas_call(feed_remote_kernel, in_specs=[vmem, vmem, pl.BlockSpec(mem...  90.9 us
    unnamed x38, local copies, waits for them, and re-layouts  16.6 us
    pallas_call x1, Pallas kernels, finish_call(): pl.pallas_call(finish_kernel, grid_spec=pltpu.PrefetchScalarGridSpec(num_...  7.95 us
  transfers between devices with their start and end apart: 3, of which 0 were waited for; matrix products, arithmetic and copies ran while one was open for 2% of the time, Pallas kernels for 27%

profile of v4, /device:TPU:0, one launch (start us, length us, event | category | flops | bytes accessed | tf_op | source)
XLA Modules:
  0.0 333.4 jit_solution(3444033643678520413)
XLA Ops:
  0.6 0.8 slice_bitcast_fusion.2
  1.4 0.0 copy-start.1
  1.4 1.4 reshape.73.norm_gain.gain
  2.8 2.7 copy.27
  5.5 0.0 copy-done.1
  5.5 0.0 slice-start
  5.5 0.0 copy-start.9
  5.5 0.0 copy-start.10
  5.5 0.0 copy-start.7
  5.5 0.0 copy-start.8
  5.5 0.0 copy-start.12
  5.5 0.0 copy-start.13
  5.5 1.3 copy.28
  6.8 0.0 slice-done
  6.8 0.1 copy.40
  7.0 0.1 copy.32
  7.1 0.0 copy-done.9
  7.1 0.1 copy.31
  7.2 0.0 copy-done.10
  7.2 0.1 reshape.74
  7.3 0.0 copy-done.7
  7.3 0.0 copy-done.8
  7.3 0.7 pad_maximum_fusion.w_feed
  8.1 0.6 pad.4.ids
  8.7 0.0 copy-done.12
  8.7 0.0 copy-done.13
  8.7 0.6 maximum_bitcast_fusion.gains
  9.3 0.7 pad_maximum_fusion.2.w_attn
  10.0 204.7 %front.1 = (bf16[4,240,768]{2,1,0:T(8,128)(2,1)}, bf16[4,240,768]{2,1,0:T(8,128)(2,1)}, bf16[2,240,768]{2,1,0:T(8,128)(2,1)}, bf16[2,240,768]{2,1,0:T(8,128)(2,1...) custom-call(bf16[4,236,768]{2,1,0:T(8,128)(2,1)} %bitcast.38, ...), custom_call_target="tpu_custom_call" | custom-call | tf_op jit(solution)/shard_map/front/pallas_call | solution.py:888
  214.7 0.5 collective-permute-start
  215.2 3.2 collective-permute-start.1
  218.5 0.0 collective-permute-start.2
  218.5 90.9 %feed_forward_scatter.1 = (f32[960,768]{1,0:T(8,128)}, f32[960,768]{1,0:T(8,128)}, f32[96,768]{1,0:T(8,128)}, f32[96,768]{1,0:T(8,128)}, f32[96,768]{1,0:T(8,128)}, /*index=5*/f32[8,128]{1,0:T(8,128)}) custom-call(bf16[960,768]{1,0:T(8,128)(2,1)} %bitcast.55, bf16[960,768]{1,0:T(8,128)(2,1)} %bitcast.56, bf16[4,8,2,96,768]{4,3,2,1,0:T(8,128)(2,1)} %bitcast.54, ...), custom_call_target="tpu_custom_call" | custom-call | flops 27179089920 | bytes 18874368 | tf_op jit(solution)/shard_map/feed_forward_scatter/pallas_call | solution.py:457
  309.4 0.0 copy-start.11
  309.4 0.9 slice.35
  310.3 1.1 slice_bitcast_fusion
  311.4 0.1 copy.35
  311.5 0.1 copy.33
  311.7 0.9 copy.38
  312.5 0.7 copy.39
  313.3 0.0 copy-done.11
  313.3 0.6 slice_bitcast_fusion.4
  313.9 0.6 slice_bitcast_fusion.3
  314.5 0.0 collective-permute-done.ret1
  314.5 0.0 copy-start.2
  314.5 0.0 collective-permute-done.1.ret2
  314.5 0.0 copy-start.3
  314.5 0.0 collective-permute-done.2.ret3
  314.5 0.0 copy-start.4
  314.5 0.8 copy-done.2
  315.3 0.3 copy-done.3
  315.6 0.3 copy-done.4
  315.8 8.0 %finish.1 = (bf16[4,236,768]{2,1,0:T(8,128)(2,1)}, f32[4,236,768]{2,1,0:T(8,128)}) custom-call(s32[1]{0:T(128)} %bitcast.place, bf16[4,236,768]{2,1,0:T(8,128)(2,1)} %bitcast.39, bf16[4,236,768]{2,1,0:T(8,128)(2,1)} %bitcast.41, f32[1,768]{1,0:T(1,128)} %reshape.73.norm_gain.gain, f32[4,240,768]{2,1,0:T(8,128)} %bitcast.42, f32[4,240,768]{2,1,0:T(8,128)} %bitcast.43, ...), custom_call_target="tpu_custom_call" | custom-call | tf_op jit(solution)/shard_map/finish/pallas_call | solution.py:973
  323.8 0.0 copy-start
  323.8 5.8 %copy.37 = f32[2,2,236,768]{3,1,2,0:T(2,128)} copy(f32[2,2,236,768]{3,2,1,0:T(8,128)} %bitcast.44) | data formatting | bytes 5799936
  329.6 0.0 copy-start.6
  329.6 0.0 copy-done
  329.6 0.0 copy-start.5
  329.6 2.2 copy.36
  331.8 0.0 copy-done.6
  331.8 0.7 copy.43
  332.5 0.0 copy-done.5
  332.5 0.7 copy.44
  (3 shorter events, 0.1 us)
Async XLA Ops:
  1.4 4.0 %copy-start.1 = (bf16[2,2,236,768]{3,1,2,0:T(2,128)(2,1)S(1)}, bf16[2,2,236,768]{3,1,2,0:T(2,128)(2,1)}, u32[]{:S(2)}) copy-start(bf16[2,2,236,768]{3,1,2,0:T(2,128)(2,1)} %param.19) | copy-start | bytes 4349956
  5.5 1.4 slice-start
  5.5 1.6 copy-start.9
  5.5 1.7 copy-start.10
  5.5 1.8 copy-start.7
  5.5 1.8 copy-start.8
  5.5 3.2 copy-start.12
  5.5 3.2 copy-start.13
  214.7 99.7 %collective-permute-start = (bf16[2,240,768]{2,1,0:T(8,128)(2,1)}, bf16[2,240,768]{2,1,0:T(8,128)(2,1)S(1)}, u32[]{:S(2)}, u32[]{:S(2)}) collective-permute-start(bf16[2,240,768]{2,1,0:T(8,128)(2,1)} %get-tuple-element.36), channel_id=1, source_target_pairs={{0,3},{1,0},{2,1},{3,2},{4,7},{5,4},{6,5},{7,6},{8,11},{9,8},{10,9... | collective-permute-start | bytes 2211848 | tf_op jit(solution)/shard_map/ppermute | solution.py:1026
  215.2 99.2 %collective-permute-start.1 = (bf16[2,240,768]{2,1,0:T(8,128)(2,1)}, bf16[2,240,768]{2,1,0:T(8,128)(2,1)S(1)}, u32[]{:S(2)}, u32[]{:S(2)}) collective-permute-start(bf16[2,240,768]{2,1,0:T(8,128)(2,1)} %get-tuple-element.37), channel_id=1, source_target_pairs={{0,2},{1,3},{2,0},{3,1},{4,6},{5,7},{6,4},{7,5},{8,10},{9,11},{10,... | collective-permute-start | bytes 2211848 | tf_op jit(solution)/shard_map/ppermute | solution.py:1026
  218.5 96.0 %collective-permute-start.2 = (bf16[2,240,768]{2,1,0:T(8,128)(2,1)}, bf16[2,240,768]{2,1,0:T(8,128)(2,1)S(1)}, u32[]{:S(2)}, u32[]{:S(2)}) collective-permute-start(bf16[2,240,768]{2,1,0:T(8,128)(2,1)} %get-tuple-element.38), channel_id=1, source_target_pairs={{0,1},{1,2},{2,3},{3,0},{4,5},{5,6},{6,7},{7,4},{8,9},{9,10},{10,1... | collective-permute-start | bytes 2211848 | tf_op jit(solution)/shard_map/ppermute | solution.py:1026
  309.4 3.9 %copy-start.11 = (f32[8,128]{1,0:T(8,128)S(1)}, f32[8,128]{1,0:T(8,128)}, u32[]{:S(2)}) copy-start(f32[8,128]{1,0:T(8,128)} %get-tuple-element.44) | copy-start | bytes 12292
  314.5 0.9 copy-start.2
  314.5 1.1 copy-start.3
  314.5 1.3 copy-start.4
  323.8 5.8 %copy-start = (bf16[4,236,768]{2,1,0:T(8,128)(2,1)S(1)}, bf16[4,236,768]{2,1,0:T(8,128)(2,1)}, u32[]{:S(2)}) copy-start(bf16[4,236,768]{2,1,0:T(8,128)(2,1)} %get-tuple-element.39) | copy-start | bytes 4349956
  329.6 2.2 copy-start.6
  329.6 2.9 copy-start.5

commit v5 on v4

--- a/solution.py
+++ b/solution.py
@@ -15,6 +15,7 @@
 REST = 256
 ROWS = BIG + REST
 VMEM = 60 * 1024 * 1024
+FRONT_VMEM = 63 * 1024 * 1024
 F32 = jnp.float32
 BF16 = jnp.bfloat16
 
@@ -733,13 +734,142 @@
     )(place, normed, grads, *received, ids, gains, norm_gain, weights)
 
 
+def group_means():
+    same = (iota((128, 128), 0) // HD == iota((128, 128), 1) // HD).astype(F32)
+    return (same * (1.0 / HD)).astype(BF16)
+
+
+def forward_chunk(
+    weights, gain, x_ref, feat_q, feat_k, raw, qk_all, v_all, stats, att, branch, begin, spill
+):
+    raw[...] = nn(x_ref[...], weights(slice(0, 640)))
+    lane = iota((1, 128), 1)
+    low = lane < HD
+    mean_of = group_means()
+    stat = jnp.zeros((ROWS, 128), F32)
+    for head in range(3):
+        qk = raw[:, 128 * head:128 * head + 128]
+        high = qk.astype(BF16)
+        mean = nn(high, mean_of) + nn((qk - high.astype(F32)).astype(BF16), mean_of)
+        centered = qk - mean
+        spread = lax.rsqrt(nn((centered * centered).astype(BF16), mean_of) + 1e-6)
+        rounded = (centered * spread * gain).astype(BF16)
+        qk_all[head] = rounded
+        rounded = rounded.astype(F32)
+        q_aug = jnp.where(low, rounded * 0.125, feat_q[...].astype(F32)).astype(BF16)
+        k_aug = jnp.where(low, pltpu.roll(rounded, HD, 1), feat_k[...].astype(F32)).astype(BF16)
+        v_tile = 384 + 128 * (head // 2)
+        v = raw[:, v_tile:v_tile + 128]
+        if head == 1:
+            v = pltpu.roll(v, HD, 1)
+        v_aug = jnp.where(low, v, 1.0).astype(BF16)
+        v_all[head] = v_aug
+        p_ref = begin(head)
+        parts = []
+        for base, count in ((0, BIG), (BIG, REST)):
+            keys = k_aug[base:base + count]
+            values = v_aug[base:base + count]
+            for row in range(base, base + count, 256):
+                rows = slice(row, row + 256)
+                prob = jnp.exp(nt(q_aug[rows], keys)).astype(BF16)
+                p_ref[rows, :count] = prob
+                parts.append(nn(prob, values))
+        spill(head)
+        gathered = jnp.concatenate(parts, axis=0)
+        inverse = 1.0 / gathered
+        attend = gathered * pltpu.roll(inverse, HD, 1)
+        stat = jnp.where((lane == head) | (lane == HD + head), spread, stat)
+        stat = jnp.where(lane == HD + 8 + head, inverse, stat)
+        if head == 0:
+            att[:, 0:128] = jnp.where(low, 0.0, pltpu.roll(attend, HD, 1)).astype(BF16)
+        elif head == 1:
+            first = attend
+        else:
+            att[:, 128:256] = jnp.where(low, first, pltpu.roll(attend, HD, 1)).astype(BF16)
+    stats[...] = stat
+    branch[...] += nt(att[...], weights(slice(512, 768)))
+
+
+def backward_chunk(
+    weights, gain, dy_ref, xt, dt, raw, d_raw, d_score_ref, qk_all, v_all, stats, att,
+    d_normed, g_gains, ready, store, poll,
+):
+    raw[:, :256] = nn(dy_ref[...], weights(slice(512, 768)))
+    lane = iota((1, 128), 1)
+    low = lane < HD
+    mean_of = group_means()
+    stat = stats[...]
+    back_gain = 1.0 / gain
+    d_gain = jnp.zeros((1, 128), F32)
+    for head in range(3):
+        qk = qk_all[head]
+        v_aug = v_all[head]
+        tile = 128 * ((head + 1) // 2)
+        da = raw[:, tile:tile + 128]
+        out = att[:, tile:tile + 128].astype(F32)
+        if head != 1:
+            da = pltpu.roll(da, HD, 1)
+            out = pltpu.roll(out, HD, 1)
+        inverse = stat[:, HD + 8 + head:HD + 9 + head]
+        scaled = jnp.where(low, da * inverse, 0.0).astype(BF16).astype(F32)
+        dot = jnp.sum(scaled * out, axis=-1, keepdims=True)
+        dot_high = dot.astype(BF16).astype(F32)
+        d_aug = jnp.where(
+            lane == HD, -dot_high, jnp.where(lane == HD + 1, dot_high - dot, scaled)
+        )
+        d_low = d_aug.astype(BF16)
+        d_t = d_aug.T.astype(BF16)
+        qk_low = qk.astype(F32)
+        qk_t = qk_low.T.astype(BF16)
+        p_ref = ready(head)
+        d_queries, d_keys, d_values = [], [], []
+        for base, count in ((0, BIG), (BIG, REST)):
+            block = slice(base, base + count)
+            for row in range(base, base + count, 256):
+                rows = slice(row, row + 256)
+                d_prob = nt(d_low[rows], v_aug[block])
+                d_score = (p_ref[rows, :count].astype(F32) * d_prob).astype(BF16)
+                d_score_ref[rows, :count] = d_score
+                d_queries.append(nn(d_score, qk[block]))
+            d_keys.append(nn(qk_t[:, block], d_score_ref[block, :count]).T)
+            d_values.append(nn(d_t[:, block], p_ref[block, :count]).T)
+        d_query = jnp.concatenate(d_queries, axis=0)
+        d_key = jnp.concatenate(d_keys, axis=0)
+        d_value = jnp.concatenate(d_values, axis=0)
+        d_qk = pltpu.roll(jnp.where(low, d_key, d_query), HD, 1) * 0.125
+        unit = qk_low * back_gain
+        spread = jnp.where(low, stat[:, head:head + 1], stat[:, HD + head:HD + head + 1])
+        d_gain = d_gain + jnp.sum(d_qk * unit, axis=0, keepdims=True)
+        scaled = d_qk * gain
+        mean = nn(scaled.astype(BF16), mean_of)
+        d_qk = spread * (scaled - mean - unit * nn((scaled * unit).astype(BF16), mean_of))
+        d_raw[:, 128 * head:128 * head + 128] = d_qk.astype(BF16)
+        if head == 0:
+            first = d_value
+        elif head == 1:
+            both = jnp.where(low, first, pltpu.roll(d_value, HD, 1))
+            d_raw[:, 384:512] = both.astype(BF16)
+        else:
+            d_raw[:, 512:640] = jnp.where(low, d_value, 0.0).astype(BF16)
+        poll(head)
+    g_gains[6:7] += d_gain
+    d_projected = d_raw[...]
+    d_normed[...] += nt(d_projected, weights(slice(0, 640)))
+    left = nn(xt[...], d_projected)
+    right = nn(dt[...], att[...])
+    store(slice(0, 512), left[:, :512].astype(BF16))
+    store(slice(512, 640), (left[:, 512:] + right[:, :128]).astype(BF16))
+    store(slice(640, 768), right[:, 128:].astype(BF16))
+
+
 def front_kernel(
     tok, cot, ids, gains, norm_gain, w_attn, w_feed,
-    normed, grads, out0, out1, out2, out3, w_ff, g_last, z_attn, g_gains,
-    got_rows, w_full, g_buf, at_core, at_first, at_second, got_z,
-    x_ref, dy_ref, xt, dt, feat_q, feat_k, pt, raw, d_raw, d_att, att, d_normed, branch,
-    row_send, row_recv, wa_send, wa_recv, wf_send, wf_recv, own_sem, at_send, at_recv,
-    z_send, z_recv,
+    normed, grads, returned, out0, out1, out2, out3, w_ff, g_last, z_attn, g_gains, p_all,
+    got_rows, back_rows, w_full, g_buf, at_core, at_first, at_second, got_z,
+    x_ref, dy_ref, xt, dt, feat_q, feat_k, pt, raw, d_raw, d_score, p_buf,
+    qk_all, v_all, stats, att, total,
+    row_send, row_recv, back_send, back_recv, wa_send, wa_recv, wf_send, wf_recv, own_sem,
+    p_out, p_in, at_send, at_recv, z_send, z_recv,
 ):
     count, part, width = tok.shape
     shard = w_attn.shape[0]
@@ -754,6 +884,10 @@
         src = (normed, grads)[kind].at[k]
         return at.copy(src, got_rows.at[k - 1, kind], row_send.at[kind, k - 1],
                        row_recv.at[kind, k - 1], mp=at.along(k))
+
+    def back_copy(k):
+        return at.copy(back_rows.at[k - 1], returned.at[k], back_send.at[k - 1],
+                       back_recv.at[k - 1], mp=at.along(-k))
 
     gather.start()
     own_ff.start()
@@ -772,6 +906,9 @@
             row_copy(0, k).start()
         grads[k, :part] = cot[sequence]
         grads[k, part:] = pad
+    place_rows(at.z, part, ids, pt, feat_q, feat_k)
+    g_gains[...] = jnp.zeros_like(g_gains)
+    total[...] = jnp.zeros_like(total)
     gather.spread(1)
     gather.spread(3)
     gather.forward(0)
@@ -781,10 +918,6 @@
     gather.forward(1)
     gather.across(0)
     gather.forward(3)
-    for k in (1, 3, 2):
-        row_copy(0, k).wait_recv()
-    for k in (1, 3, 2):
-        row_copy(1, k).start()
     gather.across(1)
     gather.forward(2)
     gather.across(3)
@@ -792,26 +925,115 @@
     for k in range(count):
         gather.last(k)
     for k in (1, 3, 2):
+        row_copy(0, k).wait_recv()
+    for k in (1, 3, 2):
+        row_copy(1, k).start()
+
+    def lay_out(kind, own, rows, columns):
+        value = 0.0
+        for k in range(count):
+            piece = own[0] if k == 0 else got_rows[k - 1, kind]
+            value = value + lax.dot_general(
+                pt[k], piece, (((0,), (0,)), ((), ())), preferred_element_type=F32
+            )
+        value = value.astype(BF16)
+        rows[...] = value
+        columns[...] = value.T
+
+    lay_out(0, normed, x_ref, xt)
+
+    def weights_of(chunk):
+        def weights(cols):
+            return w_full[chunk, :, :, :, :, cols].reshape(width, cols.stop - cols.start)
+
+        return weights
+
+    def p_write(step, head):
+        slot = lax.rem(step + head, 2)
+        return pltpu.make_async_copy(p_buf.at[slot], p_all.at[at.along(step), head],
+                                     p_out.at[slot])
+
+    def p_read(step, head):
+        slot = lax.rem(step + head, 2)
+        return pltpu.make_async_copy(p_all.at[at.along(1 + step), head], p_buf.at[slot],
+                                     p_in.at[slot])
+
+    def forward_step(step, carry):
+        chunk = at.along(step)
+
+        def begin(head):
+            if head == 2:
+                p_write(step, 0).wait()
+            else:
+                @pl.when(step >= 1)
+                def _():
+                    p_write(step - 1, 1 + head).wait()
+            return p_buf.at[lax.rem(step + head, 2)]
+
+        forward_chunk(
+            weights_of(chunk), gains[...], x_ref, feat_q, feat_k, raw, qk_all.at[chunk],
+            v_all.at[chunk], stats.at[chunk], att.at[chunk], total, begin,
+            lambda head: p_write(step, head).start(),
+        )
+        return carry
+
+    lax.fori_loop(0, count, forward_step, 0)
+    for head in (1, 2):
+        p_write(count - 1, head).wait()
+    p_read(0, 0).start()
+    value = total[...].astype(BF16)
+    returned[0] = nn(pt[0], value).astype(BF16)
+    for k in range(1, count):
+        back_rows[k - 1] = nn(pt[k], value).astype(BF16)
+    total[...] = jnp.zeros_like(total)
+    for k in (1, 3, 2):
         row_copy(1, k).wait_recv()
     gather_ff.start()
-    pieces = [(normed.at[0], grads.at[0])]
-    pieces += [(got_rows.at[k, 0], got_rows.at[k, 1]) for k in range(count - 1)]
-    prepare(at.z, part, ids, pieces, x_ref, dy_ref, xt, dt, feat_q, feat_k, pt,
-            d_normed, branch, g_gains)
+    lay_out(1, grads, dy_ref, dt)
 
     def z_copy(step):
         return at.copy(at_second.at[step, 0], got_z.at[step], z_send.at[step], z_recv.at[step],
                        mp=at.along(1 + step))
 
-    def one_step(step, carry):
+    def events(step, head):
+        if step == 0 and head == 1:
+            gather_ff.forward(0)
+        elif step == 0 and head == 2:
+            gather_ff.across(0)
+        elif step == 1 and head == 0:
+            for k in (1, 3, 2):
+                back_copy(k).start()
+            gather_ff.spread(1)
+        elif step == 1 and head == 1:
+            gather_ff.spread(3)
+        elif step == 1 and head == 2:
+            gather_ff.spread(2)
+            gather_ff.forward(1)
+        elif step == 2 and head == 0:
+            gather_ff.forward(3)
+            gather_ff.across(1)
+        elif step == 2 and head == 1:
+            gather_ff.forward(2)
+            gather_ff.across(3)
+        elif step == 2 and head == 2:
+            gather_ff.across(2)
+
+    def backward_step(step, carry):
         chunk = at.along(1 + step)
-
-        def weights(cols):
-            return w_full[chunk, :, :, :, :, cols].reshape(width, cols.stop - cols.start)
 
         def store(cols, value):
             split = (2, 2, 2, shard, cols.stop - cols.start)
             g_buf[step, 0, :, :, :, :, cols] = value.reshape(split)
+
+        def ready(head):
+            p_read(step, head).wait()
+            if head < 2:
+                p_read(step, head + 1).start()
+            else:
+                @pl.when(step + 1 < count)
+                def _():
+                    p_read(step + 1, 0).start()
+            return p_buf.at[lax.rem(step + head, 2)]
 
         def poll(head):
             @pl.when(step >= 1)
@@ -824,32 +1046,15 @@
                     scatter.after_second(step - 1)
                     z_copy(step - 1).start()
 
-            @pl.when(step == 0)
-            def _():
-                if head == 0:
-                    gather_ff.spread(1)
-                    gather_ff.forward(0)
-                elif head == 1:
-                    gather_ff.spread(3)
-                    gather_ff.across(0)
-                else:
-                    gather_ff.spread(2)
-                    gather_ff.forward(1)
-
-            @pl.when(step == 1)
-            def _():
-                if head == 0:
-                    gather_ff.forward(3)
-                    gather_ff.across(1)
-                elif head == 1:
-                    gather_ff.forward(2)
-                    gather_ff.across(3)
-                else:
-                    gather_ff.across(2)
-
-        attention_chunk(
-            weights, gains[...], x_ref, dy_ref, xt, dt, feat_q, feat_k,
-            raw, d_raw, d_att, att, d_normed, branch, g_gains, store, poll,
+            for which in range(count):
+                @pl.when(step == which)
+                def _():
+                    events(which, head)
+
+        backward_chunk(
+            weights_of(chunk), gains[...], dy_ref, xt, dt, raw, d_raw, d_score,
+            qk_all.at[chunk], v_all.at[chunk], stats.at[chunk], att.at[chunk], total, g_gains,
+            ready, store, poll,
         )
 
         @pl.when(step < count - 1)
@@ -858,25 +1063,59 @@
 
         return carry
 
-    lax.fori_loop(0, count, one_step, 0)
-    take_back((out0, out1, out2, out3), pt, x_ref, norm_gain, d_normed, branch, g_gains)
+    lax.fori_loop(0, count, backward_step, 0)
+    store_gain(g_gains, total[...], x_ref[...], norm_gain[...])
+    value = total[...].astype(BF16)
+    for k, out in enumerate((out0, out1, out2, out3)):
+        out[...] = nn(pt[k], value).astype(BF16)
     g_last[...] = g_buf[count - 1:]
-    total = 0.0
+    z_total = 0.0
     for step in range(count - 1):
         z_copy(step).wait_recv()
-        total = total + got_z[step].astype(F32)
-    z_attn[...] = total
+        z_total = z_total + got_z[step].astype(F32)
+    z_attn[...] = z_total
     for k in range(count):
         gather_ff.last(k)
+    for k in range(1, count):
+        back_copy(k).wait_recv()
 
     gather.wait_send()
     gather_ff.wait_send()
     for k in range(1, count):
+        back_copy(k).wait_send()
         for kind in range(2):
             row_copy(kind, k).wait_send()
     for step in range(count - 1):
         scatter.wait_send(step)
         z_copy(step).wait_send()
+
+
+def place_rows(me, part, ids, pt, feat_q, feat_k):
+    mp = ids.shape[1]
+    total = mp * part
+    numbers = ids[me]
+    start = jnp.zeros((1, 1), jnp.int32)
+    for image in range(IMAGES):
+        count = jnp.sum((numbers == image).astype(F32), axis=(0, 1), keepdims=True)
+        ahead = jnp.sum(
+            ((numbers >= 0) & (numbers < image)).astype(F32), axis=(0, 1), keepdims=True
+        )
+        start = start + jnp.where(count == MOST, ahead, 0.0).astype(jnp.int32)
+    line = source_of(iota((1, ROWS), 1), start, total)
+    feats = 0.0
+    for k in range(mp):
+        chunk = lax.rem(me - k + mp, mp)
+        offset = iota((PIECE, 1), 0)
+        pos = jnp.where(offset < part, chunk * part + offset, -2)
+        pick = (line == pos).astype(F32).astype(BF16)
+        pt[k] = pick
+        marks = (iota((128, 1), 0) - HD == ids[me, pl.ds(chunk, 1), :]).astype(F32)
+        feats = feats + nn(marks.astype(BF16), pick)
+    feats = feats.T
+    lane = iota((1, 128), 1)
+    feat_q[...] = (feats * 128.0).astype(BF16)
+    marked = (lane >= HD) & (lane < HD + IMAGES)
+    feat_k[...] = jnp.where(marked, (feats - 1.0) * 256.0, 0.0).astype(BF16)
 
 
 def front_call(tokens, cotangent, ids, gains, norm_gain, w_attn, w_feed):
@@ -888,17 +1127,19 @@
     return pl.pallas_call(
         front_kernel,
         in_specs=[vmem] * 6 + [hbm],
-        out_specs=[vmem] * 6 + [hbm] + [vmem] * 3,
-        out_shape=[rows, rows]
-        + [jax.ShapeDtypeStruct((2, PIECE, width), BF16)] * 4
+        out_specs=[vmem] * 7 + [hbm] + [vmem] * 3 + [hbm],
+        out_shape=[rows, rows, rows]
+        + [jax.ShapeDtypeStruct((PIECE, width), BF16)] * 4
         + [
             jax.ShapeDtypeStruct((count, 2, 2, 2, 2, shard, width), BF16),
             jax.ShapeDtypeStruct((1, 1, 2, 2, 2, shard, width), BF16),
             jax.ShapeDtypeStruct((shard, width), F32),
             jax.ShapeDtypeStruct((8, 128), F32),
+            jax.ShapeDtypeStruct((count, 3, ROWS, BIG), BF16),
         ],
         scratch_shapes=[
             pltpu.VMEM((count - 1, 2, PIECE, width), BF16),
+            pltpu.VMEM((count - 1, PIECE, width), BF16),
             pltpu.VMEM((count, 2, 2, 2, shard, width), BF16),
             pltpu.VMEM((count, 1, 2, 2, 2, shard, width), BF16),
             pltpu.VMEM((count - 1, 1, 2, 2, shard, width), BF16),
@@ -914,42 +1155,49 @@
             pltpu.VMEM((count, PIECE, ROWS), BF16),
             pltpu.VMEM((ROWS, 640), F32),
             pltpu.VMEM((ROWS, 640), BF16),
-            pltpu.VMEM((ROWS, 256), F32),
-            pltpu.VMEM((ROWS, 256), BF16),
-            pltpu.VMEM((ROWS, width), F32),
+            pltpu.VMEM((ROWS, BIG), BF16),
+            pltpu.VMEM((2, ROWS, BIG), BF16),
+            pltpu.VMEM((count, 3, ROWS, 128), BF16),
+            pltpu.VMEM((count, 3, ROWS, 128), BF16),
+            pltpu.VMEM((count, ROWS, 128), F32),
+            pltpu.VMEM((count, ROWS, 256), BF16),
             pltpu.VMEM((ROWS, width), F32),
             pltpu.SemaphoreType.DMA((2, count - 1)),
             pltpu.SemaphoreType.DMA((2, count - 1)),
+            pltpu.SemaphoreType.DMA((count - 1,)),
+            pltpu.SemaphoreType.DMA((count - 1,)),
             pltpu.SemaphoreType.DMA((8, count)),
             pltpu.SemaphoreType.DMA((8, count)),
             pltpu.SemaphoreType.DMA((8, count)),
             pltpu.SemaphoreType.DMA((8, count)),
             pltpu.SemaphoreType.DMA,
+            pltpu.SemaphoreType.DMA((2,)),
+            pltpu.SemaphoreType.DMA((2,)),
             pltpu.SemaphoreType.DMA((3, 2, count - 1)),
             pltpu.SemaphoreType.DMA((3, 2, count - 1)),
             pltpu.SemaphoreType.DMA((count - 1,)),
             pltpu.SemaphoreType.DMA((count - 1,)),
         ],
         compiler_params=pltpu.CompilerParams(
-            collective_id=1, has_side_effects=True, vmem_limit_bytes=VMEM
+            collective_id=1, has_side_effects=True, vmem_limit_bytes=FRONT_VMEM
         ),
         name="front",
     )(tokens, cotangent, ids, gains, norm_gain, w_attn, w_feed)
 
 
 def finish_kernel(
-    place, tok, cot, gain, branch, d_ff, ret0, ret1, ret2, ret3, output, input_grad
+    place, tok, cot, gain, branch, d_ff, back, ret0, ret1, ret2, ret3, output, input_grad
 ):
     step = pl.program_id(0)
     part = tok.shape[1]
 
-    for index, back in enumerate((ret0, ret1, ret2, ret3)):
+    for index, ret in enumerate((ret0, ret1, ret2, ret3)):
 
         @pl.when(step == index)
         def _():
             x = tok[0].astype(F32)
-            output[0] = (x + (branch[0] + back[1].astype(F32))[:part]).astype(BF16)
-            d_normed = (d_ff[0] + back[0].astype(F32))[:part]
+            output[0] = (x + (branch[0] + back[0].astype(F32))[:part]).astype(BF16)
+            d_normed = (d_ff[0] + ret[...].astype(F32))[:part]
             centered = x - jnp.mean(x, axis=-1, keepdims=True)
             spread = lax.rsqrt(jnp.mean(centered * centered, axis=-1, keepdims=True) + 1e-6)
             unit = centered * spread
@@ -962,20 +1210,20 @@
             input_grad[0] = cot[0].astype(F32) + d_x
 
 
-def finish_call(place, tokens, cotangent, gain, branch, d_ff, returned):
+def finish_call(place, tokens, cotangent, gain, branch, d_ff, back, returned):
     count, part, width = tokens.shape
     block = pl.BlockSpec(
         (1, part, width), lambda k, place: (lax.rem(place[0] + k, count), 0, 0)
     )
     padded = pl.BlockSpec((1, PIECE, width), lambda k, place: (k, 0, 0))
-    pair = pl.BlockSpec((2, PIECE, width), lambda k, place: (0, 0, 0))
+    piece = pl.BlockSpec((PIECE, width), lambda k, place: (0, 0))
     line = pl.BlockSpec((1, width), lambda k, place: (0, 0))
     return pl.pallas_call(
         finish_kernel,
         grid_spec=pltpu.PrefetchScalarGridSpec(
             num_scalar_prefetch=1,
             grid=(count,),
-            in_specs=[block, block, line, padded, padded] + [pair] * 4,
+            in_specs=[block, block, line, padded, padded, padded] + [piece] * 4,
             out_specs=[block, block],
         ),
         out_shape=[
@@ -984,7 +1232,7 @@
         ],
         compiler_params=pltpu.CompilerParams(vmem_limit_bytes=VMEM),
         name="finish",
-    )(place, tokens, cotangent, gain, branch, d_ff, *returned)
+    )(place, tokens, cotangent, gain, branch, d_ff, back, *returned)
 
 
 def pack_attention(w_qkv, w_proj):
@@ -1028,7 +1276,7 @@
         ]
 
     if (dp, mp) == (8, 4):
-        normed, grads, *outs, w_ff, g_attn, z_attn, g_gains = front_call(
+        normed, grads, back, *outs, w_ff, g_attn, z_attn, g_gains, _ = front_call(
             tok, cot, ids, gains, gain, w_attn, w_ff
         )
         returned = send_back(outs)
@@ -1047,7 +1295,9 @@
         *outs, g_attn, g_gains = attention_call(
             place, part, normed, grads, received, ids, gains, gain, w_attn
         )
-        returned = send_back(outs)
+        outs = send_back(outs)
+        back = jnp.stack([out[1] for out in outs])
+        returned = [out[0] for out in outs]
         flat_normed = normed.reshape(count * PIECE, width)
         branch, d_ff, g_up, g_down = feed_call(
             flat_normed, grads.reshape(count * PIECE, width),
@@ -1064,7 +1314,7 @@
         g_gains = lax.psum(g_gains, both)
     output, input_grad = finish_call(
         place, tok, cot, gain,
-        branch.reshape(count, PIECE, width), d_ff.reshape(count, PIECE, width), returned,
+        branch.reshape(count, PIECE, width), d_ff.reshape(count, PIECE, width), back, returned,
     )
     g_qkv, g_proj = unpack_attention(g_attn, w_qkv.shape[2])
     g_norm = g_gains[:width // 128].reshape(width)

time: 334 us -> 305 us (0.913)
  Pallas kernels: 304 us -> 273 us
    pallas_call x1, Pallas kernels: 90.9 us -> 75.4 us  [feed_remote_call(): pl.pallas_call(feed_remote_kernel, in_specs=[vmem, vmem, pl.BlockSpec(mem...]
    pallas_call x1, Pallas kernels: 205 us -> 189 us  [front_call(): pl.pallas_call(front_kernel, in_specs=[vmem] * 6 + [hbm], out_specs=[vmem...]
  transfers between devices with their start and end apart: 3 -> 3, of which waited for: 0 -> 0; matrix products, arithmetic and copies ran while one was open for 2% -> 2% of each run, Pallas kernels for 27% -> 25%
where the time goes in v5:
time: 305 us; the launch traced here: 306 us
  Pallas kernels  273 us (90%)
  local copies, waits for them, and re-layouts  22.7 us (7%)
  starting transfers between devices  6.51 us (2%)
    pallas_call x1, Pallas kernels, front_call(): pl.pallas_call(front_kernel, in_specs=[vmem] * 6 + [hbm], out_specs=[vmem...  189 us
    pallas_call x1, Pallas kernels, feed_remote_call(): pl.pallas_call(feed_remote_kernel, in_specs=[vmem, vmem, pl.BlockSpec(mem...  75.4 us
    unnamed x38, local copies, waits for them, and re-layouts  16.3 us
    pallas_call x1, Pallas kernels, finish_call(): pl.pallas_call(finish_kernel, grid_spec=pltpu.PrefetchScalarGridSpec(num_...  8.22 us
    ppermute x3, starting transfers between devices, send_back(): lax.ppermute(out, 'mp', [(i, (i - k) % mp) for i in range(mp)])  6.51 us
  transfers between devices with their start and end apart: 3, of which 0 were waited for; matrix products, arithmetic and copies ran while one was open for 2% of the time, Pallas kernels for 25%

profile of v5, /device:TPU:0, one launch (start us, length us, event | category | flops | bytes accessed | tf_op | source)
XLA Modules:
  0.0 305.5 jit_solution(6678764364179447058)
XLA Ops:
  0.6 0.8 slice_bitcast_fusion.2
  1.4 0.0 copy-start.1
  1.4 1.4 reshape.73.norm_gain.gain
  2.8 2.7 copy.27
  5.5 0.0 copy-done.1
  5.5 0.0 slice-start
  5.5 0.0 copy-start.9
  5.5 0.0 copy-start.10
  5.5 0.0 copy-start.7
  5.5 0.0 copy-start.8
  5.5 0.0 copy-start.12
  5.6 0.0 copy-start.13
  5.6 1.4 copy.28
  6.9 0.0 slice-done
  6.9 0.1 copy.40
  7.1 0.1 copy.32
  7.2 0.0 copy-done.9
  7.2 0.1 copy.31
  7.3 0.0 copy-done.10
  7.3 0.1 reshape.74
  7.4 0.0 copy-done.7
  7.4 0.0 copy-done.8
  7.4 0.7 pad_maximum_fusion.w_feed
  8.2 0.6 pad.4.ids
  8.8 0.0 copy-done.12
  8.8 0.0 copy-done.13
  8.8 0.6 maximum_bitcast_fusion.gains
  9.4 0.7 pad_maximum_fusion.2.w_attn
  10.1 189.5 %front.1 = (bf16[4,240,768]{2,1,0:T(8,128)(2,1)}, bf16[4,240,768]{2,1,0:T(8,128)(2,1)}, bf16[4,240,768]{2,1,0:T(8,128)(2,1)}, bf16[240,768]{1,0:T(8,128)(2,1)}, ...) custom-call(bf16[4,236,768]{2,1,0:T(8,128)(2,1)} %bitcast.38, ...), custom_call_target="tpu_custom_call" | custom-call | tf_op jit(solution)/shard_map/front/pallas_call | solution.py:1127
  199.6 5.9 %collective-permute-start = (bf16[240,768]{1,0:T(8,128)(2,1)}, bf16[240,768]{1,0:T(8,128)(2,1)S(1)}, u32[]{:S(2)}, u32[]{:S(2)}) collective-permute-start(bf16[240,768]{1,0:T(8,128)(2,1)} %get-tuple-element.38), channel_id=1, source_target_pairs={{0,3},{1,0},{2,1},{3,2},{4,7},{5,4},{6,5},{7,6},{8,11},{9,8},{10,9... | collective-permute-start | bytes 1105928 | tf_op jit(solution)/shard_map/ppermute | solution.py:1274
  205.5 0.0 collective-permute-start.1
  205.5 0.6 collective-permute-start.2
  206.1 75.4 %feed_forward_scatter.1 = (f32[960,768]{1,0:T(8,128)}, f32[960,768]{1,0:T(8,128)}, f32[96,768]{1,0:T(8,128)}, f32[96,768]{1,0:T(8,128)}, f32[96,768]{1,0:T(8,128)}, /*index=5*/f32[8,128]{1,0:T(8,128)}) custom-call(bf16[960,768]{1,0:T(8,128)(2,1)} %bitcast.55, bf16[960,768]{1,0:T(8,128)(2,1)} %bitcast.56, bf16[4,8,2,96,768]{4,3,2,1,0:T(8,128)(2,1)} %bitcast.54, ...), custom_call_target="tpu_custom_call" | custom-call | flops 27179089920 | bytes 18874368 | tf_op jit(solution)/shard_map/feed_forward_scatter/pallas_call | solution.py:458
  281.6 0.0 copy-start.11
  281.6 1.1 slice_bitcast_fusion
  282.6 0.9 slice.35
  283.6 0.1 copy.35
  283.7 0.1 copy.33
  283.8 0.9 copy.38
  284.7 0.7 copy.39
  285.5 0.0 copy-done.11
  285.5 0.6 slice_bitcast_fusion.4
  286.0 0.6 slice_bitcast_fusion.3
  286.6 0.0 collective-permute-done.ret1
  286.6 0.0 copy-start.2
  286.6 0.0 collective-permute-done.1.ret2
  286.6 0.0 copy-start.3
  286.7 0.0 collective-permute-done.2.ret3
  286.7 0.0 copy-start.4
  286.7 0.7 copy-done.2
  287.4 0.1 copy-done.3
  287.5 0.1 copy-done.4
  287.6 8.2 %finish.1 = (bf16[4,236,768]{2,1,0:T(8,128)(2,1)}, f32[4,236,768]{2,1,0:T(8,128)}) custom-call(s32[1]{0:T(128)} %bitcast.place, bf16[4,236,768]{2,1,0:T(8,128)(2,1)} %bitcast.39, bf16[4,236,768]{2,1,0:T(8,128)(2,1)} %bitcast.41, f32[1,768]{1,0:T(1,128)} %reshape.73.norm_gain.gain, f32[4,240,768]{2,1,0:T(8,128)} %bitcast.42, f32[4,240,768]{2,1,0:T(8,128)} %bitcast.43, ...), custom_call_target="tpu_custom_call" | custom-call | tf_op jit(solution)/shard_map/finish/pallas_call | solution.py:1221
  295.8 0.0 copy-start
  295.9 5.8 %copy.37 = f32[2,2,236,768]{3,1,2,0:T(2,128)} copy(f32[2,2,236,768]{3,2,1,0:T(8,128)} %bitcast.44) | data formatting | bytes 5799936
  301.6 0.0 copy-start.6
  301.6 0.0 copy-done
  301.6 0.0 copy-start.5
  301.6 2.2 copy.36
  303.8 0.0 copy-done.6
  303.8 0.7 copy.43
  304.6 0.0 copy-done.5
  304.6 0.7 copy.44
  (3 shorter events, 0.1 us)
Async XLA Ops:
  1.4 4.1 %copy-start.1 = (bf16[2,2,236,768]{3,1,2,0:T(2,128)(2,1)S(1)}, bf16[2,2,236,768]{3,1,2,0:T(2,128)(2,1)}, u32[]{:S(2)}) copy-start(bf16[2,2,236,768]{3,1,2,0:T(2,128)(2,1)} %param.19) | copy-start | bytes 4349956
  5.5 1.4 slice-start
  5.5 1.7 copy-start.9
  5.5 1.8 copy-start.10
  5.5 1.9 copy-start.7
  5.5 1.9 copy-start.8
  5.5 3.3 %copy-start.12 = (f32[64]{0:T(128)S(1)}, f32[64]{0:T(128)}, u32[]{:S(2)}) copy-start(f32[64]{0:T(128)} %param.17) | copy-start | bytes 772
  5.6 3.2 %copy-start.13 = (f32[64]{0:T(128)S(1)}, f32[64]{0:T(128)}, u32[]{:S(2)}) copy-start(f32[64]{0:T(128)} %param.16) | copy-start | bytes 772
  199.6 87.0 %collective-permute-start = (bf16[240,768]{1,0:T(8,128)(2,1)}, bf16[240,768]{1,0:T(8,128)(2,1)S(1)}, u32[]{:S(2)}, u32[]{:S(2)}) collective-permute-start(bf16[240,768]{1,0:T(8,128)(2,1)} %get-tuple-element.38), channel_id=1, source_target_pairs={{0,3},{1,0},{2,1},{3,2},{4,7},{5,4},{6,5},{7,6},{8,11},{9,8},{10,9... | collective-permute-start | bytes 1105928 | tf_op jit(solution)/shard_map/ppermute | solution.py:1274
  205.5 81.2 %collective-permute-start.1 = (bf16[240,768]{1,0:T(8,128)(2,1)}, bf16[240,768]{1,0:T(8,128)(2,1)S(1)}, u32[]{:S(2)}, u32[]{:S(2)}) collective-permute-start(bf16[240,768]{1,0:T(8,128)(2,1)} %get-tuple-element.39), channel_id=1, source_target_pairs={{0,2},{1,3},{2,0},{3,1},{4,6},{5,7},{6,4},{7,5},{8,10},{9,11},{10,... | collective-permute-start | bytes 1105928 | tf_op jit(solution)/shard_map/ppermute | solution.py:1274
  205.5 81.2 %collective-permute-start.2 = (bf16[240,768]{1,0:T(8,128)(2,1)}, bf16[240,768]{1,0:T(8,128)(2,1)S(1)}, u32[]{:S(2)}, u32[]{:S(2)}) collective-permute-start(bf16[240,768]{1,0:T(8,128)(2,1)} %get-tuple-element.40), channel_id=1, source_target_pairs={{0,1},{1,2},{2,3},{3,0},{4,5},{5,6},{6,7},{7,4},{8,9},{9,10},{10,1... | collective-permute-start | bytes 1105928 | tf_op jit(solution)/shard_map/ppermute | solution.py:1274
  281.6 3.9 %copy-start.11 = (f32[8,128]{1,0:T(8,128)S(1)}, f32[8,128]{1,0:T(8,128)}, u32[]{:S(2)}) copy-start(f32[8,128]{1,0:T(8,128)} %get-tuple-element.46) | copy-start | bytes 12292
  286.6 0.7 copy-start.2
  286.6 0.9 copy-start.3
  286.7 1.0 copy-start.4
  295.8 5.8 %copy-start = (bf16[4,236,768]{2,1,0:T(8,128)(2,1)S(1)}, bf16[4,236,768]{2,1,0:T(8,128)(2,1)}, u32[]{:S(2)}) copy-start(bf16[4,236,768]{2,1,0:T(8,128)(2,1)} %get-tuple-element.41) | copy-start | bytes 4349956
  301.6 2.2 copy-start.6
  301.6 2.9 copy-start.5

commit v6 on v5

--- a/solution.py
+++ b/solution.py
@@ -134,6 +134,11 @@
         self.beside = d + 2 - 4 * self.x
         self.above = d + 4 - 8 * self.y
 
+    def target(self, step):
+        z, high = self.z, self.z // 2
+        near = jnp.where(step == 2, 1 - z + 4 * high, z)
+        return jnp.where(step == 0, 3 - 3 * high, jnp.where(step == 1, 2 - high, near))
+
     def along(self, k):
         return lax.rem(self.z + k + self.planes, self.planes)
 
@@ -229,64 +234,148 @@
         self.at, self.shard, self.full = at, shard, full
         self.send_sem, self.recv_sem = send_sem, recv_sem
 
-    def piece(self, k, y=False, x=False, core=False):
+    def there(self, r, does):
+        plane = self.at.z + r
+
+        @pl.when((plane >= 0) & (plane < self.at.planes))
+        def _():
+            does(plane)
+
+    def piece(self, plane, y=False, x=False, core=False):
         at = self.at
-        return self.full.at[at.along(-k), 1 - at.y if y else at.y, 1 - at.x if x else at.x,
+        return self.full.at[plane, 1 - at.y if y else at.y, 1 - at.x if x else at.x,
                             1 - at.core if core else at.core]
 
-    def move(self, kind, k, src, **to):
-        sem = (kind, k)
-        self.at.copy(src, src, self.send_sem.at[sem], self.recv_sem.at[sem], **to).start()
-
-    def arrived(self, kind, k, ref):
-        sem = (kind, k)
-        self.at.copy(ref, ref, self.send_sem.at[sem], self.recv_sem.at[sem],
-                     dp=self.at.sibling).wait_recv()
+    def copy(self, kind, plane, src, dst=None, **to):
+        return self.at.copy(
+            src, src if dst is None else dst, self.send_sem.at[kind, plane],
+            self.recv_sem.at[kind % 8, plane], **to
+        )
+
+    def arrived(self, kind, plane, ref):
+        self.copy(kind, plane, ref, dp=self.at.sibling).wait_recv()
+
+    def pass_on(self, kind, plane, src, act):
+        z, dst = self.at.z, self.piece(plane)
+        if kind == 0:
+            @pl.when(z < self.at.planes - 1)
+            def _():
+                act(self.copy(0, plane, src, dst, mp=z + 1))
+        else:
+            @pl.when(z > 0)
+            def _():
+                act(self.copy(8, plane, src, dst, mp=z - 1))
 
     def start(self):
-        for k in range(1, self.at.planes):
-            sem = (0, k)
-            self.at.copy(self.shard, self.piece(0), self.send_sem.at[sem], self.recv_sem.at[sem],
-                         mp=self.at.along(k)).start()
-
-    def spread(self, k):
+        for kind in (0, 8):
+            self.pass_on(kind, self.at.z, self.shard, lambda copy: copy.start())
+
+    def spread(self, *which):
+        for r in which:
+            def does(plane):
+                src = self.piece(plane)
+                if r:
+                    self.arrived(0, plane, src)
+                    self.pass_on(0 if r < 0 else 8, plane, src, lambda copy: copy.start())
+                self.copy(1, plane, src, dp=self.at.beside).start()
+                self.copy(2, plane, src, dp=self.at.above).start()
+                self.copy(3, plane, src, dp=self.at.sibling).start()
+
+            self.there(r, does)
+
+    def forward(self, *which):
         at = self.at
-        src = self.piece(k)
-        if k:
-            self.arrived(0, k, src)
-        self.move(1, k, src, dp=at.beside)
-        self.move(2, k, src, dp=at.above)
-        self.move(3, k, src, dp=at.sibling)
-
-    def forward(self, k):
-        at = self.at
-        from_x, from_y = self.piece(k, x=True), self.piece(k, y=True)
-        self.arrived(1, k, from_x)
-        if k % 2 == 0:
-            self.move(5, k, from_x, dp=at.above)
-        self.move(4, k, from_x, dp=at.sibling)
-        self.arrived(2, k, from_y)
-        if k % 2 == 1:
-            self.move(5, k, from_y, dp=at.beside)
-        self.move(6, k, from_y, dp=at.sibling)
-
-    def across(self, k):
-        src = self.piece(k, y=True, x=True)
-        self.arrived(5, k, src)
-        self.move(7, k, src, dp=self.at.sibling)
-
-    def last(self, k):
-        self.arrived(3, k, self.piece(k, core=True))
-        self.arrived(4, k, self.piece(k, x=True, core=True))
-        self.arrived(6, k, self.piece(k, y=True, core=True))
-        self.arrived(7, k, self.piece(k, y=True, x=True, core=True))
+        for r in which:
+            def does(plane):
+                from_x, from_y = self.piece(plane, x=True), self.piece(plane, y=True)
+                self.arrived(1, plane, from_x)
+                if r % 2 == 0:
+                    self.copy(5, plane, from_x, dp=at.above).start()
+                self.copy(4, plane, from_x, dp=at.sibling).start()
+                self.arrived(2, plane, from_y)
+                if r % 2 == 1:
+                    self.copy(5, plane, from_y, dp=at.beside).start()
+                self.copy(6, plane, from_y, dp=at.sibling).start()
+
+            self.there(r, does)
+
+    def across(self, *which):
+        for r in which:
+            def does(plane):
+                src = self.piece(plane, y=True, x=True)
+                self.arrived(5, plane, src)
+                self.copy(7, plane, src, dp=self.at.sibling).start()
+
+            self.there(r, does)
+
+    def last(self):
+        for plane in range(self.at.planes):
+            self.arrived(3, plane, self.piece(plane, core=True))
+            self.arrived(4, plane, self.piece(plane, x=True, core=True))
+            self.arrived(6, plane, self.piece(plane, y=True, core=True))
+            self.arrived(7, plane, self.piece(plane, y=True, x=True, core=True))
 
     def wait_send(self):
-        for k in range(self.at.planes):
-            for kind in range(0 if k else 1, 8):
-                sem = (kind, k)
-                self.at.copy(self.piece(k), self.piece(k), self.send_sem.at[sem],
-                             self.recv_sem.at[sem], dp=self.at.sibling).wait_send()
+        for r in range(1 - self.at.planes, self.at.planes):
+            def does(plane):
+                src = self.piece(plane)
+                if r <= 0:
+                    self.pass_on(0, plane, src, lambda copy: copy.wait_send())
+                if r >= 0:
+                    self.pass_on(8, plane, src, lambda copy: copy.wait_send())
+                for kind in range(1, 8):
+                    self.copy(kind, plane, src, dp=self.at.sibling).wait_send()
+
+            self.there(r, does)
+
+
+class Along:
+    def __init__(self, at, parts, got, send_sem, recv_sem):
+        self.at, self.parts, self.got = at, parts, got
+        self.send_sem, self.recv_sem = send_sem, recv_sem
+        self.inner = (at.z == 1) | (at.z == 2)
+
+    def copy(self, step, kind):
+        at, inner = self.at, self.inner
+        side = 1 - 2 * (at.z // 2)
+        to = at.z + jnp.where(inner & (step == 2), -side, side)
+        slot = jnp.where(inner, 2 + 2 * step - 3 * (step // 2), step + step // 2)
+        return at.copy(self.parts.at[step, kind], self.got.at[kind, slot],
+                       self.send_sem.at[kind, step], self.recv_sem.at[kind, slot], mp=to)
+
+    def arrived(self, kind, slot):
+        ref = self.got.at[kind, slot]
+        self.at.copy(ref, ref, self.send_sem.at[kind, 0], self.recv_sem.at[kind, slot],
+                     mp=self.at.along(1)).wait_recv()
+
+    def send_outer(self, step):
+        @pl.when(jnp.logical_not(self.inner))
+        def _():
+            for kind in range(self.got.shape[0]):
+                self.copy(step, kind).start()
+
+    def send_inner(self, step):
+        @pl.when(self.inner)
+        def _():
+            for kind in range(self.got.shape[0]):
+                self.arrived(kind, step)
+                own = self.parts[step, kind].astype(F32)
+                total = own + self.got[kind, step].astype(F32)
+                self.parts[step, kind] = total.astype(BF16)
+                self.copy(step, kind).start()
+
+    def add(self, kind, out):
+        self.arrived(kind, 3)
+        out[...] += self.got[kind, 3].astype(F32)
+
+        @pl.when(self.inner)
+        def _():
+            self.arrived(kind, 4)
+            out[...] += self.got[kind, 4].astype(F32)
+
+    def wait_send(self, step):
+        for kind in range(self.got.shape[0]):
+            self.copy(step, kind).wait_send()
 
 
 def gelu_parts(up):
@@ -318,21 +407,13 @@
     attn = Scatter(at, halves(width), g_attn, at_core, at_first, at_second, at_send, at_recv)
     both = (0, slice(0, width), True), (1, slice(0, width), False)
     feed = Scatter(at, both, g_ff, ff_core, ff_first, ff_second, ff_send, ff_recv)
+    along = Along(at, ff_second, got_z, z_send, z_recv)
     last = steps - 1
-
-    def z_copy(step, kind):
-        return at.copy(ff_second.at[step, kind], got_z.at[kind, step],
-                       z_send.at[kind, step], z_recv.at[kind, step], mp=at.along(1 + step))
-
-    def to_z(step):
-        feed.after_second(step)
-        for kind in range(2):
-            z_copy(step, kind).start()
 
     def w_copy(step, kind):
         slot = lax.rem(step, 2)
         return pltpu.make_async_copy(
-            w_hbm.at[at.along(1 + step), :, kind], w_buf.at[slot, kind], w_sem.at[slot, kind]
+            w_hbm.at[at.target(step), :, kind], w_buf.at[slot, kind], w_sem.at[slot, kind]
         )
 
     def feed_half(step, index):
@@ -378,10 +459,15 @@
 
         @pl.when(step >= 2)
         def _():
-            to_z(step - 2)
+            feed.after_second(step - 2)
+            along.send_outer(step - 2)
 
         feed_half(step, 1)
         feed.start(step)
+
+        @pl.when(step >= 2)
+        def _():
+            along.send_inner(step - 2)
 
         @pl.when(step == 0)
         def _():
@@ -415,7 +501,9 @@
     feed.after_core(last)
     next_sum(0)
     sum_copy(1).start()
-    to_z(last - 1)
+    feed.after_second(last - 1)
+    along.send_outer(last - 1)
+    along.send_inner(last - 1)
     next_sum(1)
     sum_copy(2).start()
     for item in range(2):
@@ -427,11 +515,8 @@
         sum_z_copy(k).start()
     z_sums[at.z] = sums[3]
     for kind, out in enumerate((out_up, out_down)):
-        total = feed.total(last, kind)
-        for step in range(last):
-            z_copy(step, kind).wait_recv()
-            total = total + got_z[kind, step].astype(F32)
-        out[...] = total
+        out[...] = feed.total(last, kind)
+        along.add(kind, out)
     for k in range(1, steps):
         sum_z_copy(k).wait_recv()
     total = z_sums[0]
@@ -443,8 +528,7 @@
     for step in range(steps):
         feed.wait_send(step)
     for step in range(last):
-        for kind in range(2):
-            z_copy(step, kind).wait_send()
+        along.wait_send(step)
     for stage in range(3):
         sum_copy(stage).wait_send()
     for k in range(1, steps):
@@ -473,7 +557,7 @@
             pltpu.VMEM((1, 1, 2, 2, shard, width), BF16),
             pltpu.VMEM((1, 1, 2, shard, width), BF16),
             pltpu.VMEM((1, 1, shard, width), BF16),
-            pltpu.VMEM((2, steps - 1, shard, width), BF16),
+            pltpu.VMEM((2, 5, shard, width), BF16),
             pltpu.VMEM((4, 8, 128), F32),
             pltpu.VMEM((3, 8, 128), F32),
             pltpu.VMEM((steps, 8, 128), F32),
@@ -483,7 +567,7 @@
             pltpu.SemaphoreType.DMA((3, 2, 1)),
             pltpu.SemaphoreType.DMA((3, 2, 1)),
             pltpu.SemaphoreType.DMA((2, steps - 1)),
-            pltpu.SemaphoreType.DMA((2, steps - 1)),
+            pltpu.SemaphoreType.DMA((2, 5)),
             pltpu.SemaphoreType.DMA((6,)),
             pltpu.SemaphoreType.DMA((6,)),
         ],
@@ -791,7 +875,7 @@
 
 
 def backward_chunk(
-    weights, gain, dy_ref, xt, dt, raw, d_raw, d_score_ref, qk_all, v_all, stats, att,
+    weights, gain, dy_ref, xt, dt, raw, d_raw, qk_all, v_all, stats, att,
     d_normed, g_gains, ready, store, poll,
 ):
     raw[:, :256] = nn(dy_ref[...], weights(slice(512, 768)))
@@ -825,14 +909,14 @@
         d_queries, d_keys, d_values = [], [], []
         for base, count in ((0, BIG), (BIG, REST)):
             block = slice(base, base + count)
+            d_values.append(nn(d_t[:, block], p_ref[block, :count]).T)
             for row in range(base, base + count, 256):
                 rows = slice(row, row + 256)
                 d_prob = nt(d_low[rows], v_aug[block])
                 d_score = (p_ref[rows, :count].astype(F32) * d_prob).astype(BF16)
-                d_score_ref[rows, :count] = d_score
+                p_ref[rows, :count] = d_score
                 d_queries.append(nn(d_score, qk[block]))
-            d_keys.append(nn(qk_t[:, block], d_score_ref[block, :count]).T)
-            d_values.append(nn(d_t[:, block], p_ref[block, :count]).T)
+            d_keys.append(nn(qk_t[:, block], p_ref[block, :count]).T)
         d_query = jnp.concatenate(d_queries, axis=0)
         d_key = jnp.concatenate(d_keys, axis=0)
         d_value = jnp.concatenate(d_values, axis=0)
@@ -865,8 +949,8 @@
 def front_kernel(
     tok, cot, ids, gains, norm_gain, w_attn, w_feed,
     normed, grads, returned, out0, out1, out2, out3, w_ff, g_last, z_attn, g_gains, p_all,
-    got_rows, back_rows, w_full, g_buf, at_core, at_first, at_second, got_z,
-    x_ref, dy_ref, xt, dt, feat_q, feat_k, pt, raw, d_raw, d_score, p_buf,
+    got_rows, w_full, g_buf, at_core, at_first, at_second, got_z,
+    x_ref, dy_ref, xt, dt, feat_q, feat_k, pt, raw, d_raw, p_buf,
     qk_all, v_all, stats, att, total,
     row_send, row_recv, back_send, back_recv, wa_send, wa_recv, wf_send, wf_recv, own_sem,
     p_out, p_in, at_send, at_recv, z_send, z_recv,
@@ -878,7 +962,8 @@
     gather = Gather(at, w_attn, w_full, wa_send, wa_recv)
     gather_ff = Gather(at, w_feed, w_ff, wf_send, wf_recv)
     scatter = Scatter(at, halves(width), g_buf, at_core, at_first, at_second, at_send, at_recv)
-    own_ff = pltpu.make_async_copy(w_feed, gather_ff.piece(0), own_sem)
+    own_ff = pltpu.make_async_copy(w_feed, gather_ff.piece(at.z), own_sem)
+    along = Along(at, at_second, got_z, z_send, z_recv)
 
     def row_copy(kind, k):
         src = (normed, grads)[kind].at[k]
@@ -886,7 +971,7 @@
                        row_recv.at[kind, k - 1], mp=at.along(k))
 
     def back_copy(k):
-        return at.copy(back_rows.at[k - 1], returned.at[k], back_send.at[k - 1],
+        return at.copy(got_rows.at[k - 1, 0], returned.at[k], back_send.at[k - 1],
                        back_recv.at[k - 1], mp=at.along(-k))
 
     gather.start()
@@ -909,21 +994,20 @@
     place_rows(at.z, part, ids, pt, feat_q, feat_k)
     g_gains[...] = jnp.zeros_like(g_gains)
     total[...] = jnp.zeros_like(total)
-    gather.spread(1)
-    gather.spread(3)
+    gather.spread(-1, 1)
     gather.forward(0)
-    gather.spread(2)
+    gather.spread(-2, 2)
     own_ff.wait()
+    gather.forward(-1, 1)
+    gather.across(0)
+    gather.spread(-3, 3)
     gather_ff.spread(0)
-    gather.forward(1)
-    gather.across(0)
-    gather.forward(3)
-    gather.across(1)
-    gather.forward(2)
-    gather.across(3)
-    gather.across(2)
-    for k in range(count):
-        gather.last(k)
+    gather.forward(-2, 2)
+    gather.across(-1, 1)
+    gather.forward(-3, 3)
+    gather.across(-2, 2)
+    gather.across(-3, 3)
+    gather.last()
     for k in (1, 3, 2):
         row_copy(0, k).wait_recv()
     for k in (1, 3, 2):
@@ -955,7 +1039,7 @@
 
     def p_read(step, head):
         slot = lax.rem(step + head, 2)
-        return pltpu.make_async_copy(p_all.at[at.along(1 + step), head], p_buf.at[slot],
+        return pltpu.make_async_copy(p_all.at[at.target(step), head], p_buf.at[slot],
                                      p_in.at[slot])
 
     def forward_step(step, carry):
@@ -984,46 +1068,53 @@
     value = total[...].astype(BF16)
     returned[0] = nn(pt[0], value).astype(BF16)
     for k in range(1, count):
-        back_rows[k - 1] = nn(pt[k], value).astype(BF16)
+        got_rows[k - 1, 0] = nn(pt[k], value).astype(BF16)
     total[...] = jnp.zeros_like(total)
     for k in (1, 3, 2):
         row_copy(1, k).wait_recv()
     gather_ff.start()
     lay_out(1, grads, dy_ref, dt)
 
-    def z_copy(step):
-        return at.copy(at_second.at[step, 0], got_z.at[step], z_send.at[step], z_recv.at[step],
-                       mp=at.along(1 + step))
-
     def events(step, head):
         if step == 0 and head == 1:
+            gather_ff.spread(-1, 1)
+        elif step == 0 and head == 2:
             gather_ff.forward(0)
-        elif step == 0 and head == 2:
-            gather_ff.across(0)
+            gather_ff.spread(-2, 2)
         elif step == 1 and head == 0:
             for k in (1, 3, 2):
                 back_copy(k).start()
-            gather_ff.spread(1)
+            gather_ff.spread(-3, 3)
+            gather_ff.across(0)
         elif step == 1 and head == 1:
-            gather_ff.spread(3)
+            gather_ff.forward(-1, 1)
         elif step == 1 and head == 2:
-            gather_ff.spread(2)
-            gather_ff.forward(1)
+            gather_ff.forward(-2, 2)
         elif step == 2 and head == 0:
-            gather_ff.forward(3)
-            gather_ff.across(1)
+            gather_ff.across(-1, 1)
+            gather_ff.forward(-3, 3)
         elif step == 2 and head == 1:
-            gather_ff.forward(2)
-            gather_ff.across(3)
+            gather_ff.across(-2, 2)
         elif step == 2 and head == 2:
-            gather_ff.across(2)
+            gather_ff.across(-3, 3)
+            along.send_inner(0)
+        elif step == 3 and head == 1:
+            along.send_inner(1)
 
     def backward_step(step, carry):
-        chunk = at.along(1 + step)
+        chunk = at.target(step)
 
         def store(cols, value):
             split = (2, 2, 2, shard, cols.stop - cols.start)
-            g_buf[step, 0, :, :, :, :, cols] = value.reshape(split)
+            value = value.reshape(split)
+
+            @pl.when(step < count - 1)
+            def _():
+                g_buf[step, 0, :, :, :, :, cols] = value
+
+            @pl.when(step == count - 1)
+            def _():
+                g_last[0, 0, :, :, :, :, cols] = value
 
         def ready(head):
             p_read(step, head).wait()
@@ -1044,7 +1135,7 @@
                     scatter.after_first(step - 1)
                 else:
                     scatter.after_second(step - 1)
-                    z_copy(step - 1).start()
+                    along.send_outer(step - 1)
 
             for which in range(count):
                 @pl.when(step == which)
@@ -1052,7 +1143,7 @@
                     events(which, head)
 
         backward_chunk(
-            weights_of(chunk), gains[...], dy_ref, xt, dt, raw, d_raw, d_score,
+            weights_of(chunk), gains[...], dy_ref, xt, dt, raw, d_raw,
             qk_all.at[chunk], v_all.at[chunk], stats.at[chunk], att.at[chunk], total, g_gains,
             ready, store, poll,
         )
@@ -1068,16 +1159,12 @@
     value = total[...].astype(BF16)
     for k, out in enumerate((out0, out1, out2, out3)):
         out[...] = nn(pt[k], value).astype(BF16)
-    g_last[...] = g_buf[count - 1:]
-    z_total = 0.0
-    for step in range(count - 1):
-        z_copy(step).wait_recv()
-        z_total = z_total + got_z[step].astype(F32)
-    z_attn[...] = z_total
-    for k in range(count):
-        gather_ff.last(k)
+    along.send_inner(count - 2)
+    z_attn[...] = jnp.zeros_like(z_attn)
+    gather_ff.last()
     for k in range(1, count):
         back_copy(k).wait_recv()
+    along.add(0, z_attn)
 
     gather.wait_send()
     gather_ff.wait_send()
@@ -1087,7 +1174,7 @@
             row_copy(kind, k).wait_send()
     for step in range(count - 1):
         scatter.wait_send(step)
-        z_copy(step).wait_send()
+        along.wait_send(step)
 
 
 def place_rows(me, part, ids, pt, feat_q, feat_k):
@@ -1139,13 +1226,12 @@
         ],
         scratch_shapes=[
             pltpu.VMEM((count - 1, 2, PIECE, width), BF16),
-            pltpu.VMEM((count - 1, PIECE, width), BF16),
             pltpu.VMEM((count, 2, 2, 2, shard, width), BF16),
-            pltpu.VMEM((count, 1, 2, 2, 2, shard, width), BF16),
+            pltpu.VMEM((count - 1, 1, 2, 2, 2, shard, width), BF16),
             pltpu.VMEM((count - 1, 1, 2, 2, shard, width), BF16),
             pltpu.VMEM((count - 1, 1, 2, shard, width), BF16),
             pltpu.VMEM((count - 1, 1, shard, width), BF16),
-            pltpu.VMEM((count - 1, shard, width), BF16),
+            pltpu.VMEM((1, 5, shard, width), BF16),
             pltpu.VMEM((ROWS, width), BF16),
             pltpu.VMEM((ROWS, width), BF16),
             pltpu.VMEM((width, ROWS), BF16),
@@ -1155,7 +1241,6 @@
             pltpu.VMEM((count, PIECE, ROWS), BF16),
             pltpu.VMEM((ROWS, 640), F32),
             pltpu.VMEM((ROWS, 640), BF16),
-            pltpu.VMEM((ROWS, BIG), BF16),
             pltpu.VMEM((2, ROWS, BIG), BF16),
             pltpu.VMEM((count, 3, ROWS, 128), BF16),
             pltpu.VMEM((count, 3, ROWS, 128), BF16),
@@ -1166,17 +1251,17 @@
             pltpu.SemaphoreType.DMA((2, count - 1)),
             pltpu.SemaphoreType.DMA((count - 1,)),
             pltpu.SemaphoreType.DMA((count - 1,)),
+            pltpu.SemaphoreType.DMA((9, count)),
             pltpu.SemaphoreType.DMA((8, count)),
-            pltpu.SemaphoreType.DMA((8, count)),
-            pltpu.SemaphoreType.DMA((8, count)),
+            pltpu.SemaphoreType.DMA((9, count)),
             pltpu.SemaphoreType.DMA((8, count)),
             pltpu.SemaphoreType.DMA,
             pltpu.SemaphoreType.DMA((2,)),
             pltpu.SemaphoreType.DMA((2,)),
             pltpu.SemaphoreType.DMA((3, 2, count - 1)),
             pltpu.SemaphoreType.DMA((3, 2, count - 1)),
-            pltpu.SemaphoreType.DMA((count - 1,)),
-            pltpu.SemaphoreType.DMA((count - 1,)),
+            pltpu.SemaphoreType.DMA((1, count - 1)),
+            pltpu.SemaphoreType.DMA((1, 5)),
         ],
         compiler_params=pltpu.CompilerParams(
             collective_id=1, has_side_effects=True, vmem_limit_bytes=FRONT_VMEM

time: 305 us -> 308 us (level)
  Pallas kernels: 273 us -> 281 us
  starting transfers between devices: 6.51 us -> 2.07 us
    pallas_call x1, Pallas kernels: 189 us -> 199 us  [front_call(): pl.pallas_call(front_kernel, in_specs=[vmem] * 6 + [hbm], out_specs=[vmem...]
    ppermute x3, starting transfers between devices: 6.51 us -> 2.07 us  [send_back(): lax.ppermute(out, 'mp', [(i, (i - k) % mp) for i in range(mp)])]
  transfers between devices with their start and end apart: 3 -> 3, of which waited for: 0 -> 0; matrix products, arithmetic and copies ran while one was open for 2% -> 2% of each run, Pallas kernels for 25% -> 24%
where the time goes in v6:
time: 308 us; the launch traced here: 309 us
  Pallas kernels  281 us (91%)
  local copies, waits for them, and re-layouts  22.7 us (7%)
    pallas_call x1, Pallas kernels, front_call(): pl.pallas_call(front_kernel, in_specs=[vmem] * 6 + [hbm], out_specs=[vmem...  199 us
    pallas_call x1, Pallas kernels, feed_remote_call(): pl.pallas_call(feed_remote_kernel, in_specs=[vmem, vmem, pl.BlockSpec(mem...  73.3 us
    unnamed x38, local copies, waits for them, and re-layouts  16.3 us
    pallas_call x1, Pallas kernels, finish_call(): pl.pallas_call(finish_kernel, grid_spec=pltpu.PrefetchScalarGridSpec(num_...  8.22 us
  transfers between devices with their start and end apart: 3, of which 0 were waited for; matrix products, arithmetic and copies ran while one was open for 2% of the time, Pallas kernels for 24%

profile of v6, /device:TPU:0, one launch (start us, length us, event | category | flops | bytes accessed | tf_op | source)
XLA Modules:
  0.0 308.6 jit_solution(2284143079793234220)
XLA Ops:
  0.6 0.8 slice_bitcast_fusion.2
  1.4 0.0 copy-start.1
  1.4 1.4 reshape.73.norm_gain.gain
  2.8 2.7 copy.27
  5.5 0.0 copy-done.1
  5.5 0.0 slice-start
  5.5 0.0 copy-start.9
  5.5 0.0 copy-start.10
  5.5 0.0 copy-start.7
  5.5 0.0 copy-start.8
  5.5 0.0 copy-start.12
  5.6 0.0 copy-start.13
  5.6 1.4 copy.28
  6.9 0.0 slice-done
  6.9 0.1 copy.40
  7.1 0.1 copy.32
  7.2 0.0 copy-done.9
  7.2 0.1 copy.31
  7.3 0.0 copy-done.10
  7.3 0.1 reshape.74
  7.4 0.0 copy-done.7
  7.4 0.0 copy-done.8
  7.4 0.7 pad_maximum_fusion.w_feed
  8.2 0.6 pad.4.ids
  8.8 0.0 copy-done.12
  8.8 0.0 copy-done.13
  8.8 0.6 maximum_bitcast_fusion.gains
  9.4 0.7 pad_maximum_fusion.2.w_attn
  10.1 199.1 %front.1 = (bf16[4,240,768]{2,1,0:T(8,128)(2,1)}, bf16[4,240,768]{2,1,0:T(8,128)(2,1)}, bf16[4,240,768]{2,1,0:T(8,128)(2,1)}, bf16[240,768]{1,0:T(8,128)(2,1)}, ...) custom-call(bf16[4,236,768]{2,1,0:T(8,128)(2,1)} %bitcast.38, ...), custom_call_target="tpu_custom_call" | custom-call | tf_op jit(solution)/shard_map/front/pallas_call | solution.py:1214
  209.3 0.1 collective-permute-start
  209.3 0.8 collective-permute-start.1
  210.1 1.2 collective-permute-start.2
  211.3 73.3 %feed_forward_scatter.1 = (f32[960,768]{1,0:T(8,128)}, f32[960,768]{1,0:T(8,128)}, f32[96,768]{1,0:T(8,128)}, f32[96,768]{1,0:T(8,128)}, f32[96,768]{1,0:T(8,128)}, /*index=5*/f32[8,128]{1,0:T(8,128)}) custom-call(bf16[960,768]{1,0:T(8,128)(2,1)} %bitcast.55, bf16[960,768]{1,0:T(8,128)(2,1)} %bitcast.56, bf16[4,8,2,96,768]{4,3,2,1,0:T(8,128)(2,1)} %bitcast.54, ...), custom_call_target="tpu_custom_call" | custom-call | flops 27179089920 | bytes 18874368 | tf_op jit(solution)/shard_map/feed_forward_scatter/pallas_call | solution.py:542
  284.7 0.0 copy-start.11
  284.7 1.1 slice_bitcast_fusion
  285.8 0.9 slice.35
  286.7 0.1 copy.35
  286.8 0.1 copy.33
  287.0 0.9 copy.38
  287.9 0.7 copy.39
  288.6 0.0 copy-done.11
  288.6 0.6 slice_bitcast_fusion.4
  289.2 0.6 slice_bitcast_fusion.3
  289.8 0.0 collective-permute-done.ret1
  289.8 0.0 copy-start.2
  289.8 0.0 collective-permute-done.1.ret2
  289.8 0.0 copy-start.3
  289.8 0.0 collective-permute-done.2.ret3
  289.8 0.0 copy-start.4
  289.8 0.7 copy-done.2
  290.5 0.1 copy-done.3
  290.7 0.1 copy-done.4
  290.8 8.2 %finish.1 = (bf16[4,236,768]{2,1,0:T(8,128)(2,1)}, f32[4,236,768]{2,1,0:T(8,128)}) custom-call(s32[1]{0:T(128)} %bitcast.place, bf16[4,236,768]{2,1,0:T(8,128)(2,1)} %bitcast.39, bf16[4,236,768]{2,1,0:T(8,128)(2,1)} %bitcast.41, f32[1,768]{1,0:T(1,128)} %reshape.73.norm_gain.gain, f32[4,240,768]{2,1,0:T(8,128)} %bitcast.42, f32[4,240,768]{2,1,0:T(8,128)} %bitcast.43, ...), custom_call_target="tpu_custom_call" | custom-call | tf_op jit(solution)/shard_map/finish/pallas_call | solution.py:1306
  299.0 0.0 copy-start
  299.0 5.8 %copy.37 = f32[2,2,236,768]{3,1,2,0:T(2,128)} copy(f32[2,2,236,768]{3,2,1,0:T(8,128)} %bitcast.44) | data formatting | bytes 5799936
  304.8 0.0 copy-start.6
  304.8 0.0 copy-done
  304.8 0.0 copy-start.5
  304.8 2.2 copy.36
  307.0 0.0 copy-done.6
  307.0 0.7 copy.43
  307.7 0.0 copy-done.5
  307.7 0.7 copy.44
  (3 shorter events, 0.1 us)
Async XLA Ops:
  1.4 4.1 %copy-start.1 = (bf16[2,2,236,768]{3,1,2,0:T(2,128)(2,1)S(1)}, bf16[2,2,236,768]{3,1,2,0:T(2,128)(2,1)}, u32[]{:S(2)}) copy-start(bf16[2,2,236,768]{3,1,2,0:T(2,128)(2,1)} %param.19) | copy-start | bytes 4349956
  5.5 1.4 slice-start
  5.5 1.7 copy-start.9
  5.5 1.8 copy-start.10
  5.5 1.9 copy-start.7
  5.5 1.9 copy-start.8
  5.5 3.3 %copy-start.12 = (f32[64]{0:T(128)S(1)}, f32[64]{0:T(128)}, u32[]{:S(2)}) copy-start(f32[64]{0:T(128)} %param.17) | copy-start | bytes 772
  5.6 3.2 %copy-start.13 = (f32[64]{0:T(128)S(1)}, f32[64]{0:T(128)}, u32[]{:S(2)}) copy-start(f32[64]{0:T(128)} %param.16) | copy-start | bytes 772
  209.3 80.5 %collective-permute-start = (bf16[240,768]{1,0:T(8,128)(2,1)}, bf16[240,768]{1,0:T(8,128)(2,1)S(1)}, u32[]{:S(2)}, u32[]{:S(2)}) collective-permute-start(bf16[240,768]{1,0:T(8,128)(2,1)} %get-tuple-element.38), channel_id=1, source_target_pairs={{0,3},{1,0},{2,1},{3,2},{4,7},{5,4},{6,5},{7,6},{8,11},{9,8},{10,9... | collective-permute-start | bytes 1105928 | tf_op jit(solution)/shard_map/ppermute | solution.py:1359
  209.3 80.5 %collective-permute-start.1 = (bf16[240,768]{1,0:T(8,128)(2,1)}, bf16[240,768]{1,0:T(8,128)(2,1)S(1)}, u32[]{:S(2)}, u32[]{:S(2)}) collective-permute-start(bf16[240,768]{1,0:T(8,128)(2,1)} %get-tuple-element.39), channel_id=1, source_target_pairs={{0,2},{1,3},{2,0},{3,1},{4,6},{5,7},{6,4},{7,5},{8,10},{9,11},{10,... | collective-permute-start | bytes 1105928 | tf_op jit(solution)/shard_map/ppermute | solution.py:1359
  210.1 79.7 %collective-permute-start.2 = (bf16[240,768]{1,0:T(8,128)(2,1)}, bf16[240,768]{1,0:T(8,128)(2,1)S(1)}, u32[]{:S(2)}, u32[]{:S(2)}) collective-permute-start(bf16[240,768]{1,0:T(8,128)(2,1)} %get-tuple-element.40), channel_id=1, source_target_pairs={{0,1},{1,2},{2,3},{3,0},{4,5},{5,6},{6,7},{7,4},{8,9},{9,10},{10,1... | collective-permute-start | bytes 1105928 | tf_op jit(solution)/shard_map/ppermute | solution.py:1359
  284.7 3.9 %copy-start.11 = (f32[8,128]{1,0:T(8,128)S(1)}, f32[8,128]{1,0:T(8,128)}, u32[]{:S(2)}) copy-start(f32[8,128]{1,0:T(8,128)} %get-tuple-element.46) | copy-start | bytes 12292
  289.8 0.7 copy-start.2
  289.8 0.9 copy-start.3
  289.8 1.0 copy-start.4
  299.0 5.8 %copy-start = (bf16[4,236,768]{2,1,0:T(8,128)(2,1)S(1)}, bf16[4,236,768]{2,1,0:T(8,128)(2,1)}, u32[]{:S(2)}) copy-start(bf16[4,236,768]{2,1,0:T(8,128)(2,1)} %get-tuple-element.41) | copy-start | bytes 4349956
  304.8 2.2 copy-start.6
  304.8 2.9 copy-start.5

commit v7 on v6

--- a/solution.py
+++ b/solution.py
@@ -10,6 +10,8 @@
 HD = 64
 MOST = 709
 IMAGES = 8
+STRIP = 48
+EARLY = 144
 PIECE = 240
 BIG = 768
 REST = 256
@@ -395,13 +397,12 @@
 def feed_remote_kernel(
     x_ref, dy_ref, w_hbm, g_attn, z_attn, gain, gains_in,
     branch, d_normed, out_attn, out_up, out_down, out_gains,
-    xt, dt, w_buf, g_ff, ff_core, ff_first, ff_second, at_core, at_first, at_second, got_z,
+    xt, dt, w_buf, hidden, d_up, g_ff, ff_core, ff_first, ff_second, at_core, at_first, at_second, got_z,
     sums, got_sums, z_sums,
     w_sem, ff_send, ff_recv, at_send, at_recv, z_send, z_recv, sum_send, sum_recv,
 ):
     width = x_ref.shape[1]
     steps, shard = w_hbm.shape[0], w_hbm.shape[3]
-    half = width // 2
     at = Place(steps)
     at.greet()
     attn = Scatter(at, halves(width), g_attn, at_core, at_first, at_second, at_send, at_recv)
@@ -416,20 +417,6 @@
             w_hbm.at[at.target(step), :, kind], w_buf.at[slot, kind], w_sem.at[slot, kind]
         )
 
-    def feed_half(step, index):
-        cols = slice(half * index, half * index + half)
-        slot = lax.rem(step, 2)
-        upper = w_buf[slot, 0, :, :, cols].reshape(width, half)
-        lower = w_buf[slot, 1, :, :, cols].reshape(width, half)
-        value, slope = gelu_parts(nn(x_ref[...], upper))
-        hidden = value.astype(BF16)
-        d_up = (nn(dy_ref[...], lower) * slope).astype(BF16)
-        split = (2, 2, 2, shard, half)
-        g_ff[step, 0, :, :, :, :, cols] = nn(xt[...], d_up).astype(BF16).reshape(split)
-        g_ff[step, 1, :, :, :, :, cols] = nn(dt[...], hidden).astype(BF16).reshape(split)
-        branch[...] += nt(hidden, lower)
-        d_normed[...] += nt(d_up, upper)
-
     attn.start(0)
     for kind in range(2):
         w_copy(0, kind).start()
@@ -447,27 +434,31 @@
             for kind in range(2):
                 w_copy(step + 1, kind).start()
 
-        feed_half(step, 0)
+        slot = lax.rem(step, 2)
+        split = (2, 2, 2, shard, width)
+
+        def weights(kind):
+            return w_buf[slot, kind].reshape(width, width)
+
+        value, slope = gelu_parts(nn(x_ref[...], weights(0)))
+        hidden[...] = value.astype(BF16)
+        d_up[...] = (nn(dy_ref[...], weights(1)) * slope).astype(BF16)
 
         @pl.when(step == 0)
         def _():
             attn.after_core(0)
 
+        g_ff[step, 0] = nn(xt[...], d_up[...]).astype(BF16).reshape(split)
+        g_ff[step, 1] = nn(dt[...], hidden[...]).astype(BF16).reshape(split)
+        feed.start(step)
+
         @pl.when(step >= 1)
         def _():
-            feed.after_core(step - 1)
-
-        @pl.when(step >= 2)
-        def _():
-            feed.after_second(step - 2)
-            along.send_outer(step - 2)
-
-        feed_half(step, 1)
-        feed.start(step)
-
-        @pl.when(step >= 2)
-        def _():
-            along.send_inner(step - 2)
+            feed.after_first(step - 1)
+
+        branch[...] += nt(hidden[...], weights(1))
+        d_normed[...] += nt(d_up[...], weights(0))
+        feed.after_core(step)
 
         @pl.when(step == 0)
         def _():
@@ -475,7 +466,8 @@
 
         @pl.when(step >= 1)
         def _():
-            feed.after_first(step - 1)
+            feed.after_second(step - 1)
+            along.send_outer(step - 1)
 
         return carry
 
@@ -498,18 +490,17 @@
         sums[stage + 1] = sums[stage] + got_sums[stage]
 
     sum_copy(0).start()
-    feed.after_core(last)
-    next_sum(0)
-    sum_copy(1).start()
-    feed.after_second(last - 1)
-    along.send_outer(last - 1)
-    along.send_inner(last - 1)
-    next_sum(1)
-    sum_copy(2).start()
     for item in range(2):
         cols = attn.items[item][1]
         out_attn[:, cols] = attn.total(0, item) + z_attn[:, cols]
+    next_sum(0)
+    sum_copy(1).start()
+    along.send_inner(0)
+    along.send_inner(1)
+    next_sum(1)
+    sum_copy(2).start()
     feed.after_first(last)
+    along.send_inner(2)
     next_sum(2)
     for k in range(1, steps):
         sum_z_copy(k).start()
@@ -550,6 +541,8 @@
             pltpu.VMEM((width, rows), BF16),
             pltpu.VMEM((width, rows), BF16),
             pltpu.VMEM((2, 2, 8, shard, width), BF16),
+            pltpu.VMEM((rows, width), BF16),
+            pltpu.VMEM((rows, width), BF16),
             pltpu.VMEM((steps, 2, 2, 2, 2, shard, width), BF16),
             pltpu.VMEM((steps, 2, 2, 2, shard, width), BF16),
             pltpu.VMEM((steps, 2, 2, shard, width), BF16),
@@ -970,9 +963,12 @@
         return at.copy(src, got_rows.at[k - 1, kind], row_send.at[kind, k - 1],
                        row_recv.at[kind, k - 1], mp=at.along(k))
 
-    def back_copy(k):
-        return at.copy(got_rows.at[k - 1, 0], returned.at[k], back_send.at[k - 1],
-                       back_recv.at[k - 1], mp=at.along(-k))
+    def back_copy(k, strip):
+        rows, sem = pl.ds(strip * STRIP, STRIP), (k - 1, strip)
+        return at.copy(got_rows.at[k - 1, 0, rows], returned.at[k, rows], back_send.at[sem],
+                       back_recv.at[sem], mp=at.along(-k))
+
+    strips = [(k, strip) for strip in range(EARLY // STRIP) for k in (1, 3, 2)]
 
     gather.start()
     own_ff.start()
@@ -987,31 +983,32 @@
         pad = jnp.zeros((PIECE - part, width), BF16)
         normed[k, :part] = (centered * spread * gain).astype(BF16)
         normed[k, part:] = pad
-        if k:
-            row_copy(0, k).start()
         grads[k, :part] = cot[sequence]
         grads[k, part:] = pad
+        if k == 2:
+            gather.spread(-1, 1)
+    gather.spread(-2, 2)
+    for kind in range(2):
+        for k in (1, 3, 2):
+            row_copy(kind, k).start()
     place_rows(at.z, part, ids, pt, feat_q, feat_k)
     g_gains[...] = jnp.zeros_like(g_gains)
     total[...] = jnp.zeros_like(total)
-    gather.spread(-1, 1)
     gather.forward(0)
-    gather.spread(-2, 2)
+    gather.spread(-3, 3)
     own_ff.wait()
     gather.forward(-1, 1)
     gather.across(0)
-    gather.spread(-3, 3)
-    gather_ff.spread(0)
     gather.forward(-2, 2)
     gather.across(-1, 1)
     gather.forward(-3, 3)
     gather.across(-2, 2)
     gather.across(-3, 3)
     gather.last()
+    gather_ff.spread(0)
+    gather_ff.start()
     for k in (1, 3, 2):
         row_copy(0, k).wait_recv()
-    for k in (1, 3, 2):
-        row_copy(1, k).start()
 
     def lay_out(kind, own, rows, columns):
         value = 0.0
@@ -1045,6 +1042,10 @@
     def forward_step(step, carry):
         chunk = at.along(step)
 
+        @pl.when(step == 2)
+        def _():
+            gather_ff.forward(0)
+
         def begin(head):
             if head == 2:
                 p_write(step, 0).wait()
@@ -1066,40 +1067,52 @@
         p_write(count - 1, head).wait()
     p_read(0, 0).start()
     value = total[...].astype(BF16)
-    returned[0] = nn(pt[0], value).astype(BF16)
-    for k in range(1, count):
-        got_rows[k - 1, 0] = nn(pt[k], value).astype(BF16)
+    for k, out in enumerate((out0, out1, out2, out3)):
+        piece = nn(pt[k], value).astype(BF16)
+        out[PIECE:] = piece[EARLY:]
+        if k == 0:
+            returned[0, :EARLY] = piece[:EARLY]
+        else:
+            got_rows[k - 1, 0, :EARLY] = piece[:EARLY]
     total[...] = jnp.zeros_like(total)
     for k in (1, 3, 2):
         row_copy(1, k).wait_recv()
-    gather_ff.start()
+    gather_ff.across(0)
     lay_out(1, grads, dy_ref, dt)
 
-    def events(step, head):
-        if step == 0 and head == 1:
+    def events(poll):
+        if poll == 1:
             gather_ff.spread(-1, 1)
-        elif step == 0 and head == 2:
-            gather_ff.forward(0)
+        elif poll == 3:
             gather_ff.spread(-2, 2)
-        elif step == 1 and head == 0:
-            for k in (1, 3, 2):
-                back_copy(k).start()
+            scatter.after_core(0)
+        elif poll == 4:
+            gather_ff.forward(-1, 1)
+        elif poll == 5:
             gather_ff.spread(-3, 3)
-            gather_ff.across(0)
-        elif step == 1 and head == 1:
-            gather_ff.forward(-1, 1)
-        elif step == 1 and head == 2:
+        elif poll == 6:
             gather_ff.forward(-2, 2)
-        elif step == 2 and head == 0:
+            scatter.after_core(1)
+        elif poll == 7:
             gather_ff.across(-1, 1)
+            scatter.after_first(0)
+        elif poll == 8:
             gather_ff.forward(-3, 3)
-        elif step == 2 and head == 1:
+            scatter.after_second(0)
+            along.send_outer(0)
+        elif poll == 9:
             gather_ff.across(-2, 2)
-        elif step == 2 and head == 2:
+            scatter.after_core(2)
+            scatter.after_first(1)
+        elif poll == 10:
+            scatter.after_second(1)
+            along.send_outer(1)
             gather_ff.across(-3, 3)
+        elif poll == 11:
             along.send_inner(0)
-        elif step == 3 and head == 1:
-            along.send_inner(1)
+            scatter.after_first(2)
+        for k, strip in strips[max(0, poll - 3):max(0, poll - 2)]:
+            back_copy(k, strip).start()
 
     def backward_step(step, carry):
         chunk = at.target(step)
@@ -1127,20 +1140,10 @@
             return p_buf.at[lax.rem(step + head, 2)]
 
         def poll(head):
-            @pl.when(step >= 1)
-            def _():
-                if head == 0:
-                    scatter.after_core(step - 1)
-                elif head == 1:
-                    scatter.after_first(step - 1)
-                else:
-                    scatter.after_second(step - 1)
-                    along.send_outer(step - 1)
-
             for which in range(count):
                 @pl.when(step == which)
                 def _():
-                    events(which, head)
+                    events(3 * which + head)
 
         backward_chunk(
             weights_of(chunk), gains[...], dy_ref, xt, dt, raw, d_raw,
@@ -1155,21 +1158,25 @@
         return carry
 
     lax.fori_loop(0, count, backward_step, 0)
+    along.send_inner(1)
+    scatter.after_second(2)
+    along.send_outer(2)
+    along.send_inner(2)
     store_gain(g_gains, total[...], x_ref[...], norm_gain[...])
     value = total[...].astype(BF16)
     for k, out in enumerate((out0, out1, out2, out3)):
-        out[...] = nn(pt[k], value).astype(BF16)
-    along.send_inner(count - 2)
+        out[:PIECE] = nn(pt[k], value).astype(BF16)
     z_attn[...] = jnp.zeros_like(z_attn)
     gather_ff.last()
-    for k in range(1, count):
-        back_copy(k).wait_recv()
+    for k, strip in strips:
+        back_copy(k, strip).wait_recv()
     along.add(0, z_attn)
 
     gather.wait_send()
     gather_ff.wait_send()
+    for k, strip in strips:
+        back_copy(k, strip).wait_send()
     for k in range(1, count):
-        back_copy(k).wait_send()
         for kind in range(2):
             row_copy(kind, k).wait_send()
     for step in range(count - 1):
@@ -1215,8 +1222,8 @@
         front_kernel,
         in_specs=[vmem] * 6 + [hbm],
         out_specs=[vmem] * 7 + [hbm] + [vmem] * 3 + [hbm],
-        out_shape=[rows, rows, rows]
-        + [jax.ShapeDtypeStruct((PIECE, width), BF16)] * 4
+        out_shape=[rows, rows, jax.ShapeDtypeStruct((count, EARLY, width), BF16)]
+        + [jax.ShapeDtypeStruct((2 * PIECE - EARLY, width), BF16)] * 4
         + [
             jax.ShapeDtypeStruct((count, 2, 2, 2, 2, shard, width), BF16),
             jax.ShapeDtypeStruct((1, 1, 2, 2, 2, shard, width), BF16),
@@ -1249,8 +1256,8 @@
             pltpu.VMEM((ROWS, width), F32),
             pltpu.SemaphoreType.DMA((2, count - 1)),
             pltpu.SemaphoreType.DMA((2, count - 1)),
-            pltpu.SemaphoreType.DMA((count - 1,)),
-            pltpu.SemaphoreType.DMA((count - 1,)),
+            pltpu.SemaphoreType.DMA((count - 1, EARLY // STRIP)),
+            pltpu.SemaphoreType.DMA((count - 1, EARLY // STRIP)),
             pltpu.SemaphoreType.DMA((9, count)),
             pltpu.SemaphoreType.DMA((8, count)),
             pltpu.SemaphoreType.DMA((9, count)),
@@ -1281,8 +1288,8 @@
         @pl.when(step == index)
         def _():
             x = tok[0].astype(F32)
-            output[0] = (x + (branch[0] + back[0].astype(F32))[:part]).astype(BF16)
-            d_normed = (d_ff[0] + ret[...].astype(F32))[:part]
+            output[0] = (x + (branch[0] + jnp.concatenate([back[0], ret[PIECE:]]).astype(F32))[:part]).astype(BF16)
+            d_normed = (d_ff[0] + ret[:PIECE].astype(F32))[:part]
             centered = x - jnp.mean(x, axis=-1, keepdims=True)
             spread = lax.rsqrt(jnp.mean(centered * centered, axis=-1, keepdims=True) + 1e-6)
             unit = centered * spread
@@ -1301,14 +1308,15 @@
         (1, part, width), lambda k, place: (lax.rem(place[0] + k, count), 0, 0)
     )
     padded = pl.BlockSpec((1, PIECE, width), lambda k, place: (k, 0, 0))
-    piece = pl.BlockSpec((PIECE, width), lambda k, place: (0, 0))
+    piece = pl.BlockSpec((2 * PIECE - EARLY, width), lambda k, place: (0, 0))
+    early = pl.BlockSpec((1, EARLY, width), lambda k, place: (k, 0, 0))
     line = pl.BlockSpec((1, width), lambda k, place: (0, 0))
     return pl.pallas_call(
         finish_kernel,
         grid_spec=pltpu.PrefetchScalarGridSpec(
             num_scalar_prefetch=1,
             grid=(count,),
-            in_specs=[block, block, line, padded, padded, padded] + [piece] * 4,
+            in_specs=[block, block, line, padded, padded, early] + [piece] * 4,
             out_specs=[block, block],
         ),
         out_shape=[
@@ -1381,8 +1389,8 @@
             place, part, normed, grads, received, ids, gains, gain, w_attn
         )
         outs = send_back(outs)
-        back = jnp.stack([out[1] for out in outs])
-        returned = [out[0] for out in outs]
+        back = jnp.stack([out[1, :EARLY] for out in outs])
+        returned = [jnp.concatenate([out[0], out[1, EARLY:]]) for out in outs]
         flat_normed = normed.reshape(count * PIECE, width)
         branch, d_ff, g_up, g_down = feed_call(
             flat_normed, grads.reshape(count * PIECE, width),

time: 308 us -> 283 us (0.919); the launches traced: 309 us -> 278 us
  Pallas kernels: 281 us -> 244 us
  starting transfers between devices: 2.07 us -> 8.17 us
    pallas_call x1, Pallas kernels: 199 us -> 167 us  [front_call(): pl.pallas_call(front_kernel, in_specs=[vmem] * 6 + [hbm], out_specs=[vmem...]
    ppermute x3, starting transfers between devices: 2.07 us -> 8.17 us  [send_back(): lax.ppermute(out, 'mp', [(i, (i - k) % mp) for i in range(mp)])]
    pallas_call x1, Pallas kernels: 73.3 us -> 68.4 us  [feed_remote_call(): pl.pallas_call(feed_remote_kernel, in_specs=[vmem, vmem, pl.BlockSpec(mem...]
  transfers between devices with their start and end apart: 3 -> 3, of which waited for: 0 -> 0; matrix products, arithmetic and copies ran while one was open for 2% -> 2% of each run, Pallas kernels for 24% -> 25%
where the time goes in v7:
time: 283 us; the launch traced here: 278 us
  Pallas kernels  244 us (86%)
  local copies, waits for them, and re-layouts  22.8 us (8%)
  starting transfers between devices  8.17 us (3%)
    pallas_call x1, Pallas kernels, front_call(): pl.pallas_call(front_kernel, in_specs=[vmem] * 6 + [hbm], out_specs=[vmem...  167 us
    pallas_call x1, Pallas kernels, feed_remote_call(): pl.pallas_call(feed_remote_kernel, in_specs=[vmem, vmem, pl.BlockSpec(mem...  68.4 us
    unnamed x38, local copies, waits for them, and re-layouts  16.4 us
    ppermute x3, starting transfers between devices, send_back(): lax.ppermute(out, 'mp', [(i, (i - k) % mp) for i in range(mp)])  8.17 us
    pallas_call x1, Pallas kernels, finish_call(): pl.pallas_call(finish_kernel, grid_spec=pltpu.PrefetchScalarGridSpec(num_...  8.05 us
  transfers between devices with their start and end apart: 3, of which 0 were waited for; matrix products, arithmetic and copies ran while one was open for 2% of the time, Pallas kernels for 25%

profile of v7, /device:TPU:0, one launch (start us, length us, event | category | flops | bytes accessed | tf_op | source)
XLA Modules:
  0.0 277.9 jit_solution(9047923055477458240)
XLA Ops:
  0.6 0.8 slice_bitcast_fusion.2
  1.4 0.0 copy-start.1
  1.4 1.4 reshape.73.norm_gain.gain
  2.8 2.7 copy.27
  5.5 0.0 copy-done.1
  5.5 0.0 slice-start
  5.5 0.0 copy-start.9
  5.5 0.0 copy-start.10
  5.5 0.0 copy-start.7
  5.5 0.0 copy-start.8
  5.5 0.0 copy-start.12
  5.6 0.0 copy-start.13
  5.6 1.4 copy.28
  6.9 0.0 slice-done
  6.9 0.1 copy.40
  7.1 0.1 copy.32
  7.2 0.0 copy-done.9
  7.2 0.1 copy.31
  7.3 0.0 copy-done.10
  7.3 0.1 reshape.74
  7.4 0.0 copy-done.7
  7.4 0.0 copy-done.8
  7.4 0.7 pad_maximum_fusion.w_feed
  8.2 0.6 pad.4.ids
  8.8 0.0 copy-done.12
  8.8 0.0 copy-done.13
  8.8 0.6 maximum_bitcast_fusion.gains
  9.4 0.7 pad_maximum_fusion.2.w_attn
  10.1 167.2 %front.1 = (bf16[4,240,768]{2,1,0:T(8,128)(2,1)}, bf16[4,240,768]{2,1,0:T(8,128)(2,1)}, bf16[4,144,768]{2,1,0:T(8,128)(2,1)}, bf16[336,768]{1,0:T(8,128)(2,1)}, ...) custom-call(bf16[4,236,768]{2,1,0:T(8,128)(2,1)} %bitcast.38, ...), custom_call_target="tpu_custom_call" | custom-call | tf_op jit(solution)/shard_map/front/pallas_call | solution.py:1221
  177.4 4.9 %collective-permute-start = (bf16[336,768]{1,0:T(8,128)(2,1)}, bf16[336,768]{1,0:T(8,128)(2,1)S(1)}, u32[]{:S(2)}, u32[]{:S(2)}) collective-permute-start(bf16[336,768]{1,0:T(8,128)(2,1)} %get-tuple-element.38), channel_id=1, source_target_pairs={{0,3},{1,0},{2,1},{3,2},{4,7},{5,4},{6,5},{7,6},{8,11},{9,8},{10,9... | collective-permute-start | bytes 1548296 | tf_op jit(solution)/shard_map/ppermute | solution.py:1367
  182.3 1.4 collective-permute-start.1
  183.6 1.9 collective-permute-start.2
  185.6 68.4 %feed_forward_scatter.1 = (f32[960,768]{1,0:T(8,128)}, f32[960,768]{1,0:T(8,128)}, f32[96,768]{1,0:T(8,128)}, f32[96,768]{1,0:T(8,128)}, f32[96,768]{1,0:T(8,128)}, /*index=5*/f32[8,128]{1,0:T(8,128)}) custom-call(bf16[960,768]{1,0:T(8,128)(2,1)} %bitcast.55, bf16[960,768]{1,0:T(8,128)(2,1)} %bitcast.56, bf16[4,8,2,96,768]{4,3,2,1,0:T(8,128)(2,1)} %bitcast.54, ...), custom_call_target="tpu_custom_call" | custom-call | flops 27179089920 | bytes 18874368 | tf_op jit(solution)/shard_map/feed_forward_scatter/pallas_call | solution.py:533
  254.0 0.0 copy-start.11
  254.0 1.1 slice_bitcast_fusion
  255.1 0.9 slice.35
  256.0 0.1 copy.35
  256.1 0.1 copy.33
  256.3 0.9 copy.38
  257.2 0.7 copy.39
  257.9 0.0 copy-done.11
  257.9 0.6 slice_bitcast_fusion.4
  258.5 0.6 slice_bitcast_fusion.3
  259.1 0.0 collective-permute-done.ret1
  259.1 0.0 copy-start.2
  259.1 0.0 collective-permute-done.1.ret2
  259.1 0.0 copy-start.3
  259.1 0.0 collective-permute-done.2.ret3
  259.1 0.0 copy-start.4
  259.1 0.7 copy-done.2
  259.9 0.2 copy-done.3
  260.1 0.2 copy-done.4
  260.2 8.0 %finish.1 = (bf16[4,236,768]{2,1,0:T(8,128)(2,1)}, f32[4,236,768]{2,1,0:T(8,128)}) custom-call(s32[1]{0:T(128)} %bitcast.place, bf16[4,236,768]{2,1,0:T(8,128)(2,1)} %bitcast.39, bf16[4,236,768]{2,1,0:T(8,128)(2,1)} %bitcast.41, f32[1,768]{1,0:T(1,128)} %reshape.73.norm_gain.gain, f32[4,240,768]{2,1,0:T(8,128)} %bitcast.42, f32[4,240,768]{2,1,0:T(8,128)} %bitcast.43, ...), custom_call_target="tpu_custom_call" | custom-call | tf_op jit(solution)/shard_map/finish/pallas_call | solution.py:1314
  268.3 0.0 copy-start
  268.3 5.8 %copy.37 = f32[2,2,236,768]{3,1,2,0:T(2,128)} copy(f32[2,2,236,768]{3,2,1,0:T(8,128)} %bitcast.44) | data formatting | bytes 5799936
  274.1 0.0 copy-start.6
  274.1 0.0 copy-done
  274.1 0.0 copy-start.5
  274.1 2.2 copy.36
  276.3 0.0 copy-done.6
  276.3 0.7 copy.43
  277.0 0.0 copy-done.5
  277.0 0.7 copy.44
  (3 shorter events, 0.1 us)
Async XLA Ops:
  1.4 4.1 %copy-start.1 = (bf16[2,2,236,768]{3,1,2,0:T(2,128)(2,1)S(1)}, bf16[2,2,236,768]{3,1,2,0:T(2,128)(2,1)}, u32[]{:S(2)}) copy-start(bf16[2,2,236,768]{3,1,2,0:T(2,128)(2,1)} %param.19) | copy-start | bytes 4349956
  5.5 1.4 slice-start
  5.5 1.7 copy-start.9
  5.5 1.8 copy-start.10
  5.5 1.9 copy-start.7
  5.5 1.9 copy-start.8
  5.5 3.3 %copy-start.12 = (f32[64]{0:T(128)S(1)}, f32[64]{0:T(128)}, u32[]{:S(2)}) copy-start(f32[64]{0:T(128)} %param.17) | copy-start | bytes 772
  5.6 3.2 %copy-start.13 = (f32[64]{0:T(128)S(1)}, f32[64]{0:T(128)}, u32[]{:S(2)}) copy-start(f32[64]{0:T(128)} %param.16) | copy-start | bytes 772
  177.4 81.7 %collective-permute-start = (bf16[336,768]{1,0:T(8,128)(2,1)}, bf16[336,768]{1,0:T(8,128)(2,1)S(1)}, u32[]{:S(2)}, u32[]{:S(2)}) collective-permute-start(bf16[336,768]{1,0:T(8,128)(2,1)} %get-tuple-element.38), channel_id=1, source_target_pairs={{0,3},{1,0},{2,1},{3,2},{4,7},{5,4},{6,5},{7,6},{8,11},{9,8},{10,9... | collective-permute-start | bytes 1548296 | tf_op jit(solution)/shard_map/ppermute | solution.py:1367
  182.3 76.8 %collective-permute-start.1 = (bf16[336,768]{1,0:T(8,128)(2,1)}, bf16[336,768]{1,0:T(8,128)(2,1)S(1)}, u32[]{:S(2)}, u32[]{:S(2)}) collective-permute-start(bf16[336,768]{1,0:T(8,128)(2,1)} %get-tuple-element.39), channel_id=1, source_target_pairs={{0,2},{1,3},{2,0},{3,1},{4,6},{5,7},{6,4},{7,5},{8,10},{9,11},{10,... | collective-permute-start | bytes 1548296 | tf_op jit(solution)/shard_map/ppermute | solution.py:1367
  183.6 75.5 %collective-permute-start.2 = (bf16[336,768]{1,0:T(8,128)(2,1)}, bf16[336,768]{1,0:T(8,128)(2,1)S(1)}, u32[]{:S(2)}, u32[]{:S(2)}) collective-permute-start(bf16[336,768]{1,0:T(8,128)(2,1)} %get-tuple-element.40), channel_id=1, source_target_pairs={{0,1},{1,2},{2,3},{3,0},{4,5},{5,6},{6,7},{7,4},{8,9},{9,10},{10,1... | collective-permute-start | bytes 1548296 | tf_op jit(solution)/shard_map/ppermute | solution.py:1367
  254.0 3.9 %copy-start.11 = (f32[8,128]{1,0:T(8,128)S(1)}, f32[8,128]{1,0:T(8,128)}, u32[]{:S(2)}) copy-start(f32[8,128]{1,0:T(8,128)} %get-tuple-element.46) | copy-start | bytes 12292
  259.1 0.8 copy-start.2
  259.1 1.0 copy-start.3
  259.1 1.1 copy-start.4
  268.3 5.8 %copy-start = (bf16[4,236,768]{2,1,0:T(8,128)(2,1)S(1)}, bf16[4,236,768]{2,1,0:T(8,128)(2,1)}, u32[]{:S(2)}) copy-start(bf16[4,236,768]{2,1,0:T(8,128)(2,1)} %get-tuple-element.41) | copy-start | bytes 4349956
  274.1 2.2 copy-start.6
  274.1 2.9 %copy-start.5 = (f32[96,768]{1,0:T(8,128)S(1)}, f32[96,768]{1,0:T(8,128)}, u32[]{:S(2)}) copy-start(f32[96,768]{1,0:T(8,128)} %get-tuple-element.45) | copy-start | bytes 884740

commit v8 on v7

--- a/solution.py
+++ b/solution.py
@@ -291,11 +291,11 @@
             def does(plane):
                 from_x, from_y = self.piece(plane, x=True), self.piece(plane, y=True)
                 self.arrived(1, plane, from_x)
-                if r % 2 == 0:
+                if r in (0, 1, -3):
                     self.copy(5, plane, from_x, dp=at.above).start()
                 self.copy(4, plane, from_x, dp=at.sibling).start()
                 self.arrived(2, plane, from_y)
-                if r % 2 == 1:
+                if r not in (0, 1, -3):
                     self.copy(5, plane, from_y, dp=at.beside).start()
                 self.copy(6, plane, from_y, dp=at.sibling).start()
 
@@ -395,11 +395,12 @@
 
 
 def feed_remote_kernel(
-    x_ref, dy_ref, w_hbm, g_attn, z_attn, gain, gains_in,
-    branch, d_normed, out_attn, out_up, out_down, out_gains,
+    x_ref, dy_ref, w_hbm, g_attn, z_attn, gain, gains_in, back0, back1, back2, back3,
+    branch, d_normed, out_attn, out_up, out_down, out_gains, returned,
     xt, dt, w_buf, hidden, d_up, g_ff, ff_core, ff_first, ff_second, at_core, at_first, at_second, got_z,
-    sums, got_sums, z_sums,
-    w_sem, ff_send, ff_recv, at_send, at_recv, z_send, z_recv, sum_send, sum_recv,
+    parts, got_za, sums, got_sums, z_sums,
+    w_sem, ff_send, ff_recv, at_send, at_recv, z_send, z_recv, za_send, za_recv,
+    sum_send, sum_recv, back_send, back_recv, own_sem,
 ):
     width = x_ref.shape[1]
     steps, shard = w_hbm.shape[0], w_hbm.shape[3]
@@ -409,6 +410,7 @@
     both = (0, slice(0, width), True), (1, slice(0, width), False)
     feed = Scatter(at, both, g_ff, ff_core, ff_first, ff_second, ff_send, ff_recv)
     along = Along(at, ff_second, got_z, z_send, z_recv)
+    along_attn = Along(at, parts, got_za, za_send, za_recv)
     last = steps - 1
 
     def w_copy(step, kind):
@@ -417,9 +419,24 @@
             w_hbm.at[at.target(step), :, kind], w_buf.at[slot, kind], w_sem.at[slot, kind]
         )
 
+    strips = [(k, strip) for strip in range(returned.shape[1] // STRIP) for k in (1, 3, 2)]
+    first = len(strips) - 4 * steps + 1
+
+    def back_copy(k, strip):
+        rows, sem = pl.ds(strip * STRIP, STRIP), (k - 1, strip)
+        return at.copy((back0, back1, back2, back3)[k].at[rows], returned.at[k, rows],
+                       back_send.at[sem], back_recv.at[sem], mp=at.along(-k))
+
+    own_back = pltpu.make_async_copy(back0, returned.at[0], own_sem)
+    own_back.start()
     attn.start(0)
     for kind in range(2):
         w_copy(0, kind).start()
+    for k, strip in strips[:first]:
+        back_copy(k, strip).start()
+    parts[...] = z_attn[...]
+    for step in range(last):
+        along_attn.send_outer(step)
     xt[...] = x_ref[...].T
     dt[...] = dy_ref[...].T
     branch[...] = jnp.zeros_like(branch)
@@ -444,9 +461,24 @@
         hidden[...] = value.astype(BF16)
         d_up[...] = (nn(dy_ref[...], weights(1)) * slope).astype(BF16)
 
+        for which in range(steps):
+            @pl.when(step == which)
+            def _():
+                for k, strip in strips[first + 4 * which:first + 4 * which + 4]:
+                    back_copy(k, strip).start()
+
         @pl.when(step == 0)
         def _():
             attn.after_core(0)
+
+        @pl.when(step == 2)
+        def _():
+            along_attn.send_inner(0)
+
+        @pl.when(step == 3)
+        def _():
+            along_attn.send_inner(1)
+            along_attn.send_inner(2)
 
         g_ff[step, 0] = nn(xt[...], d_up[...]).astype(BF16).reshape(split)
         g_ff[step, 1] = nn(dt[...], hidden[...]).astype(BF16).reshape(split)
@@ -492,7 +524,7 @@
     sum_copy(0).start()
     for item in range(2):
         cols = attn.items[item][1]
-        out_attn[:, cols] = attn.total(0, item) + z_attn[:, cols]
+        out_attn[:, cols] = attn.total(0, item)
     next_sum(0)
     sum_copy(1).start()
     along.send_inner(0)
@@ -505,6 +537,7 @@
     for k in range(1, steps):
         sum_z_copy(k).start()
     z_sums[at.z] = sums[3]
+    along_attn.add(0, out_attn)
     for kind, out in enumerate((out_up, out_down)):
         out[...] = feed.total(last, kind)
         along.add(kind, out)
@@ -515,28 +548,35 @@
         total = total + z_sums[k]
     out_gains[...] = total
 
+    own_back.wait()
+    for k, strip in strips:
+        back_copy(k, strip).wait_recv()
+        back_copy(k, strip).wait_send()
     attn.wait_send(0)
     for step in range(steps):
         feed.wait_send(step)
     for step in range(last):
         along.wait_send(step)
+        along_attn.wait_send(step)
     for stage in range(3):
         sum_copy(stage).wait_send()
     for k in range(1, steps):
         sum_z_copy(k).wait_send()
 
 
-def feed_remote_call(normed, grads, w_ff, g_attn, z_attn, gain, gains):
+def feed_remote_call(normed, grads, w_ff, g_attn, z_attn, gain, gains, backs):
     rows, width = normed.shape
     steps, _, _, shard, _ = w_ff.shape
     vmem = pl.BlockSpec(memory_space=pltpu.VMEM)
+    hbm = pl.BlockSpec(memory_space=pl.ANY)
     return pl.pallas_call(
         feed_remote_kernel,
-        in_specs=[vmem, vmem, pl.BlockSpec(memory_space=pl.ANY)] + [vmem] * 4,
-        out_specs=[vmem] * 6,
+        in_specs=[vmem, vmem, hbm] + [vmem] * 4 + [hbm] * 4,
+        out_specs=[vmem] * 6 + [hbm],
         out_shape=[jax.ShapeDtypeStruct((rows, width), F32)] * 2
         + [jax.ShapeDtypeStruct((shard, width), F32)] * 3
-        + [jax.ShapeDtypeStruct((8, 128), F32)],
+        + [jax.ShapeDtypeStruct((8, 128), F32)]
+        + [jax.ShapeDtypeStruct((steps,) + backs[0].shape, BF16)],
         scratch_shapes=[
             pltpu.VMEM((width, rows), BF16),
             pltpu.VMEM((width, rows), BF16),
@@ -551,6 +591,8 @@
             pltpu.VMEM((1, 1, 2, shard, width), BF16),
             pltpu.VMEM((1, 1, shard, width), BF16),
             pltpu.VMEM((2, 5, shard, width), BF16),
+            pltpu.VMEM((steps - 1, 1, shard, width), BF16),
+            pltpu.VMEM((1, 5, shard, width), BF16),
             pltpu.VMEM((4, 8, 128), F32),
             pltpu.VMEM((3, 8, 128), F32),
             pltpu.VMEM((steps, 8, 128), F32),
@@ -561,8 +603,13 @@
             pltpu.SemaphoreType.DMA((3, 2, 1)),
             pltpu.SemaphoreType.DMA((2, steps - 1)),
             pltpu.SemaphoreType.DMA((2, 5)),
+            pltpu.SemaphoreType.DMA((1, steps - 1)),
+            pltpu.SemaphoreType.DMA((1, 5)),
             pltpu.SemaphoreType.DMA((6,)),
             pltpu.SemaphoreType.DMA((6,)),
+            pltpu.SemaphoreType.DMA((steps - 1, backs[0].shape[0] // STRIP)),
+            pltpu.SemaphoreType.DMA((steps - 1, backs[0].shape[0] // STRIP)),
+            pltpu.SemaphoreType.DMA,
         ],
         compiler_params=pltpu.CompilerParams(
             collective_id=0, has_side_effects=True, vmem_limit_bytes=VMEM
@@ -573,7 +620,7 @@
             transcendentals=rows * width * steps,
         ),
         name="feed_forward_scatter",
-    )(normed, grads, w_ff, g_attn, z_attn, gain, gains)
+    )(normed, grads, w_ff, g_attn, z_attn, gain, gains, *backs)
 
 
 def iota(shape, axis):
@@ -823,8 +870,8 @@
     lane = iota((1, 128), 1)
     low = lane < HD
     mean_of = group_means()
-    stat = jnp.zeros((ROWS, 128), F32)
-    for head in range(3):
+
+    def ahead(head):
         qk = raw[:, 128 * head:128 * head + 128]
         high = qk.astype(BF16)
         mean = nn(high, mean_of) + nn((qk - high.astype(F32)).astype(BF16), mean_of)
@@ -841,7 +888,9 @@
             v = pltpu.roll(v, HD, 1)
         v_aug = jnp.where(low, v, 1.0).astype(BF16)
         v_all[head] = v_aug
-        p_ref = begin(head)
+        return spread, q_aug, k_aug, v_aug
+
+    def products(p_ref, spread, q_aug, k_aug, v_aug):
         parts = []
         for base, count in ((0, BIG), (BIG, REST)):
             keys = k_aug[base:base + count]
@@ -851,18 +900,31 @@
                 prob = jnp.exp(nt(q_aug[rows], keys)).astype(BF16)
                 p_ref[rows, :count] = prob
                 parts.append(nn(prob, values))
-        spill(head)
-        gathered = jnp.concatenate(parts, axis=0)
+        return spread, jnp.concatenate(parts, axis=0)
+
+    def after(head, stat, spread, gathered):
         inverse = 1.0 / gathered
         attend = gathered * pltpu.roll(inverse, HD, 1)
         stat = jnp.where((lane == head) | (lane == HD + head), spread, stat)
-        stat = jnp.where(lane == HD + 8 + head, inverse, stat)
-        if head == 0:
-            att[:, 0:128] = jnp.where(low, 0.0, pltpu.roll(attend, HD, 1)).astype(BF16)
-        elif head == 1:
-            first = attend
-        else:
-            att[:, 128:256] = jnp.where(low, first, pltpu.roll(attend, HD, 1)).astype(BF16)
+        return jnp.where(lane == HD + 8 + head, inverse, stat), attend
+
+    held = ahead(0)
+    p_ref = begin(0)
+    done0 = products(p_ref, *held)
+    held = ahead(1)
+    spill(0)
+    p_ref = begin(1)
+    done1 = products(p_ref, *held)
+    held = ahead(2)
+    stat, first = after(0, jnp.zeros((ROWS, 128), F32), *done0)
+    att[:, 0:128] = jnp.where(low, 0.0, pltpu.roll(first, HD, 1)).astype(BF16)
+    spill(1)
+    p_ref = begin(2)
+    done2 = products(p_ref, *held)
+    stat, second = after(1, stat, *done1)
+    spill(2)
+    stat, third = after(2, stat, *done2)
+    att[:, 128:256] = jnp.where(low, second, pltpu.roll(third, HD, 1)).astype(BF16)
     stats[...] = stat
     branch[...] += nt(att[...], weights(slice(512, 768)))
 
@@ -875,61 +937,72 @@
     lane = iota((1, 128), 1)
     low = lane < HD
     mean_of = group_means()
-    stat = stats[...]
     back_gain = 1.0 / gain
-    d_gain = jnp.zeros((1, 128), F32)
-    for head in range(3):
-        qk = qk_all[head]
-        v_aug = v_all[head]
+
+    def ahead(head):
         tile = 128 * ((head + 1) // 2)
         da = raw[:, tile:tile + 128]
         out = att[:, tile:tile + 128].astype(F32)
         if head != 1:
             da = pltpu.roll(da, HD, 1)
             out = pltpu.roll(out, HD, 1)
-        inverse = stat[:, HD + 8 + head:HD + 9 + head]
+        inverse = stats[:, HD + 8 + head:HD + 9 + head]
         scaled = jnp.where(low, da * inverse, 0.0).astype(BF16).astype(F32)
         dot = jnp.sum(scaled * out, axis=-1, keepdims=True)
         dot_high = dot.astype(BF16).astype(F32)
         d_aug = jnp.where(
             lane == HD, -dot_high, jnp.where(lane == HD + 1, dot_high - dot, scaled)
         )
-        d_low = d_aug.astype(BF16)
-        d_t = d_aug.T.astype(BF16)
-        qk_low = qk.astype(F32)
-        qk_t = qk_low.T.astype(BF16)
-        p_ref = ready(head)
+        qk_t = qk_all[head].astype(F32).T.astype(BF16)
+        return d_aug.astype(BF16), d_aug.T.astype(BF16), qk_t
+
+    def products(head, p_ref, d_low, d_t, qk_t):
+        qk = qk_all[head]
+        v_aug = v_all[head]
         d_queries, d_keys, d_values = [], [], []
         for base, count in ((0, BIG), (BIG, REST)):
             block = slice(base, base + count)
-            d_values.append(nn(d_t[:, block], p_ref[block, :count]).T)
+            d_values.append(nn(d_t[:, block], p_ref[block, :count]))
             for row in range(base, base + count, 256):
                 rows = slice(row, row + 256)
                 d_prob = nt(d_low[rows], v_aug[block])
                 d_score = (p_ref[rows, :count].astype(F32) * d_prob).astype(BF16)
                 p_ref[rows, :count] = d_score
                 d_queries.append(nn(d_score, qk[block]))
-            d_keys.append(nn(qk_t[:, block], p_ref[block, :count]).T)
+            d_keys.append(nn(qk_t[:, block], p_ref[block, :count]))
+        return d_queries, d_keys, d_values
+
+    def after(head, d_queries, d_keys, d_values):
         d_query = jnp.concatenate(d_queries, axis=0)
-        d_key = jnp.concatenate(d_keys, axis=0)
-        d_value = jnp.concatenate(d_values, axis=0)
+        d_key = jnp.concatenate([part.T for part in d_keys], axis=0)
+        d_value = jnp.concatenate([part.T for part in d_values], axis=0)
         d_qk = pltpu.roll(jnp.where(low, d_key, d_query), HD, 1) * 0.125
-        unit = qk_low * back_gain
-        spread = jnp.where(low, stat[:, head:head + 1], stat[:, HD + head:HD + head + 1])
-        d_gain = d_gain + jnp.sum(d_qk * unit, axis=0, keepdims=True)
+        unit = qk_all[head].astype(F32) * back_gain
+        spread = jnp.where(low, stats[:, head:head + 1], stats[:, HD + head:HD + head + 1])
+        g_gains[6:7] += jnp.sum(d_qk * unit, axis=0, keepdims=True)
         scaled = d_qk * gain
         mean = nn(scaled.astype(BF16), mean_of)
         d_qk = spread * (scaled - mean - unit * nn((scaled * unit).astype(BF16), mean_of))
         d_raw[:, 128 * head:128 * head + 128] = d_qk.astype(BF16)
-        if head == 0:
-            first = d_value
-        elif head == 1:
-            both = jnp.where(low, first, pltpu.roll(d_value, HD, 1))
-            d_raw[:, 384:512] = both.astype(BF16)
-        else:
-            d_raw[:, 512:640] = jnp.where(low, d_value, 0.0).astype(BF16)
-        poll(head)
-    g_gains[6:7] += d_gain
+        return d_value
+
+    held = ahead(0)
+    p_ref = ready(0)
+    done0 = products(0, p_ref, *held)
+    held = ahead(1)
+    poll(0)
+    p_ref = ready(1)
+    done1 = products(1, p_ref, *held)
+    held = ahead(2)
+    first = after(0, *done0)
+    poll(1)
+    p_ref = ready(2)
+    done2 = products(2, p_ref, *held)
+    second = after(1, *done1)
+    d_raw[:, 384:512] = jnp.where(low, first, pltpu.roll(second, HD, 1)).astype(BF16)
+    poll(2)
+    third = after(2, *done2)
+    d_raw[:, 512:640] = jnp.where(low, third, 0.0).astype(BF16)
     d_projected = d_raw[...]
     d_normed[...] += nt(d_projected, weights(slice(0, 640)))
     left = nn(xt[...], d_projected)
@@ -941,12 +1014,12 @@
 
 def front_kernel(
     tok, cot, ids, gains, norm_gain, w_attn, w_feed,
-    normed, grads, returned, out0, out1, out2, out3, w_ff, g_last, z_attn, g_gains, p_all,
-    got_rows, w_full, g_buf, at_core, at_first, at_second, got_z,
+    normed, grads, returned, out0, out1, out2, out3, w_ff, g_last, at_second, g_gains, p_all,
+    got_rows, w_full, g_buf, at_core, at_first,
     x_ref, dy_ref, xt, dt, feat_q, feat_k, pt, raw, d_raw, p_buf,
     qk_all, v_all, stats, att, total,
     row_send, row_recv, back_send, back_recv, wa_send, wa_recv, wf_send, wf_recv, own_sem,
-    p_out, p_in, at_send, at_recv, z_send, z_recv,
+    p_out, p_in, at_send, at_recv,
 ):
     count, part, width = tok.shape
     shard = w_attn.shape[0]
@@ -956,7 +1029,6 @@
     gather_ff = Gather(at, w_feed, w_ff, wf_send, wf_recv)
     scatter = Scatter(at, halves(width), g_buf, at_core, at_first, at_second, at_send, at_recv)
     own_ff = pltpu.make_async_copy(w_feed, gather_ff.piece(at.z), own_sem)
-    along = Along(at, at_second, got_z, z_send, z_recv)
 
     def row_copy(kind, k):
         src = (normed, grads)[kind].at[k]
@@ -988,9 +1060,8 @@
         if k == 2:
             gather.spread(-1, 1)
     gather.spread(-2, 2)
-    for kind in range(2):
-        for k in (1, 3, 2):
-            row_copy(kind, k).start()
+    for k in (1, 3, 2):
+        row_copy(0, k).start()
     place_rows(at.z, part, ids, pt, feat_q, feat_k)
     g_gains[...] = jnp.zeros_like(g_gains)
     total[...] = jnp.zeros_like(total)
@@ -1006,9 +1077,10 @@
     gather.across(-3, 3)
     gather.last()
     gather_ff.spread(0)
-    gather_ff.start()
     for k in (1, 3, 2):
         row_copy(0, k).wait_recv()
+    for k in (1, 3, 2):
+        row_copy(1, k).start()
 
     def lay_out(kind, own, rows, columns):
         value = 0.0
@@ -1077,39 +1149,37 @@
     total[...] = jnp.zeros_like(total)
     for k in (1, 3, 2):
         row_copy(1, k).wait_recv()
+    gather_ff.start()
     gather_ff.across(0)
     lay_out(1, grads, dy_ref, dt)
 
     def events(poll):
-        if poll == 1:
+        if poll == 2:
             gather_ff.spread(-1, 1)
         elif poll == 3:
-            gather_ff.spread(-2, 2)
             scatter.after_core(0)
         elif poll == 4:
+            gather_ff.spread(-2, 2)
+        elif poll == 5:
             gather_ff.forward(-1, 1)
-        elif poll == 5:
+        elif poll == 6:
             gather_ff.spread(-3, 3)
-        elif poll == 6:
-            gather_ff.forward(-2, 2)
             scatter.after_core(1)
         elif poll == 7:
-            gather_ff.across(-1, 1)
+            gather_ff.forward(-2, 2)
             scatter.after_first(0)
         elif poll == 8:
+            gather_ff.across(-1, 1)
+        elif poll == 9:
             gather_ff.forward(-3, 3)
-            scatter.after_second(0)
-            along.send_outer(0)
-        elif poll == 9:
-            gather_ff.across(-2, 2)
             scatter.after_core(2)
             scatter.after_first(1)
+            scatter.after_second(0)
         elif poll == 10:
+            gather_ff.across(-2, 2)
+        elif poll == 11:
+            gather_ff.across(-3, 3)
             scatter.after_second(1)
-            along.send_outer(1)
-            gather_ff.across(-3, 3)
-        elif poll == 11:
-            along.send_inner(0)
             scatter.after_first(2)
         for k, strip in strips[max(0, poll - 3):max(0, poll - 2)]:
             back_copy(k, strip).start()
@@ -1158,19 +1228,14 @@
         return carry
 
     lax.fori_loop(0, count, backward_step, 0)
-    along.send_inner(1)
-    scatter.after_second(2)
-    along.send_outer(2)
-    along.send_inner(2)
     store_gain(g_gains, total[...], x_ref[...], norm_gain[...])
     value = total[...].astype(BF16)
     for k, out in enumerate((out0, out1, out2, out3)):
         out[:PIECE] = nn(pt[k], value).astype(BF16)
-    z_attn[...] = jnp.zeros_like(z_attn)
+    scatter.after_second(2)
     gather_ff.last()
     for k, strip in strips:
         back_copy(k, strip).wait_recv()
-    along.add(0, z_attn)
 
     gather.wait_send()
     gather_ff.wait_send()
@@ -1181,7 +1246,6 @@
             row_copy(kind, k).wait_send()
     for step in range(count - 1):
         scatter.wait_send(step)
-        along.wait_send(step)
 
 
 def place_rows(me, part, ids, pt, feat_q, feat_k):
@@ -1227,7 +1291,7 @@
         + [
             jax.ShapeDtypeStruct((count, 2, 2, 2, 2, shard, width), BF16),
             jax.ShapeDtypeStruct((1, 1, 2, 2, 2, shard, width), BF16),
-            jax.ShapeDtypeStruct((shard, width), F32),
+            jax.ShapeDtypeStruct((count - 1, 1, shard, width), BF16),
             jax.ShapeDtypeStruct((8, 128), F32),
             jax.ShapeDtypeStruct((count, 3, ROWS, BIG), BF16),
         ],
@@ -1237,8 +1301,6 @@
             pltpu.VMEM((count - 1, 1, 2, 2, 2, shard, width), BF16),
             pltpu.VMEM((count - 1, 1, 2, 2, shard, width), BF16),
             pltpu.VMEM((count - 1, 1, 2, shard, width), BF16),
-            pltpu.VMEM((count - 1, 1, shard, width), BF16),
-            pltpu.VMEM((1, 5, shard, width), BF16),
             pltpu.VMEM((ROWS, width), BF16),
             pltpu.VMEM((ROWS, width), BF16),
             pltpu.VMEM((width, ROWS), BF16),
@@ -1267,8 +1329,6 @@
             pltpu.SemaphoreType.DMA((2,)),
             pltpu.SemaphoreType.DMA((3, 2, count - 1)),
             pltpu.SemaphoreType.DMA((3, 2, count - 1)),
-            pltpu.SemaphoreType.DMA((1, count - 1)),
-            pltpu.SemaphoreType.DMA((1, 5)),
         ],
         compiler_params=pltpu.CompilerParams(
             collective_id=1, has_side_effects=True, vmem_limit_bytes=FRONT_VMEM
@@ -1278,28 +1338,23 @@
 
 
 def finish_kernel(
-    place, tok, cot, gain, branch, d_ff, back, ret0, ret1, ret2, ret3, output, input_grad
+    place, tok, cot, gain, branch, d_ff, back, ret, output, input_grad
 ):
-    step = pl.program_id(0)
     part = tok.shape[1]
-
-    for index, ret in enumerate((ret0, ret1, ret2, ret3)):
-
-        @pl.when(step == index)
-        def _():
-            x = tok[0].astype(F32)
-            output[0] = (x + (branch[0] + jnp.concatenate([back[0], ret[PIECE:]]).astype(F32))[:part]).astype(BF16)
-            d_normed = (d_ff[0] + ret[:PIECE].astype(F32))[:part]
-            centered = x - jnp.mean(x, axis=-1, keepdims=True)
-            spread = lax.rsqrt(jnp.mean(centered * centered, axis=-1, keepdims=True) + 1e-6)
-            unit = centered * spread
-            scaled = d_normed * gain[...]
-            d_x = spread * (
-                scaled
-                - jnp.mean(scaled, axis=-1, keepdims=True)
-                - unit * jnp.mean(scaled * unit, axis=-1, keepdims=True)
-            )
-            input_grad[0] = cot[0].astype(F32) + d_x
+    x = tok[0].astype(F32)
+    added = branch[0] + jnp.concatenate([back[0], ret[0, PIECE:]]).astype(F32)
+    output[0] = (x + added[:part]).astype(BF16)
+    d_normed = (d_ff[0] + ret[0, :PIECE].astype(F32))[:part]
+    centered = x - jnp.mean(x, axis=-1, keepdims=True)
+    spread = lax.rsqrt(jnp.mean(centered * centered, axis=-1, keepdims=True) + 1e-6)
+    unit = centered * spread
+    scaled = d_normed * gain[...]
+    d_x = spread * (
+        scaled
+        - jnp.mean(scaled, axis=-1, keepdims=True)
+        - unit * jnp.mean(scaled * unit, axis=-1, keepdims=True)
+    )
+    input_grad[0] = cot[0].astype(F32) + d_x
 
 
 def finish_call(place, tokens, cotangent, gain, branch, d_ff, back, returned):
@@ -1308,7 +1363,7 @@
         (1, part, width), lambda k, place: (lax.rem(place[0] + k, count), 0, 0)
     )
     padded = pl.BlockSpec((1, PIECE, width), lambda k, place: (k, 0, 0))
-    piece = pl.BlockSpec((2 * PIECE - EARLY, width), lambda k, place: (0, 0))
+    piece = pl.BlockSpec((1, 2 * PIECE - EARLY, width), lambda k, place: (k, 0, 0))
     early = pl.BlockSpec((1, EARLY, width), lambda k, place: (k, 0, 0))
     line = pl.BlockSpec((1, width), lambda k, place: (0, 0))
     return pl.pallas_call(
@@ -1316,7 +1371,7 @@
         grid_spec=pltpu.PrefetchScalarGridSpec(
             num_scalar_prefetch=1,
             grid=(count,),
-            in_specs=[block, block, line, padded, padded, early] + [piece] * 4,
+            in_specs=[block, block, line, padded, padded, early, piece],
             out_specs=[block, block],
         ),
         out_shape=[
@@ -1325,7 +1380,7 @@
         ],
         compiler_params=pltpu.CompilerParams(vmem_limit_bytes=VMEM),
         name="finish",
-    )(place, tokens, cotangent, gain, branch, d_ff, back, *returned)
+    )(place, tokens, cotangent, gain, branch, d_ff, back, returned)
 
 
 def pack_attention(w_qkv, w_proj):
@@ -1372,10 +1427,9 @@
         normed, grads, back, *outs, w_ff, g_attn, z_attn, g_gains, _ = front_call(
             tok, cot, ids, gains, gain, w_attn, w_ff
         )
-        returned = send_back(outs)
-        branch, d_ff, g_attn, g_up, g_down, g_gains = feed_remote_call(
+        branch, d_ff, g_attn, g_up, g_down, g_gains, returned = feed_remote_call(
             normed.reshape(count * PIECE, width), grads.reshape(count * PIECE, width),
-            w_ff.reshape(mp, dp, 2, shard, width), g_attn, z_attn, gain, g_gains,
+            w_ff.reshape(mp, dp, 2, shard, width), g_attn, z_attn, gain, g_gains, outs,
         )
     else:
         w_attn = lax.all_gather(w_attn, both).reshape(mp, width, width)
@@ -1390,7 +1444,7 @@
         )
         outs = send_back(outs)
         back = jnp.stack([out[1, :EARLY] for out in outs])
-        returned = [jnp.concatenate([out[0], out[1, EARLY:]]) for out in outs]
+        returned = jnp.stack([jnp.concatenate([out[0], out[1, EARLY:]]) for out in outs])
         flat_normed = normed.reshape(count * PIECE, width)
         branch, d_ff, g_up, g_down = feed_call(
             flat_normed, grads.reshape(count * PIECE, width),

time: 283 us -> 262 us (0.926)
  Pallas kernels: 244 us -> 234 us
  starting transfers between devices: 8.17 us -> 0 us
    pallas_call x1, Pallas kernels: 167 us -> 152 us  [front_call(): pl.pallas_call(front_kernel, in_specs=[vmem] * 6 + [hbm], out_specs=[vmem...]
    ppermute x3 -> x0, starting transfers between devices: 8.17 us -> none  [send_back(): lax.ppermute(out, 'mp', [(i, (i - k) % mp) for i in range(mp)])]
    pallas_call x1, Pallas kernels: 68.4 us -> 74.9 us  [feed_remote_call(): pl.pallas_call(feed_remote_kernel, in_specs=[vmem, vmem, hbm] + [vmem] *...]
    unnamed x38 -> x34, local copies, waits for them, and re-layouts: 16.4 us -> 15.3 us
  transfers between devices with their start and end apart: 3 -> 0, of which waited for: 0 -> 0; matrix products, arithmetic and copies ran while one was open for 2% -> 0% of each run, Pallas kernels for 25% -> 0%
where the time goes in v8:
time: 262 us; the launch traced here: 258 us
  Pallas kernels  234 us (89%)
  local copies, waits for them, and re-layouts  20.9 us (8%)
    pallas_call x1, Pallas kernels, front_call(): pl.pallas_call(front_kernel, in_specs=[vmem] * 6 + [hbm], out_specs=[vmem...  152 us
    pallas_call x1, Pallas kernels, feed_remote_call(): pl.pallas_call(feed_remote_kernel, in_specs=[vmem, vmem, hbm] + [vmem] *...  74.9 us
    unnamed x34, local copies, waits for them, and re-layouts  15.3 us
    pallas_call x1, Pallas kernels, finish_call(): pl.pallas_call(finish_kernel, grid_spec=pltpu.PrefetchScalarGridSpec(num_...  7.4 us

profile of v8, /device:TPU:0, one launch (start us, length us, event | category | flops | bytes accessed | tf_op | source)
XLA Modules:
  0.0 257.9 jit_solution(7374139014368227578)
XLA Ops:
  0.6 0.0 copy-start.1
  0.7 1.4 reshape.73.norm_gain.gain
  2.0 2.7 %copy.27 = bf16[2,2,236,768]{3,2,1,0:T(8,128)(2,1)} copy(bf16[2,2,236,768]{3,1,2,0:T(2,128)(2,1)} %param.10) | data formatting | bytes 2899968 | tf_op args[0]
  4.7 0.0 copy-done.1
  4.7 0.0 slice-start
  4.7 0.0 copy-start.7
  4.7 0.0 copy-start.2
  4.7 0.0 copy-start.5
  4.7 0.0 copy-start.6
  4.7 1.4 copy.28
  6.1 0.0 copy-start.8
  6.1 0.0 copy-start.10
  6.1 0.0 copy-start.11
  6.1 0.0 slice-done
  6.1 0.1 copy.40
  6.2 0.1 copy.32
  6.4 0.0 copy-done.7
  6.4 0.1 copy.31
  6.5 0.0 copy-done.2
  6.5 0.7 pad_maximum_fusion.2.w_attn
  7.2 0.0 copy-done.5
  7.2 0.0 copy-done.6
  7.3 0.7 pad_maximum_fusion.w_feed
  8.0 0.0 copy-done.8
  8.0 0.1 reshape.74
  8.1 0.6 pad.4.ids
  8.7 0.0 copy-done.10
  8.7 0.0 copy-done.11
  8.7 0.6 maximum_bitcast_fusion.gains
  9.3 151.6 %front.1 = (bf16[4,240,768]{2,1,0:T(8,128)(2,1)}, bf16[4,240,768]{2,1,0:T(8,128)(2,1)}, bf16[4,144,768]{2,1,0:T(8,128)(2,1)}, bf16[336,768]{1,0:T(8,128)(2,1)}, ...) custom-call(bf16[4,236,768]{2,1,0:T(8,128)(2,1)} %bitcast.38, ...), custom_call_target="tpu_custom_call" | custom-call | tf_op jit(solution)/shard_map/front/pallas_call | solution.py:1285
  160.9 74.9 %feed_forward_scatter.1 = (f32[960,768]{1,0:T(8,128)}, f32[960,768]{1,0:T(8,128)}, f32[96,768]{1,0:T(8,128)}, f32[96,768]{1,0:T(8,128)}, f32[96,768]{1,0:T(8,128...) custom-call(bf16[960,768]{1,0:T(8,128)(2,1)} %bitcast.55, bf16[960,768]{1,0:T(8,128)(2,1)} %bitcast.56, ...), custom_call_target="tpu_custom_call" | custom-call | flops 27179089920 | bytes 18874368 | tf_op jit(solution)/shard_map/feed_forward_scatter/pallas_call | solution.py:572
  235.8 0.9 slice.35
  236.7 0.1 copy.33
  236.9 1.1 slice_bitcast_fusion
  238.0 0.1 copy.35
  238.1 0.9 copy.38
  239.0 7.4 %finish.1 = (bf16[4,236,768]{2,1,0:T(8,128)(2,1)}, f32[4,236,768]{2,1,0:T(8,128)}) custom-call(s32[1]{0:T(128)} %bitcast.place, bf16[4,236,768]{2,1,0:T(8,128)(2,1)} %bitcast.39, bf16[4,236,768]{2,1,0:T(8,128)(2,1)} %bitcast.41, f32[1,768]{1,0:T(1,128)} %reshape.73.norm_gain.gain, f32[4,240,768]{2,1,0:T(8,128)} %bitcast.42, f32[4,240,768]{2,1,0:T(8,128)} %bitcast.43, ...), custom_call_target="tpu_custom_call" | custom-call | tf_op jit(solution)/shard_map/finish/pallas_call | solution.py:1369
  246.4 0.0 copy-start
  246.4 5.8 %copy.37 = f32[2,2,236,768]{3,1,2,0:T(2,128)} copy(f32[2,2,236,768]{3,2,1,0:T(8,128)} %bitcast.44) | data formatting | bytes 5799936
  252.1 0.0 copy-done
  252.1 0.0 copy-start.9
  252.1 0.0 copy-start.4
  252.1 0.0 copy-start.3
  252.2 2.2 copy.36
  254.4 0.7 copy.39
  255.1 0.0 copy-done.9
  255.1 0.6 slice_bitcast_fusion.3
  255.7 0.6 slice_bitcast_fusion.4
  256.3 0.0 copy-done.4
  256.3 0.7 copy.43
  257.0 0.0 copy-done.3
  257.0 0.7 copy.44
  (4 shorter events, 0.1 us)
Async XLA Ops:
  0.6 4.1 %copy-start.1 = (bf16[2,2,236,768]{3,1,2,0:T(2,128)(2,1)S(1)}, bf16[2,2,236,768]{3,1,2,0:T(2,128)(2,1)}, u32[]{:S(2)}) copy-start(bf16[2,2,236,768]{3,1,2,0:T(2,128)(2,1)} %param.19) | copy-start | bytes 4349956
  4.7 1.4 slice-start
  4.7 1.7 copy-start.7
  4.7 1.8 copy-start.2
  4.7 2.5 copy-start.5
  4.7 2.5 copy-start.6
  6.1 1.9 copy-start.8
  6.1 2.6 %copy-start.10 = (f32[64]{0:T(128)S(1)}, f32[64]{0:T(128)}, u32[]{:S(2)}) copy-start(f32[64]{0:T(128)} %param.17) | copy-start | bytes 772
  6.1 2.6 %copy-start.11 = (f32[64]{0:T(128)S(1)}, f32[64]{0:T(128)}, u32[]{:S(2)}) copy-start(f32[64]{0:T(128)} %param.16) | copy-start | bytes 772
  246.4 5.8 %copy-start = (bf16[4,236,768]{2,1,0:T(8,128)(2,1)S(1)}, bf16[4,236,768]{2,1,0:T(8,128)(2,1)}, u32[]{:S(2)}) copy-start(bf16[4,236,768]{2,1,0:T(8,128)(2,1)} %get-tuple-element.43) | copy-start | bytes 4349956
  252.1 3.0 %copy-start.9 = (f32[8,128]{1,0:T(8,128)S(1)}, f32[8,128]{1,0:T(8,128)}, u32[]{:S(2)}) copy-start(f32[8,128]{1,0:T(8,128)} %get-tuple-element.48) | copy-start | bytes 12292
  252.1 4.2 %copy-start.4 = (f32[96,768]{1,0:T(8,128)S(1)}, f32[96,768]{1,0:T(8,128)}, u32[]{:S(2)}) copy-start(f32[96,768]{1,0:T(8,128)} %get-tuple-element.83) | copy-start | bytes 884740
  252.1 4.9 %copy-start.3 = (f32[96,768]{1,0:T(8,128)S(1)}, f32[96,768]{1,0:T(8,128)}, u32[]{:S(2)}) copy-start(f32[96,768]{1,0:T(8,128)} %get-tuple-element.47) | copy-start | bytes 884740

commit v9 on v8

--- a/solution.py
+++ b/solution.py
@@ -1338,7 +1338,7 @@
 
 
 def finish_kernel(
-    place, tok, cot, gain, branch, d_ff, back, ret, output, input_grad
+    seqs, place, tok, cot, gain, branch, d_ff, back, ret, output, input_grad
 ):
     part = tok.shape[1]
     x = tok[0].astype(F32)
@@ -1354,29 +1354,36 @@
         - jnp.mean(scaled, axis=-1, keepdims=True)
         - unit * jnp.mean(scaled * unit, axis=-1, keepdims=True)
     )
-    input_grad[0] = cot[0].astype(F32) + d_x
-
-
-def finish_call(place, tokens, cotangent, gain, branch, d_ff, back, returned):
+    total = cot[0].astype(F32) + d_x
+    sequence = lax.rem(place[0] + pl.program_id(0), pl.num_programs(0))
+    for inner in range(seqs):
+
+        @pl.when(lax.rem(sequence, seqs) == inner)
+        def _():
+            input_grad[sequence // seqs, :, inner, :] = total
+
+
+def finish_call(place, seqs, tokens, cotangent, gain, branch, d_ff, back, returned):
     count, part, width = tokens.shape
     block = pl.BlockSpec(
         (1, part, width), lambda k, place: (lax.rem(place[0] + k, count), 0, 0)
     )
     padded = pl.BlockSpec((1, PIECE, width), lambda k, place: (k, 0, 0))
     piece = pl.BlockSpec((1, 2 * PIECE - EARLY, width), lambda k, place: (k, 0, 0))
+    ordered = (count // seqs, part, seqs, width)
     early = pl.BlockSpec((1, EARLY, width), lambda k, place: (k, 0, 0))
     line = pl.BlockSpec((1, width), lambda k, place: (0, 0))
     return pl.pallas_call(
-        finish_kernel,
+        functools.partial(finish_kernel, seqs),
         grid_spec=pltpu.PrefetchScalarGridSpec(
             num_scalar_prefetch=1,
             grid=(count,),
             in_specs=[block, block, line, padded, padded, early, piece],
-            out_specs=[block, block],
+            out_specs=[block, pl.BlockSpec(ordered, lambda k, place: (0, 0, 0, 0))],
         ),
         out_shape=[
             jax.ShapeDtypeStruct(tokens.shape, BF16),
-            jax.ShapeDtypeStruct(tokens.shape, F32),
+            jax.ShapeDtypeStruct(ordered, F32),
         ],
         compiler_params=pltpu.CompilerParams(vmem_limit_bytes=VMEM),
         name="finish",
@@ -1460,15 +1467,16 @@
         g_gains = g_gains.at[:width // 128].add(own.reshape(-1, 128))
         g_gains = lax.psum(g_gains, both)
     output, input_grad = finish_call(
-        place, tok, cot, gain,
+        place, seqs, tok, cot, gain,
         branch.reshape(count, PIECE, width), d_ff.reshape(count, PIECE, width), back, returned,
     )
+    input_grad = input_grad.transpose(0, 2, 1, 3)
     g_qkv, g_proj = unpack_attention(g_attn, w_qkv.shape[2])
     g_norm = g_gains[:width // 128].reshape(width)
     g_gains = g_gains[6]
     return (
         output.reshape(tokens.shape),
-        input_grad.reshape(tokens.shape),
+        input_grad,
         g_qkv,
         g_up,
         g_proj,

time: 262 us -> 259 us (0.989)
  local copies, waits for them, and re-layouts: 20.9 us -> 16.6 us
    unnamed x34 -> x31, local copies, waits for them, and re-layouts: 15.3 us -> 11 us
where the time goes in v9:
time: 259 us; the launch traced here: 255 us
  Pallas kernels  235 us (91%)
  local copies, waits for them, and re-layouts  16.6 us (6%)
    pallas_call x1, Pallas kernels, front_call(): pl.pallas_call(front_kernel, in_specs=[vmem] * 6 + [hbm], out_specs=[vmem...  152 us
    pallas_call x1, Pallas kernels, feed_remote_call(): pl.pallas_call(feed_remote_kernel, in_specs=[vmem, vmem, hbm] + [vmem] *...  74.9 us
    unnamed x31, local copies, waits for them, and re-layouts  11 us
    pallas_call x1, Pallas kernels, finish_call(): pl.pallas_call(functools.partial(finish_kernel, seqs), grid_spec=pltpu.Pr...  8.27 us

profile of v9, /device:TPU:0, one launch (start us, length us, event | category | flops | bytes accessed | tf_op | source)
XLA Modules:
  0.0 254.8 jit_solution(1196124322212029358)
XLA Ops:
  0.6 0.0 copy-start
  0.7 1.4 reshape.70.norm_gain.gain
  2.0 2.7 %copy.26 = bf16[2,2,236,768]{3,2,1,0:T(8,128)(2,1)} copy(bf16[2,2,236,768]{3,1,2,0:T(2,128)(2,1)} %param.10) | data formatting | bytes 2899968 | tf_op args[0]
  4.8 0.0 copy-done
  4.8 0.0 slice-start
  4.8 0.0 copy-start.6
  4.8 0.0 copy-start.1
  4.8 0.0 copy-start.4
  4.8 0.0 copy-start.5
  4.8 1.3 copy.27
  6.1 0.0 copy-start.7
  6.1 0.0 copy-start.9
  6.1 0.0 copy-start.10
  6.1 0.0 slice-done
  6.1 0.1 copy.38
  6.3 0.1 copy.31
  6.4 0.0 copy-done.6
  6.4 0.1 copy.30
  6.5 0.0 copy-done.1
  6.5 0.7 pad_maximum_fusion.2.w_attn
  7.3 0.0 copy-done.4
  7.3 0.0 copy-done.5
  7.3 0.7 pad_maximum_fusion.w_feed
  8.0 0.0 copy-done.7
  8.0 0.1 reshape.71
  8.1 0.6 pad.4.ids
  8.7 0.0 copy-done.9
  8.7 0.0 copy-done.10
  8.7 0.6 maximum_bitcast_fusion.gains
  9.3 151.6 %front.1 = (bf16[4,240,768]{2,1,0:T(8,128)(2,1)}, bf16[4,240,768]{2,1,0:T(8,128)(2,1)}, bf16[4,144,768]{2,1,0:T(8,128)(2,1)}, bf16[336,768]{1,0:T(8,128)(2,1)}, ...) custom-call(bf16[4,236,768]{2,1,0:T(8,128)(2,1)} %bitcast.38, ...), custom_call_target="tpu_custom_call" | custom-call | tf_op jit(solution)/shard_map/front/pallas_call | solution.py:1285
  160.9 74.9 %feed_forward_scatter.1 = (f32[960,768]{1,0:T(8,128)}, f32[960,768]{1,0:T(8,128)}, f32[96,768]{1,0:T(8,128)}, f32[96,768]{1,0:T(8,128)}, f32[96,768]{1,0:T(8,128...) custom-call(bf16[960,768]{1,0:T(8,128)(2,1)} %bitcast.55, bf16[960,768]{1,0:T(8,128)(2,1)} %bitcast.56, ...), custom_call_target="tpu_custom_call" | custom-call | flops 27179089920 | bytes 18874368 | tf_op jit(solution)/shard_map/feed_forward_scatter/pallas_call | solution.py:572
  235.9 0.9 slice.35
  236.8 0.1 copy.32
  236.9 1.1 slice_bitcast_fusion
  238.0 0.1 copy.34
  238.1 0.9 copy.36
  239.0 8.3 %finish.1 = (bf16[4,236,768]{2,1,0:T(8,128)(2,1)}, f32[2,236,2,768]{3,2,1,0:T(2,128)}) custom-call(s32[1]{0:T(128)} %bitcast.place, bf16[4,236,768]{2,1,0:T(8,128)(2,1)} %bitcast.39, bf16[4,236,768]{2,1,0:T(8,128)(2,1)} %bitcast.41, f32[1,768]{1,0:T(1,128)} %reshape.70.norm_gain.gain, f32[4,240,768]{2,1,0:T(8,128)} %bitcast.42, f32[4,240,768]{2,1,0:T(8,128)} %bitcast.43, ...), custom_call_target="tpu_custom_call" | custom-call | tf_op jit(solution)/shard_map/finish/pallas_call | solution.py:1376
  247.3 0.0 copy-start.8
  247.3 0.0 copy-start.3
  247.3 0.0 copy-start.2
  247.3 3.7 %copy.35 = bf16[2,2,236,768]{3,1,2,0:T(2,128)(2,1)} copy(bf16[2,2,236,768]{3,2,1,0:T(8,128)(2,1)} %bitcast.44) | data formatting | bytes 2899968
  250.9 0.7 copy.37
  251.7 0.0 copy-done.8
  251.7 0.6 slice_bitcast_fusion.3
  252.3 0.6 slice_bitcast_fusion.4
  252.9 0.0 copy-done.3
  252.9 0.7 copy.41
  253.6 0.0 copy-done.2
  253.6 0.7 copy.42
  (4 shorter events, 0.1 us)
Async XLA Ops:
  0.6 4.1 %copy-start = (bf16[2,2,236,768]{3,1,2,0:T(2,128)(2,1)S(1)}, bf16[2,2,236,768]{3,1,2,0:T(2,128)(2,1)}, u32[]{:S(2)}) copy-start(bf16[2,2,236,768]{3,1,2,0:T(2,128)(2,1)} %param.19) | copy-start | bytes 4349956
  4.8 1.3 slice-start
  4.8 1.6 copy-start.6
  4.8 1.7 copy-start.1
  4.8 2.5 copy-start.4
  4.8 2.5 copy-start.5
  6.1 1.9 copy-start.7
  6.1 2.6 %copy-start.9 = (f32[64]{0:T(128)S(1)}, f32[64]{0:T(128)}, u32[]{:S(2)}) copy-start(f32[64]{0:T(128)} %param.17) | copy-start | bytes 772
  6.1 2.6 %copy-start.10 = (f32[64]{0:T(128)S(1)}, f32[64]{0:T(128)}, u32[]{:S(2)}) copy-start(f32[64]{0:T(128)} %param.16) | copy-start | bytes 772
  247.3 4.4 %copy-start.8 = (f32[8,128]{1,0:T(8,128)S(1)}, f32[8,128]{1,0:T(8,128)}, u32[]{:S(2)}) copy-start(f32[8,128]{1,0:T(8,128)} %get-tuple-element.48) | copy-start | bytes 12292
  247.3 5.6 %copy-start.3 = (f32[96,768]{1,0:T(8,128)S(1)}, f32[96,768]{1,0:T(8,128)}, u32[]{:S(2)}) copy-start(f32[96,768]{1,0:T(8,128)} %get-tuple-element.83) | copy-start | bytes 884740
  247.3 6.3 %copy-start.2 = (f32[96,768]{1,0:T(8,128)S(1)}, f32[96,768]{1,0:T(8,128)}, u32[]{:S(2)}) copy-start(f32[96,768]{1,0:T(8,128)} %get-tuple-element.47) | copy-start | bytes 884740

commit v10 on v9

--- a/solution.py
+++ b/solution.py
@@ -11,7 +11,7 @@
 MOST = 709
 IMAGES = 8
 STRIP = 48
-EARLY = 144
+EARLY = 192
 PIECE = 240
 BIG = 768
 REST = 256
@@ -420,7 +420,7 @@
         )
 
     strips = [(k, strip) for strip in range(returned.shape[1] // STRIP) for k in (1, 3, 2)]
-    first = len(strips) - 4 * steps + 1
+    first = len(strips) - 3 * steps
 
     def back_copy(k, strip):
         rows, sem = pl.ds(strip * STRIP, STRIP), (k - 1, strip)
@@ -464,7 +464,7 @@
         for which in range(steps):
             @pl.when(step == which)
             def _():
-                for k, strip in strips[first + 4 * which:first + 4 * which + 4]:
+                for k, strip in strips[first + 3 * which:first + 3 * which + 3]:
                     back_copy(k, strip).start()
 
         @pl.when(step == 0)
@@ -1181,7 +1181,7 @@
             gather_ff.across(-3, 3)
             scatter.after_second(1)
             scatter.after_first(2)
-        for k, strip in strips[max(0, poll - 3):max(0, poll - 2)]:
+        for k, strip in strips[poll:poll + 1]:
             back_copy(k, strip).start()
 
     def backward_step(step, carry):

time: 259 us -> 256 us (0.988)
  Pallas kernels: 235 us -> 231 us
    pallas_call x1, Pallas kernels: 74.9 us -> 70.9 us  [feed_remote_call(): pl.pallas_call(feed_remote_kernel, in_specs=[vmem, vmem, hbm] + [vmem] *...]
where the time goes in v10:
time: 256 us; the launch traced here: 251 us
  Pallas kernels  231 us (90%)
  local copies, waits for them, and re-layouts  16.6 us (6%)
    pallas_call x1, Pallas kernels, front_call(): pl.pallas_call(front_kernel, in_specs=[vmem] * 6 + [hbm], out_specs=[vmem...  152 us
    pallas_call x1, Pallas kernels, feed_remote_call(): pl.pallas_call(feed_remote_kernel, in_specs=[vmem, vmem, hbm] + [vmem] *...  70.9 us
    unnamed x31, local copies, waits for them, and re-layouts  11 us
    pallas_call x1, Pallas kernels, finish_call(): pl.pallas_call(functools.partial(finish_kernel, seqs), grid_spec=pltpu.Pr...  8.28 us

profile of v10, /device:TPU:0, one launch (start us, length us, event | category | flops | bytes accessed | tf_op | source)
XLA Modules:
  0.0 251.1 jit_solution(13996760282064337506)
XLA Ops:
  0.6 0.0 copy-start
  0.7 1.4 reshape.70.norm_gain.gain
  2.0 2.7 %copy.26 = bf16[2,2,236,768]{3,2,1,0:T(8,128)(2,1)} copy(bf16[2,2,236,768]{3,1,2,0:T(2,128)(2,1)} %param.10) | data formatting | bytes 2899968 | tf_op args[0]
  4.8 0.0 copy-done
  4.8 0.0 slice-start
  4.8 0.0 copy-start.6
  4.8 0.0 copy-start.1
  4.8 0.0 copy-start.4
  4.8 0.0 copy-start.5
  4.8 1.3 copy.27
  6.1 0.0 copy-start.7
  6.1 0.0 copy-start.9
  6.1 0.0 copy-start.10
  6.1 0.0 slice-done
  6.1 0.1 copy.38
  6.3 0.1 copy.31
  6.4 0.0 copy-done.6
  6.4 0.1 copy.30
  6.5 0.0 copy-done.1
  6.5 0.7 pad_maximum_fusion.2.w_attn
  7.3 0.0 copy-done.4
  7.3 0.0 copy-done.5
  7.3 0.7 pad_maximum_fusion.w_feed
  8.0 0.0 copy-done.7
  8.0 0.1 reshape.71
  8.1 0.6 pad.4.ids
  8.7 0.0 copy-done.9
  8.7 0.0 copy-done.10
  8.7 0.6 maximum_bitcast_fusion.gains
  9.3 151.9 %front.1 = (bf16[4,240,768]{2,1,0:T(8,128)(2,1)}, bf16[4,240,768]{2,1,0:T(8,128)(2,1)}, bf16[4,192,768]{2,1,0:T(8,128)(2,1)}, bf16[288,768]{1,0:T(8,128)(2,1)}, ...) custom-call(bf16[4,236,768]{2,1,0:T(8,128)(2,1)} %bitcast.38, ...), custom_call_target="tpu_custom_call" | custom-call | tf_op jit(solution)/shard_map/front/pallas_call | solution.py:1285
  161.2 70.9 %feed_forward_scatter.1 = (f32[960,768]{1,0:T(8,128)}, f32[960,768]{1,0:T(8,128)}, f32[96,768]{1,0:T(8,128)}, f32[96,768]{1,0:T(8,128)}, f32[96,768]{1,0:T(8,128...) custom-call(bf16[960,768]{1,0:T(8,128)(2,1)} %bitcast.55, bf16[960,768]{1,0:T(8,128)(2,1)} %bitcast.56, ...), custom_call_target="tpu_custom_call" | custom-call | flops 27179089920 | bytes 18874368 | tf_op jit(solution)/shard_map/feed_forward_scatter/pallas_call | solution.py:572
  232.2 0.9 slice.35
  233.1 0.1 copy.32
  233.2 1.1 slice_bitcast_fusion
  234.3 0.1 copy.34
  234.4 0.9 copy.36
  235.3 8.3 %finish.1 = (bf16[4,236,768]{2,1,0:T(8,128)(2,1)}, f32[2,236,2,768]{3,2,1,0:T(2,128)}) custom-call(s32[1]{0:T(128)} %bitcast.place, bf16[4,236,768]{2,1,0:T(8,128)(2,1)} %bitcast.39, bf16[4,236,768]{2,1,0:T(8,128)(2,1)} %bitcast.41, f32[1,768]{1,0:T(1,128)} %reshape.70.norm_gain.gain, f32[4,240,768]{2,1,0:T(8,128)} %bitcast.42, f32[4,240,768]{2,1,0:T(8,128)} %bitcast.43, ...), custom_call_target="tpu_custom_call" | custom-call | tf_op jit(solution)/shard_map/finish/pallas_call | solution.py:1376
  243.6 0.0 copy-start.8
  243.6 0.0 copy-start.3
  243.6 0.0 copy-start.2
  243.6 3.7 %copy.35 = bf16[2,2,236,768]{3,1,2,0:T(2,128)(2,1)} copy(bf16[2,2,236,768]{3,2,1,0:T(8,128)(2,1)} %bitcast.44) | data formatting | bytes 2899968
  247.3 0.7 copy.37
  248.0 0.0 copy-done.8
  248.0 0.6 slice_bitcast_fusion.3
  248.6 0.6 slice_bitcast_fusion.4
  249.2 0.0 copy-done.3
  249.2 0.7 copy.41
  249.9 0.0 copy-done.2
  249.9 0.7 copy.42
  (4 shorter events, 0.1 us)
Async XLA Ops:
  0.6 4.1 %copy-start = (bf16[2,2,236,768]{3,1,2,0:T(2,128)(2,1)S(1)}, bf16[2,2,236,768]{3,1,2,0:T(2,128)(2,1)}, u32[]{:S(2)}) copy-start(bf16[2,2,236,768]{3,1,2,0:T(2,128)(2,1)} %param.19) | copy-start | bytes 4349956
  4.8 1.3 slice-start
  4.8 1.6 copy-start.6
  4.8 1.7 copy-start.1
  4.8 2.5 copy-start.4
  4.8 2.5 copy-start.5
  6.1 1.9 copy-start.7
  6.1 2.6 %copy-start.9 = (f32[64]{0:T(128)S(1)}, f32[64]{0:T(128)}, u32[]{:S(2)}) copy-start(f32[64]{0:T(128)} %param.17) | copy-start | bytes 772
  6.1 2.6 %copy-start.10 = (f32[64]{0:T(128)S(1)}, f32[64]{0:T(128)}, u32[]{:S(2)}) copy-start(f32[64]{0:T(128)} %param.16) | copy-start | bytes 772
  243.6 4.4 %copy-start.8 = (f32[8,128]{1,0:T(8,128)S(1)}, f32[8,128]{1,0:T(8,128)}, u32[]{:S(2)}) copy-start(f32[8,128]{1,0:T(8,128)} %get-tuple-element.48) | copy-start | bytes 12292
  243.6 5.6 %copy-start.3 = (f32[96,768]{1,0:T(8,128)S(1)}, f32[96,768]{1,0:T(8,128)}, u32[]{:S(2)}) copy-start(f32[96,768]{1,0:T(8,128)} %get-tuple-element.83) | copy-start | bytes 884740
  243.6 6.3 %copy-start.2 = (f32[96,768]{1,0:T(8,128)S(1)}, f32[96,768]{1,0:T(8,128)}, u32[]{:S(2)}) copy-start(f32[96,768]{1,0:T(8,128)} %get-tuple-element.47) | copy-start | bytes 884740
